TPU v7x, 32 devices: a whole 2x2x4 slice. The times are simulated.
32 devices in a mesh: grp: 2 (over x), row: 16 (over z, y, core).
Axes of the slice: x: 2, y: 2, z: 4, core: 2. Of those that a mesh axis runs over, the one named last changes fastest.
Arguments:
- object_strip: float32 [2, 8192, 1024], P(None, ('grp', 'row')), parts along dimension 1, may hold values from -6 to 6
- probe_store: float32 [32, 2, 2, 128, 128], P(('grp', 'row')), parts along dimension 0, may hold values from -5 to 5
- amplitudes: float32 [512, 128, 128], P(('grp', 'row')), parts along dimension 0, may hold values from 0.2 to 4
- scan_of: int32 [512], P(('grp', 'row')), parts along dimension 0, may hold values from 0 to 7
- offsets: int32 [512, 2], P(('grp', 'row')), parts along dimension 0, may hold values from 0 to 3968, as said below
- counts: int32 [32], P(('grp', 'row')), parts along dimension 0, may hold values from 1 to 16, 160 in all
- owner: int32 [16], P('grp'), parts along dimension 0, may hold values from 0 to 15, as said below
Outputs:
- new_object: float32 [2, 8192, 1024], P(None, ('grp', 'row')), parts along dimension 1
- new_probes: float32 [32, 2, 2, 128, 128], P(('grp', 'row')), parts along dimension 0
There are 2 independent parts, one for each index of `grp`. A program takes and returns all parts, laid end to end along the dimension named above; each array names one. Nothing has to cross between parts.
Inputs may be any that keep to these rules, and one draw needn't show every extreme that they name: offsets[p, 0] is a window's first row and offsets[p, 1] its first column; the windows of device d's slots (p // 16 = d) start in rows d * 256 to (d + 1) * 256 - 1 and lie wholly inside the strip. Slots p mod 16 >= counts[p // 16] are not live. `owner`: the owners of the 8 scans are distinct devices.
All inputs are finite; a program needn't handle non-finite values. No bound on the sum of `counts` on one device may be relied on, other than what follows from the above.
Results may differ from a plain program's by a relative error of at most 0.0001.
Values sent between devices are 32-bit elements; how exact they have to be, the bound alone decides.
No kernel may reach another device: no remote copies, remote signals or barrier semaphores. Data moves between devices by JAX's collectives and lax.ppermute only.
A program may use at most 128 MiB of HBM per device.

v0:
```python
import math

import jax
import jax.numpy as jnp
from jax import lax
from jax.sharding import PartitionSpec as P

damping = 1.0
floor_level = 0.3
highest = lax.Precision.HIGHEST


def passed_along(block, axis, distance):
    devices = range(lax.axis_size(axis))
    route = [(i - distance, i) for i in devices if i - distance in devices]
    return lax.ppermute(block, axis, route)


def broadcast(value, axis, root):
    mine = lax.axis_index(axis) == root
    return lax.psum(jnp.where(mine, value, jnp.zeros_like(value)), axis)


def dft_tables(points):
    index_row = jnp.arange(points, dtype=jnp.int32)
    phase_index = index_row[:, None] * index_row[None, :] % points
    angles = phase_index.astype(jnp.float32) * (2.0 * math.pi / points)
    scale_factor = 1.0 / math.sqrt(points)
    return (jnp.cos(angles) * scale_factor, jnp.sin(angles) * scale_factor)


def right_pass(real_part, imag_part, cos_table, sin_table, direction):
    real_cos = jnp.matmul(real_part, cos_table, precision=highest)
    real_sin = jnp.matmul(real_part, sin_table, precision=highest)
    imag_cos = jnp.matmul(imag_part, cos_table, precision=highest)
    imag_sin = jnp.matmul(imag_part, sin_table, precision=highest)
    return (real_cos - direction * imag_sin, imag_cos + direction * real_sin)


def transform_flip(real_part, imag_part, cos_table, sin_table, direction):
    first_real, first_imag = right_pass(real_part, imag_part, cos_table, sin_table, direction)
    first_real = jnp.swapaxes(first_real, -1, -2)
    first_imag = jnp.swapaxes(first_imag, -1, -2)
    return right_pass(first_real, first_imag, cos_table, sin_table, direction)


def local(object_strip, probe_store, amplitudes, scan_of, offsets, counts, owner):
    device = lax.axis_index("row")
    tile_rows = object_strip.shape[1]
    points = probe_store.shape[-1]
    slot_count = amplitudes.shape[0]
    scan_count = owner.shape[0]
    own_probe = probe_store[0]
    lower_rim = passed_along(object_strip[:, :points, :], "row", -1)
    extended = jnp.concatenate([object_strip, lower_rim], axis=1)
    probe_table = jnp.stack([broadcast(own_probe, "row", owner[s]) for s in range(scan_count)])
    cos_table, sin_table = dft_tables(points)
    live_count = counts[0]
    live_flags = (jnp.arange(slot_count, dtype=jnp.int32) < live_count).astype(jnp.float32)
    row_starts = offsets[:, 0] - device * tile_rows
    col_starts = offsets[:, 1]

    def take_window(row_start, col_start):
        return lax.dynamic_slice(extended, (0, row_start, col_start), (2, points, points))

    windows = jax.vmap(take_window)(row_starts, col_starts)
    one_hot = (scan_of[:, None] == jnp.arange(scan_count, dtype=jnp.int32)[None, :]).astype(
        jnp.float32
    )
    table_flat = probe_table.reshape(scan_count, -1)
    slot_probes = jnp.matmul(one_hot, table_flat, precision=highest).reshape(
        (slot_count,) + probe_table.shape[1:]
    )
    probe_real = slot_probes[:, :, 0]
    probe_imag = slot_probes[:, :, 1]
    win_real = windows[:, 0][:, None]
    win_imag = windows[:, 1][:, None]
    exit_real = probe_real * win_real - probe_imag * win_imag
    exit_imag = probe_real * win_imag + probe_imag * win_real
    spec_real, spec_imag = transform_flip(exit_real, exit_imag, cos_table, sin_table, -1.0)
    intensity = jnp.sum(spec_real * spec_real + spec_imag * spec_imag, axis=1)
    magnitude = jnp.maximum(jnp.sqrt(intensity), floor_level)
    factor = (jnp.swapaxes(amplitudes, -1, -2) / magnitude - 1.0)[:, None]
    change_real, change_imag = transform_flip(
        factor * spec_real, factor * spec_imag, cos_table, sin_table, 1.0
    )
    flags = live_flags[:, None, None]
    term_real = jnp.sum(probe_real * change_real + probe_imag * change_imag, axis=1) * flags
    term_imag = jnp.sum(probe_real * change_imag - probe_imag * change_real, axis=1) * flags
    den_term = jnp.sum(probe_real * probe_real + probe_imag * probe_imag, axis=1) * flags
    patch_terms = jnp.stack([term_real, term_imag, den_term], axis=1)
    grad_real = (win_real * change_real + win_imag * change_imag) * flags[:, None]
    grad_imag = (win_real * change_imag - win_imag * change_real) * flags[:, None]
    probe_terms = jnp.stack([grad_real, grad_imag], axis=2).reshape(slot_count, -1)
    probe_num = jnp.matmul(one_hot.T, probe_terms, precision=highest).reshape(probe_table.shape)
    window_den = ((windows[:, 0] * windows[:, 0] + windows[:, 1] * windows[:, 1]) * flags).reshape(
        slot_count, -1
    )
    probe_den = jnp.matmul(one_hot.T, window_den, precision=highest).reshape(
        scan_count, points, points
    )

    def visit(j, accum):
        row_start = row_starts[j]
        col_start = col_starts[j]
        current = lax.dynamic_slice(accum, (0, row_start, col_start), (3, points, points))
        addend = lax.dynamic_index_in_dim(patch_terms, j, 0, keepdims=False)
        return lax.dynamic_update_slice(accum, current + addend, (0, row_start, col_start))

    start_accum = jnp.zeros((3,) + extended.shape[1:], jnp.float32)
    accum = lax.fori_loop(0, slot_count, visit, start_accum)
    obj_num = accum[:2]
    obj_den = accum[2]
    received = passed_along((obj_num[:, tile_rows:, :], obj_den[tile_rows:, :]), "row", 1)
    top_num = obj_num[:, :tile_rows, :].at[:, :points, :].add(received[0])
    top_den = obj_den[:tile_rows, :].at[:points, :].add(received[1])
    new_object = object_strip + top_num / (top_den + damping)[None]
    summed_num, summed_den = lax.psum((probe_num, probe_den), "row")
    fresh = probe_table + summed_num / (summed_den[:, None, None] + damping)
    owned = owner == device
    picked = jnp.sum(jnp.where(owned[:, None, None, None, None], fresh, 0.0), axis=0)
    new_probes = jnp.where(jnp.any(owned), picked, own_probe)[None]
    return (new_object, new_probes)


def solution(mesh):
    return jax.shard_map(
        local,
        mesh=mesh,
        in_specs=(
            P(None, ("grp", "row"), None),
            P(("grp", "row"), None, None, None, None),
            P(("grp", "row"), None, None),
            P(("grp", "row")),
            P(("grp", "row"), None),
            P(("grp", "row")),
            P("grp"),
        ),
        out_specs=(P(None, ("grp", "row"), None), P(("grp", "row"), None, None, None, None)),
        check_vma=False,
    )
```

profile of v0, /device:TPU:0, one launch (start us, length us, event | category | flops | bytes accessed | tf_op | source)
XLA Modules:
  0.0 518.0 jit_solution(7727992108803525433)
XLA Ops:
  21.2 3.2 pad_maximum_fusion.1
  24.4 59.6 %while.17 = (s32[]{:T(128)}, f32[2,384,1024]{2,1,0:T(8,128)}, s32[16,3]{0,1:T(4,128)S(1)}, f32[16,2,128,128]{3,2,1,0:T(8,128)}, s32[]{:T(128)}) while((s32[]{:T(128)}, f32[2,384,1024]{2,1,0:T(8,128)}, s32[16,3]{0,1:T(4,128)S(1)}, f32[16,2,128,128]{3,2,1,0:T(8,128)}, s32[]{:T(128)}) %tuple.85), condition=%wide.while_cond.2, body=%wide.while_body.2.sunk | while | flops 2 | bytes 263285 | solution.py:64
  88.0 34.3 %all-reduce.7.cloned.1.call-done = (f32[2,2,128,128]{3,2,1,0:T(8,128)}, f32[2,2,128,128]{3,2,1,0:T(8,128)}, f32[2,2,128,128]{3,2,1,0:T(8,128)}, f32[2,2,128,128]...) async-done(((f32[2,2,128,128]{3,2,1,0:T(8,128)}, ...) | async-done | bytes 2097168 | tf_op jit(solution)/shard_map/psum | solution.py:21
  122.3 7.1 %stack.68 = f32[8,65536]{1,0:T(8,128)} concatenate(f32[1,65536]{1,0:T(1,128)} %bitcast.248, f32[1,65536]{1,0:T(1,128)} %bitcast.250, f32[1,65536]{1,0:T(1,128)} %bitcast.252, f32[1,65536]{1,0:T(1,128)} %bitcast.254, f32[1,65536]{1,0:T(1,128)} %bitcast.256, f32[1,65536]{1,0:T(1,128)} %bitcast.258, f32[1,65536]{1,0:T(1,128)} %bitcast.260, f32[1,65536]{1,0:T(1,128)} %bitcast.262), dimensions={0} | concatenate | bytes 4194304 | tf_op jit(solution)/shard_map/stack | solution.py:56
  129.4 3.6 fusion.75
  142.7 3.8 fusion.2
  146.6 3.7 fusion.4
  153.0 3.6 multiply_subtract_fusion
  156.5 3.9 add_reduce_fusion.2
  165.1 3.4 add_bitcast_fusion
  182.2 5.6 %multiply_bitcast_fusion.1 = (f32[16,2,1,128,128]{4,0,3,1,2:T(8,128)}, f32[16,2,1,128,128]{4,0,3,1,2:T(8,128)}, f32[16,128,128]{2,0,1:T(8,128)S(1)}, f32[16,128,128]{2,0,1:T(8,128)S(1)}, f32[16,128,128]{2,0,1:T(8,128)S(1)}) fusion(f32[16,2,128,128]{3,0,2,1:T(8,128)S(1)} %convolution_add_fusion, f32[16]{0:T(128)S(1)} %compare_convert_fusion, ...), kind=kOutput, calls=%fused_computation.22 | convolution fusion | flops 815775744 | bytes 19923008 | tf_op jit(solution)/shard_map/dot_general | solution.py:36
  192.6 187.6 %while.16 = (s32[]{:T(128)}, f32[3,384,1024]{2,1,0:T(8,128)}, s32[16]{0:T(128)S(1)}, s32[16]{0:T(128)S(1)}, f32[16,3,128,128]{3,0,2,1:T(8,128)}, /*index=5*/s32[]{:T(128)}, s32[]{:T(128)}, s32[]{:T(128)}, s32[]{:T(128)}) while((s32[]{:T(128)}, f32[3,384,1024]{2,1,0:T(8,128)}, s32[16]{0:T(128)S(1)}, s32[16]{0:T(128)S(1)}, ...), condition=%wide.region_13.14_spmd, body=%wide.region_12.13_spmd.sunk | while | flops 49160 | bytes 1376465 | solution.py:111
  211.0 4.0 dynamic_update_slice.8
  222.7 4.0 dynamic_update_slice.8
  234.5 4.1 dynamic_update_slice.8
  246.4 4.1 dynamic_update_slice.8
  258.2 4.0 dynamic_update_slice.8
  270.0 3.7 dynamic_update_slice.8
  281.5 4.0 dynamic_update_slice.8
  293.3 4.0 dynamic_update_slice.8
  305.1 4.0 dynamic_update_slice.8
  316.9 4.1 dynamic_update_slice.8
  328.7 4.0 dynamic_update_slice.8
  340.5 4.1 dynamic_update_slice.8
  352.4 4.1 dynamic_update_slice.8
  364.2 4.0 dynamic_update_slice.8
  376.1 4.1 dynamic_update_slice.8
  389.6 5.3 %fusion = f32[8,2,2,128,128]{4,0,3,2,1:T(8,128)} fusion(f32[2,2,128,128,16]{3,2,1,0,4:T(8,128)S(1)} %bitcast.245, s32[16]{0:T(128)S(1)} %copy-done.14), kind=kOutput, calls=%fused_computation.6 | convolution fusion | flops 100663424 | bytes 6291520 | tf_op jit(solution)/shard_map/dot_general | solution.py:95
  397.4 3.9 collective-permute-start.1
  406.2 6.6 %stack.78 = f32[8,2,2,128,128]{4,0,3,2,1:T(8,128)} concatenate(f32[1,2,2,128,128]{4,0,3,2,1:T(1,128)S(1)} %bitcast.249, f32[1,2,2,128,128]{4,0,3,2,1:T(1,128)} %bitcast.251, f32[1,2,2,128,128]{4,0,3,2,1:T(1,128)} %bitcast.253, f32[1,2,2,128,128]{4,0,3,2,1:T(1,128)} %bitcast.255, f32[1,2,2,128,128]{4,0,3,2,1:T(1,128)} %bitcast.257, f32[1,2,2,128,128]{4,0,3,2,1:T(1,128)} %bitcast.259, ...), dimensions={0} | concatenate | bytes 4194304 | tf_op jit(solution)/shard_map/stack | solution.py:56
  418.3 87.0 %all-reduce.5.cloned.1.call-done = (f32[8,2,2,128,128]{4,0,3,2,1:T(8,128)}, f32[8,128,128]{2,0,1:T(8,128)}) async-done(((f32[8,2,2,128,128]{4,0,3,2,1:T(8,128)}, f32[8,128,128]{2,0,1:T(8,128)}), (f32[8,2,2,128,128]{4,0,3,2,1:T(8,128)}, f32[8,128,128]{2,0,1:T(8,128)})) %all-reduce.5.cloned.1.call-update) | async-done | bytes 2621456 | tf_op jit(solution)/shard_map/psum | solution.py:118
  506.5 3.1 select_reduce_fusion
  (199 shorter events, 196.3 us)
Async XLA Ops:
  7.2 3.7 copy-start.13
  7.2 9.4 %copy-start.11 = (f32[1,2,2,128,128]{4,3,2,1,0:T(8,128)S(1)}, f32[1,2,2,128,128]{4,3,2,1,0:T(8,128)}, u32[]{:S(2)}) copy-start(f32[1,2,2,128,128]{4,3,2,1,0:T(8,128)} %param.14) | copy-start | bytes 786436
  7.2 115.1 %all-reduce.7.cloned.1.call-start = ((), (), s32[]{:S(2)}) async-start(), calls=%async_computation.1 | async-start | bytes 4194304 | tf_op jit(solution)/shard_map/psum | solution.py:21
  9.6 11.6 %collective-permute-start = (f32[2,128,1024]{2,1,0:T(8,128)}, f32[2,128,1024]{2,1,0:T(8,128)}, u32[]{:S(2)}, u32[]{:S(2)}) collective-permute-start(f32[2,128,1024]{2,1,0:T(8,128)} %slice.129), channel_id=1, source_target_pairs={{1,0},{2,1},{3,2},{4,3},{5,4},{6,5},{7,6},{8,7},{9,8},{10,9},{11,1... | collective-permute-start | bytes 3145736 | tf_op jit(solution)/shard_map/ppermute | solution.py:16
  18.0 2.5 copy-start.15
  18.0 3.2 copy-start.3
  18.0 487.4 %all-reduce.5.cloned.1.call-start = ((), (), s32[]{:S(2)}) async-start(), calls=%async_computation | async-start | bytes 5242880 | tf_op jit(solution)/shard_map/psum | solution.py:118
  88.0 45.0 %copy-start.5 = (f32[16,128,128]{2,0,1:T(8,128)}, f32[16,128,128]{2,0,1:T(8,128)S(1)}, u32[]{:S(2)}) copy-start(f32[16,128,128]{2,0,1:T(8,128)S(1)} %copy.69) | copy-start | bytes 3145732
  122.3 7.1 %copy-start.14 = (s32[16]{0:T(128)S(1)}, s32[16]{0:T(128)}, u32[]{:S(2)}) copy-start(s32[16]{0:T(128)} %param.16) | copy-start | bytes 196
  133.0 2.0 copy-start
  175.4 2.2 copy-start.2
  179.7 2.2 copy-start.1
  179.7 2.5 copy-start.6
  192.6 192.0 %copy-start.8 = (f32[16,2,1,128,128]{4,0,3,1,2:T(8,128)S(1)}, f32[16,2,1,128,128]{4,0,3,1,2:T(8,128)}, u32[]{:S(2)}) copy-start(f32[16,2,1,128,128]{4,0,3,1,2:T(8,128)} %get-tuple-element.170) | copy-start | bytes 6291460
  380.3 4.4 copy-start.7
  389.6 11.7 %copy-start.9 = (f32[16,1,128,128]{3,2,1,0:T(8,128)S(1)}, f32[16,1,128,128]{3,2,1,0:T(8,128)}, u32[]{:S(2)}) copy-start(f32[16,1,128,128]{3,2,1,0:T(8,128)} %get-tuple-element.176) | copy-start | bytes 3145732
  395.0 17.9 %collective-permute-start.2 = (f32[128,1024]{1,0:T(8,128)}, f32[128,1024]{1,0:T(8,128)}, u32[]{:S(2)}, u32[]{:S(2)}) collective-permute-start(f32[128,1024]{1,0:T(8,128)} %slice_bitcast_fusion.5), channel_id=1, source_target_pairs={{0,1},{1,2},{2,3},{3,4},{4,5},{5,6},{6,7},{7,8},{8,9},{9,10},{10,1... | collective-permute-start | bytes 1572872 | tf_op jit(solution)/shard_map/ppermute | solution.py:16
  397.4 16.8 %collective-permute-start.1 = (f32[2,128,1024]{2,1,0:T(8,128)}, f32[2,128,1024]{2,1,0:T(8,128)}, u32[]{:S(2)}, u32[]{:S(2)}) collective-permute-start(f32[2,128,1024]{2,1,0:T(8,128)} %slice.135), channel_id=1, source_target_pairs={{0,1},{1,2},{2,3},{3,4},{4,5},{5,6},{6,7},{7,8},{8,9},{9,10},{10,1... | collective-permute-start | bytes 3145736 | tf_op jit(solution)/shard_map/ppermute | solution.py:16
  404.5 1.8 copy-start.10
  414.2 2.2 copy-start.4
  506.5 3.1 copy-start.12
Sparse Core Ops, SparseCore 0:
  18.1 104.1 all-reduce.6
  403.3 102.0 all-reduce.4
where the time goes:
time: 527 us; the launch traced here: 518 us
  local copies, waits for them, and re-layouts  207 us (39%)
  waiting for transfers between devices  121 us (23%)
  loops' own time  62.6 us (12%)
  matrix products  58.5 us (11%)
  other arithmetic  40.4 us (8%)
  between operations  20.5 us (4%)
  starting transfers between devices  7.68 us (1%)
    psum x1, waiting for transfers between devices, local(): summed_num, summed_den = lax.psum((probe_num, probe_den), 'row')  87 us
    dynamic_update_slice x16, local copies, waits for them, and re-layouts, visit(): lax.dynamic_update_slice(accum, current + addend, (0, row_start, col_start))  63.1 us
    another operation x1, loops' own time, local(): accum = lax.fori_loop(0, slot_count, visit, start_accum)  62.6 us
    gather x48, local copies, waits for them, and re-layouts  59.6 us
    psum x1, waiting for transfers between devices, broadcast(): return lax.psum(jnp.where(mine, value, jnp.zeros_like(value)), axis)  34.3 us
    dynamic_slice x16, local copies, waits for them, and re-layouts, visit(): addend = lax.dynamic_index_in_dim(patch_terms, j, 0, keepdims=False)  24.8 us
    add x16, other arithmetic, visit(): current + addend  18.3 us
    dot_general x4, matrix products, right_pass(): imag_sin = jnp.matmul(imag_part, sin_table, precision=highest)  13.9 us
  transfers between devices with their start and end apart: 5, of which 2 were waited for; matrix products, arithmetic and copies ran while one was open for 17% of the time, Pallas kernels for 0%

commit v1 on v0

v1 whole, which is shorter than its diff:
```python
import functools
import math

import jax
import jax.numpy as jnp
import numpy as np
from jax import lax
from jax.experimental import pallas as pl
from jax.experimental.pallas import tpu as pltpu
from jax.sharding import PartitionSpec as P

damping = 1.0
floor_level = 0.3
LANES = 128
SLOTS_AT_ONCE = 2
VMEM_BYTES = 48 * 1024 * 1024


def moved(block, distance):
    size = lax.axis_size("row")
    return lax.ppermute(block, "row", [(i, i + distance) for i in range(size) if 0 <= i + distance < size])


def swapped(block, mask):
    return lax.ppermute(block, "row", [(i, i ^ mask) for i in range(lax.axis_size("row"))])


def split(value):
    high = value.astype(jnp.bfloat16)
    low = (value - high.astype(jnp.float32)).astype(jnp.bfloat16)
    return high, low


def transform_tables(points):
    index = np.arange(points)
    angle = (index[:, None] * index[None, :] % points) * (2.0 * math.pi / points)
    cos, sin = np.cos(angle) / math.sqrt(points), np.sin(angle) / math.sqrt(points)
    minus = np.block([[cos, -sin], [sin, cos]])
    plus = np.block([[cos, sin], [-sin, cos]])

    def parts(matrix, axis):
        matrix = matrix.astype(np.float32)
        high = matrix.astype(jnp.bfloat16)
        low = (matrix - high.astype(np.float32)).astype(jnp.bfloat16)
        return jnp.asarray(np.concatenate([high, high, low], axis=axis))

    return parts(minus, 0), parts(plus, 1), parts(minus, 1), parts(plus, 0)


def right_product(rows, table):
    high, low = split(rows)
    return jnp.dot(jnp.concatenate([high, low, high], axis=1), table, preferred_element_type=jnp.float32)


def left_product(table, columns):
    high, low = split(columns)
    return jnp.dot(table, jnp.concatenate([high, low, high], axis=0), preferred_element_type=jnp.float32)


def update_kernel(dims, meta, slot_of, live, amplitudes, obj, rim, right_f, left_f, left_i, right_i, *rest):
    piece_sizes, group_sizes, slots = dims
    pieces = rest[: len(piece_sizes)]
    rest = rest[len(piece_sizes) :]
    num_top, num_low, squares = rest[:3]
    groups = rest[3 : 3 + len(group_sizes)]
    table, ext, acc, part, piece_sems, out_sems = rest[3 + len(group_sizes) :]
    points = LANES
    tile_rows = obj.shape[1]
    blocks = obj.shape[2] // LANES
    modes = table.shape[1] // 2

    copies = []
    at = 0
    for k, size in enumerate(piece_sizes):
        copies.append(pltpu.make_async_copy(pieces[k], table.at[pl.ds(at, size)], piece_sems.at[k]))
        at += size
    for copy in copies:
        copy.start()
    for b in range(blocks):
        ext[:, b, :tile_rows, :] = obj[:, :, b * LANES : (b + 1) * LANES]
        ext[:, b, tile_rows:, :] = rim[:, :, b * LANES : (b + 1) * LANES]
    ext[:, blocks] = jnp.zeros_like(ext[:, blocks])
    acc[...] = jnp.zeros_like(acc)
    part[...] = jnp.zeros_like(part)
    for copy in copies:
        copy.wait()
    for s in range(squares.shape[0]):
        probe = table[slot_of[s]]
        squares[s] = jnp.sum(probe * probe, axis=0)

    lane = lax.broadcasted_iota(jnp.int32, (points, LANES), 1)
    count = live[0]

    def step(i, carry):
        wins, probes, places, waves, flags = [], [], [], [], []
        for u in range(SLOTS_AT_ONCE):
            p = i * SLOTS_AT_ONCE + u
            flags.append((p < count).astype(jnp.float32))
            row, col, scan = meta[4 * p], meta[4 * p + 1], meta[4 * p + 2]
            slot = slot_of[scan]
            block, shift = col // LANES, col % LANES
            back = lax.rem(LANES - shift, LANES)
            keep = lane < LANES - shift
            win = []
            for ch in range(2):
                first = pltpu.roll(ext[ch, block, pl.ds(row, points), :], back, 1)
                second = pltpu.roll(ext[ch, block + 1, pl.ds(row, points), :], back, 1)
                win.append(jnp.where(keep, first, second))
            probe = [(table[slot, 2 * m], table[slot, 2 * m + 1]) for m in range(modes)]
            for pr, pi in probe:
                waves.append(
                    jnp.concatenate([pr * win[0] - pi * win[1], pr * win[1] + pi * win[0]], axis=1)
                )
            wins.append(win)
            probes.append(probe)
            places.append((p, row, block, shift, slot))
        half = right_product(jnp.concatenate(waves, axis=0), right_f[...])
        columns = []
        for k in range(SLOTS_AT_ONCE * modes):
            rows = half[k * points : (k + 1) * points]
            columns.append(jnp.concatenate([rows[:, :points], rows[:, points:]], axis=0))
        spec = left_product(left_f[...], jnp.concatenate(columns, axis=1))
        columns = []
        for u in range(SLOTS_AT_ONCE):
            own = [spec[:, (u * modes + m) * points : (u * modes + m + 1) * points] for m in range(modes)]
            total = functools.reduce(jnp.add, [s * s for s in own])
            intensity = total[:points] + total[points:]
            factor = amplitudes[places[u][0]] * lax.rsqrt(jnp.maximum(intensity, floor_level * floor_level)) - 1.0
            factor = factor * flags[u]
            factor = jnp.concatenate([factor, factor], axis=0)
            columns += [s * factor for s in own]
        half = left_product(left_i[...], jnp.concatenate(columns, axis=1))
        rows = []
        for k in range(SLOTS_AT_ONCE * modes):
            column = half[:, k * points : (k + 1) * points]
            rows.append(jnp.concatenate([column[:points], column[points:]], axis=1))
        change = right_product(jnp.concatenate(rows, axis=0), right_i[...])
        for u in range(SLOTS_AT_ONCE):
            p, row, block, shift, slot = places[u]
            wr, wi = wins[u]
            term_r = term_i = None
            for m in range(modes):
                k = u * modes + m
                pr, pi = probes[u][m]
                dr = change[k * points : (k + 1) * points, :points]
                di = change[k * points : (k + 1) * points, points:]
                tr, ti = pr * dr + pi * di, pr * di - pi * dr
                term_r = tr if m == 0 else term_r + tr
                term_i = ti if m == 0 else term_i + ti
                part[slot, 2 * m] += wr * dr + wi * di
                part[slot, 2 * m + 1] += wr * di - wi * dr
            part[slot, 2 * modes] += (wr * wr + wi * wi) * flags[u]
            first = lane >= shift
            for ch, term in enumerate((term_r, term_i)):
                term = pltpu.roll(term, shift, 1)
                acc[ch, block, pl.ds(row, points), :] += jnp.where(first, term, 0.0)
                acc[ch, block + 1, pl.ds(row, points), :] += jnp.where(first, 0.0, term)
        return carry

    lax.fori_loop(0, (count + SLOTS_AT_ONCE - 1) // SLOTS_AT_ONCE, step, 0)

    copies = []
    at = 0
    for k, size in enumerate(group_sizes):
        copies.append(pltpu.make_async_copy(part.at[pl.ds(at, size)], groups[k], out_sems.at[k]))
        at += size
    k = len(group_sizes)
    copies.append(
        pltpu.make_async_copy(acc.at[:, pl.ds(0, blocks), pl.ds(tile_rows, points), :], num_low, out_sems.at[k])
    )
    copies.append(
        pltpu.make_async_copy(acc.at[:, pl.ds(0, blocks), pl.ds(0, tile_rows), :], num_top, out_sems.at[k + 1])
    )
    for copy in copies:
        copy.start()
    for copy in copies:
        copy.wait()


def update(meta, slot_of, live, amplitudes, obj, rim, tables, pieces, group_sizes):
    points = amplitudes.shape[-1]
    tile_rows = obj.shape[1]
    blocks = obj.shape[2] // LANES
    channels = pieces[0].shape[1]
    scans = slot_of.shape[0]
    piece_sizes = tuple(piece.shape[0] for piece in pieces)
    slots = sum(piece_sizes)
    f32 = jnp.float32
    smem = pl.BlockSpec(memory_space=pltpu.SMEM)
    vmem = pl.BlockSpec(memory_space=pltpu.VMEM)
    anywhere = pl.BlockSpec(memory_space=pl.ANY)
    return pl.pallas_call(
        functools.partial(update_kernel, (piece_sizes, group_sizes, slots)),
        out_shape=[
            jax.ShapeDtypeStruct((2, blocks, tile_rows, LANES), f32),
            jax.ShapeDtypeStruct((2, blocks, points, LANES), f32),
            jax.ShapeDtypeStruct((scans, points, points), f32),
        ]
        + [jax.ShapeDtypeStruct((size, channels + 1, points, points), f32) for size in group_sizes],
        in_specs=[smem] * 3 + [vmem] * 7 + [anywhere] * len(pieces),
        out_specs=[anywhere, anywhere, vmem] + [anywhere] * len(group_sizes),
        scratch_shapes=[
            pltpu.VMEM((slots, channels, points, points), f32),
            pltpu.VMEM((2, blocks + 1, tile_rows + points, LANES), f32),
            pltpu.VMEM((2, blocks + 1, tile_rows + points, LANES), f32),
            pltpu.VMEM((slots, channels + 1, points, points), f32),
            pltpu.SemaphoreType.DMA((len(pieces),)),
            pltpu.SemaphoreType.DMA((len(group_sizes) + 2,)),
        ],
        compiler_params=pltpu.CompilerParams(vmem_limit_bytes=VMEM_BYTES),
        cost_estimate=pl.CostEstimate(flops=6 * 10**9, bytes_accessed=16 * 2**20, transcendentals=2**18),
        name="update",
    )(meta, slot_of, live, amplitudes, obj, rim, *tables, *pieces)


def density_kernel(tile_rows, meta, above, squares, density, ext):
    points = LANES
    blocks = density.shape[0]
    ext[...] = jnp.zeros_like(ext)
    lane = lax.broadcasted_iota(jnp.int32, (points, LANES), 1)

    def place(values, row, col):
        block, shift = col // LANES, col % LANES
        first = lane >= shift
        values = pltpu.roll(values, shift, 1)
        ext[block, pl.ds(row, points), :] += jnp.where(first, values, 0.0)
        ext[block + 1, pl.ds(row, points), :] += jnp.where(first, 0.0, values)

    def own(p, carry):
        @pl.when(meta[4 * p + 3] > 0)
        def _():
            place(squares[meta[4 * p + 2]], meta[4 * p] + points, meta[4 * p + 1])

        return carry

    def upper(p, carry):
        row = above[4 * p] - tile_rows + points

        @pl.when((above[4 * p + 3] > 0) & (row > 0))
        def _():
            place(squares[above[4 * p + 2]], row, above[4 * p + 1])

        return carry

    lax.fori_loop(0, meta.shape[0] // 4, own, 0)
    lax.fori_loop(0, above.shape[0] // 4, upper, 0)
    density[...] = ext[:blocks, points : points + tile_rows, :]


def density_of(meta, above, squares, tile_rows, blocks):
    points = squares.shape[-1]
    smem = pl.BlockSpec(memory_space=pltpu.SMEM)
    vmem = pl.BlockSpec(memory_space=pltpu.VMEM)
    return pl.pallas_call(
        functools.partial(density_kernel, tile_rows),
        out_shape=jax.ShapeDtypeStruct((blocks, tile_rows, LANES), jnp.float32),
        in_specs=[smem, smem, vmem],
        out_specs=vmem,
        scratch_shapes=[pltpu.VMEM((blocks + 1, points + tile_rows + points, LANES), jnp.float32)],
        compiler_params=pltpu.CompilerParams(vmem_limit_bytes=VMEM_BYTES),
        cost_estimate=pl.CostEstimate(flops=2**23, bytes_accessed=8 * 2**20, transcendentals=0),
        name="density",
    )(meta, above, squares)


def finish_kernel(obj, num_top, received, density, out):
    points = received.shape[2]
    for b in range(density.shape[0]):
        columns = slice(b * LANES, (b + 1) * LANES)
        scale = 1.0 / (density[b] + damping)
        for ch in range(2):
            head = num_top[ch, b, :points] + received[ch, b]
            out[ch, :points, columns] = obj[ch, :points, columns] + head * scale[:points]
            out[ch, points:, columns] = obj[ch, points:, columns] + num_top[ch, b, points:] * scale[points:]


def finish(obj, num_top, received, density):
    vmem = pl.BlockSpec(memory_space=pltpu.VMEM)
    return pl.pallas_call(
        finish_kernel,
        out_shape=jax.ShapeDtypeStruct(obj.shape, obj.dtype),
        in_specs=[vmem] * 4,
        out_specs=vmem,
        compiler_params=pltpu.CompilerParams(vmem_limit_bytes=VMEM_BYTES),
        cost_estimate=pl.CostEstimate(flops=2**21, bytes_accessed=8 * 2**20, transcendentals=0),
        name="finish",
    )(obj, num_top, received, density)


def local(object_strip, probe_store, amplitudes, scan_of, offsets, counts, owner):
    device = lax.axis_index("row")
    size = lax.axis_size("row")
    tile_rows = object_strip.shape[1]
    blocks = object_strip.shape[2] // LANES
    points = probe_store.shape[-1]
    modes = probe_store.shape[1]
    slot_count = amplitudes.shape[0]
    scan_count = owner.shape[0]
    channels = 2 * modes
    swaps = size == 16
    own_probe = probe_store.reshape(1, channels, points, points)

    is_live = (jnp.arange(slot_count, dtype=jnp.int32) < counts[0]).astype(jnp.int32)
    meta = jnp.stack([offsets[:, 0] - device * tile_rows, offsets[:, 1], scan_of, is_live], axis=1).reshape(-1)
    above = moved(meta, 1)

    if swaps:
        held = {0: own_probe}
        for far in (12, 8, 4):
            held[far] = swapped(own_probe, far)
        for far in (0, 12, 8, 4):
            held[far | 2] = swapped(held[far], 2)
        for far in (0, 2, 12, 14, 8, 10, 4, 6):
            held[far | 1] = swapped(held[far], 1)
        order = [far | side | core for core in (0, 1) for far in (12, 8, 4, 0) for side in (0, 2)]
        pieces = [held[k] for k in order]
        place = np.zeros(size, np.int32)
        place[np.array(order)] = np.arange(size)
        slot_of = jnp.asarray(place)[jnp.bitwise_xor(owner, device)]
        group_sizes = (2,) * 8
    else:
        owned = (owner == device)[:, None, None, None]
        pieces = [lax.psum(jnp.where(owned, own_probe, 0.0), "row")]
        slot_of = jnp.arange(scan_count, dtype=jnp.int32)
        group_sizes = (scan_count,)
    rim = moved(object_strip[:, :points, :], -1)

    num_top, num_low, squares, *groups = update(
        meta, slot_of, counts, amplitudes, object_strip, rim, transform_tables(points), pieces, group_sizes
    )

    if swaps:
        mine, theirs = groups[:4], groups[4:]
        other = [swapped(block, 1) for block in theirs]
        near = []
        for j in range(4):
            across = swapped(mine[j][1] + other[j][1], 2)
            near.append(mine[j][0] + other[j][0] + across)
        total = near[3]
        for j, far in enumerate((12, 8, 4)):
            total = total + swapped(near[j], far)
    else:
        summed = lax.psum(groups[0], "row")
        total = jnp.sum(jnp.where(owned, summed, 0.0), axis=0)
    received = moved(num_low, 1)
    density = density_of(meta, above, squares, tile_rows, blocks)
    new_object = finish(object_strip, num_top, received, density)
    new_probes = own_probe[0] + total[:channels] / (total[channels] + damping)
    return (new_object, new_probes.reshape(probe_store.shape))


def solution(mesh):
    return jax.shard_map(
        local,
        mesh=mesh,
        in_specs=(
            P(None, ("grp", "row"), None),
            P(("grp", "row"), None, None, None, None),
            P(("grp", "row"), None, None),
            P(("grp", "row")),
            P(("grp", "row"), None),
            P(("grp", "row")),
            P("grp"),
        ),
        out_specs=(P(None, ("grp", "row"), None), P(("grp", "row"), None, None, None, None)),
        check_vma=False,
    )
```

time: 527 us -> 152 us (0.29); the launches traced: 518 us -> 151 us
  local copies, waits for them, and re-layouts: 207 us -> 7.15 us
  loops' own time: 62.6 us -> 0 us
  waiting for transfers between devices: 121 us -> 61.4 us
  matrix products: 58.5 us -> 0 us
  starting transfers between devices: 7.68 us -> 56.6 us
  other arithmetic: 40.4 us -> 3.26 us
  Pallas kernels: 0 us -> 20.7 us
  between operations: 20.5 us -> 1.57 us
    psum x2 -> x0, waiting for transfers between devices: 121 us -> none  [the longest x1 87 us: local(): summed_num, summed_den = lax.psum((probe_num, probe_den), 'row')]
    dynamic_update_slice x16 -> x0, local copies, waits for them, and re-layouts: 63.1 us -> none  [visit(): lax.dynamic_update_slice(accum, current + addend, (0, row_start, col_start))]
    another operation x2 -> x0, loops' own time: 62.6 us -> none  [the longest x1 62.6 us: local(): accum = lax.fori_loop(0, slot_count, visit, start_accum)]
    ppermute x3 -> x29, waiting for transfers between devices: 0.01 us -> 61.4 us  [the longest x26 61.4 us: swapped(): lax.ppermute(block, 'row', [(i, i ^ mask) for i in range(lax.axis_size('r...]
    gather x48 -> x1, local copies, waits for them, and re-layouts: 59.6 us -> 0.64 us  [local(): slot_of = jnp.asarray(place)[jnp.bitwise_xor(owner, device)]]
    dot_general x19 -> x0, matrix products: 58.5 us -> none  [the longest x4 13.9 us: right_pass(): imag_sin = jnp.matmul(imag_part, sin_table, precision=highest)]
    ppermute x3 -> x29, starting transfers between devices: 7.6 us -> 56.6 us  [the longest x26 51.4 us: swapped(): lax.ppermute(block, 'row', [(i, i ^ mask) for i in range(lax.axis_size('r...]
    dynamic_slice x48 -> x0, local copies, waits for them, and re-layouts: 43.6 us -> none  [the longest x16 24.8 us: visit(): addend = lax.dynamic_index_in_dim(patch_terms, j, 0, keepdims=False)]
  transfers between devices with their start and end apart: 5 -> 29, of which waited for: 2 -> 11; matrix products, arithmetic and copies ran while one was open for 17% -> 4% of each run, Pallas kernels for 0% -> 4%
where the time goes in v1:
time: 152 us; the launch traced here: 151 us
  waiting for transfers between devices  61.4 us (40%)
  starting transfers between devices  56.6 us (37%)
  Pallas kernels  20.7 us (14%)
  local copies, waits for them, and re-layouts  7.15 us (5%)
  other arithmetic  3.26 us (2%)
  between operations  1.57 us (1%)
    ppermute x26, waiting for transfers between devices, swapped(): lax.ppermute(block, 'row', [(i, i ^ mask) for i in range(lax.axis_size('r...  61.4 us
    ppermute x26, starting transfers between devices, swapped(): lax.ppermute(block, 'row', [(i, i ^ mask) for i in range(lax.axis_size('r...  51.4 us
    pallas_call x1, Pallas kernels, update(): pl.pallas_call(functools.partial(update_kernel, (piece_sizes, group_sizes...  15.3 us
    ppermute x3, starting transfers between devices, moved(): lax.ppermute(block, 'row', [(i, i + distance) for i in range(size) if 0 <...  5.24 us
    unnamed x30, local copies, waits for them, and re-layouts  4.03 us
    pallas_call x1, Pallas kernels, finish(): pl.pallas_call(finish_kernel, out_shape=jax.ShapeDtypeStruct(obj.shape, o...  3.58 us
  transfers between devices with their start and end apart: 29, of which 11 were waited for; matrix products, arithmetic and copies ran while one was open for 4% of the time, Pallas kernels for 4%

profile of v1, /device:TPU:0, one launch (start us, length us, event | category | flops | bytes accessed | tf_op | source)
XLA Modules:
  0.0 150.8 jit_solution(17833256442770471608)
XLA Ops:
  0.7 4.1 %collective-permute-start.3 = (f32[1,4,128,128]{3,2,1,0:T(8,128)}, f32[1,4,128,128]{3,2,1,0:T(8,128)S(1)}, u32[]{:S(2)}, u32[]{:S(2)}) collective-permute-start(f32[1,4,128,128]{3,2,1,0:T(8,128)} %bitcast.39), channel_id=1, source_target_pairs={{0,8},{1,9},{2,10},{3,11},{4,12},{5,13},{6,14},{7,15},{8,0},{9,1},... | collective-permute-start | bytes 786440 | tf_op jit(solution)/shard_map/ppermute | solution.py:25
  4.8 1.6 %collective-permute-start.5 = (f32[1,4,128,128]{3,2,1,0:T(8,128)}, f32[1,4,128,128]{3,2,1,0:T(8,128)S(1)}, u32[]{:S(2)}, u32[]{:S(2)}) collective-permute-start(f32[1,4,128,128]{3,2,1,0:T(8,128)} %bitcast.40), channel_id=1, source_target_pairs={{0,4},{1,5},{2,6},{3,7},{4,0},{5,1},{6,2},{7,3},{8,12},{9,13},{10,... | collective-permute-start | bytes 786440 | tf_op jit(solution)/shard_map/ppermute | solution.py:25
  6.4 2.3 %slice.65 = f32[2,128,1024]{2,1,0:T(8,128)} slice(f32[2,256,1024]{2,1,0:T(8,128)} %obj.3), slice={[0:2], [0:128], [0:1024]} | slice | bytes 2097152 | tf_op jit(solution)/shard_map/slice | solution.py:326
  8.7 1.3 collective-permute-start
  10.0 2.4 %collective-permute-start.7 = (f32[1,4,128,128]{3,2,1,0:T(8,128)S(1)}, f32[1,4,128,128]{3,2,1,0:T(8,128)S(1)}, u32[]{:S(2)}, u32[]{:S(2)}) collective-permute-start(f32[1,4,128,128]{3,2,1,0:T(8,128)S(1)} %bitcast.42), channel_id=1, source_target_pairs={{0,2},{1,3},{2,0},{3,1},{4,6},{5,7},{6,4},{7,5},{8,10},{9,11},{10,... | collective-permute-start | bytes 786440 | tf_op jit(solution)/shard_map/ppermute | solution.py:25
  12.4 6.3 %collective-permute-done.3.rest_2_ = f32[1,4,128,128]{3,2,1,0:T(8,128)S(1)} collective-permute-done((f32[1,4,128,128]{3,2,1,0:T(8,128)}, f32[1,4,128,128]{3,2,1,0:T(8,128)S(1)}, u32[]{:S(2)}, u32[]{:S(2)}) %collective-permute-start.3) | collective-permute-done | bytes 262176 | tf_op jit(solution)/shard_map/ppermute | solution.py:25
  18.7 6.6 %collective-permute-start.4 = (f32[1,4,128,128]{3,2,1,0:T(8,128)S(1)}, f32[1,4,128,128]{3,2,1,0:T(8,128)S(1)}, u32[]{:S(2)}, u32[]{:S(2)}) collective-permute-start(f32[1,4,128,128]{3,2,1,0:T(8,128)S(1)} %collective-permute-done.3.rest_2_), channel_id=1, source_target_pairs={{0,2},{1,3},{2,0},{3,1},{4,6},{5,7},{6,4},{7,5},{8,10},{9,11},{10,... | collective-permute-start | bytes 786440 | tf_op jit(solution)/shard_map/ppermute | solution.py:25
  25.4 9.1 %collective-permute-done.7.rest_7_ = f32[1,4,128,128]{3,2,1,0:T(8,128)S(1)} collective-permute-done((f32[1,4,128,128]{3,2,1,0:T(8,128)S(1)}, f32[1,4,128,128]{3,2,1,0:T(8,128)S(1)}, u32[]{:S(2)}, u32[]{:S(2)}) %collective-permute-start.7) | collective-permute-done | bytes 262176 | tf_op jit(solution)/shard_map/ppermute | solution.py:25
  35.0 4.0 %collective-permute-done.4.rest_3_ = f32[1,4,128,128]{3,2,1,0:T(8,128)S(1)} collective-permute-done((f32[1,4,128,128]{3,2,1,0:T(8,128)S(1)}, f32[1,4,128,128]{3,2,1,0:T(8,128)S(1)}, u32[]{:S(2)}, u32[]{:S(2)}) %collective-permute-start.4) | collective-permute-done | bytes 262176 | tf_op jit(solution)/shard_map/ppermute | solution.py:25
  39.0 2.2 %collective-permute-start.2 = (f32[1,4,128,128]{3,2,1,0:T(8,128)S(1)}, f32[1,4,128,128]{3,2,1,0:T(8,128)S(1)}, u32[]{:S(2)}, u32[]{:S(2)}) collective-permute-start(f32[1,4,128,128]{3,2,1,0:T(8,128)S(1)} %collective-permute-done.1.rest_0_), channel_id=1, source_target_pairs={{0,2},{1,3},{2,0},{3,1},{4,6},{5,7},{6,4},{7,5},{8,10},{9,11},{10,... | collective-permute-start | bytes 786440 | tf_op jit(solution)/shard_map/ppermute | solution.py:25
  41.2 3.1 %collective-permute-done.6.rest_5_ = f32[1,4,128,128]{3,2,1,0:T(8,128)S(1)} collective-permute-done((f32[1,4,128,128]{3,2,1,0:T(8,128)S(1)}, f32[1,4,128,128]{3,2,1,0:T(8,128)S(1)}, u32[]{:S(2)}, u32[]{:S(2)}) %collective-permute-start.6) | collective-permute-done | bytes 262176 | tf_op jit(solution)/shard_map/ppermute | solution.py:25
  45.2 4.7 %collective-permute-done.2.rest_1_ = f32[1,4,128,128]{3,2,1,0:T(8,128)S(1)} collective-permute-done((f32[1,4,128,128]{3,2,1,0:T(8,128)S(1)}, f32[1,4,128,128]{3,2,1,0:T(8,128)S(1)}, u32[]{:S(2)}, u32[]{:S(2)}) %collective-permute-start.2) | collective-permute-done | bytes 262176 | tf_op jit(solution)/shard_map/ppermute | solution.py:25
  52.7 1.0 copy-done.3
  53.7 1.0 copy-done.4
  54.7 1.0 copy-done.5
  55.7 1.0 copy-done.6
  56.7 15.3 %update.1 = (f32[2,8,256,128]{3,2,1,0:T(8,128)}, f32[2,8,128,128]{3,2,1,0:T(8,128)}, f32[8,128,128]{2,1,0:T(8,128)}, f32[2,5,128,128]{3,2,1,0:T(8,128)}, f32[2,5...) custom-call(s32[64]{0:T(128)S(1)} %reshape.31.meta, ...), custom_call_target="tpu_custom_call" | custom-call | flops 6000000000 | bytes 16777216 | tf_op jit(solution)/shard_map/update/pallas_call | solution.py:192
  72.1 5.7 %collective-permute-start.18 = (f32[2,5,128,128]{3,2,1,0:T(8,128)}, f32[2,5,128,128]{3,2,1,0:T(8,128)S(1)}, u32[]{:S(2)}, u32[]{:S(2)}) collective-permute-start(f32[2,5,128,128]{3,2,1,0:T(8,128)} %get-tuple-element.17), channel_id=1, source_target_pairs={{0,1},{1,0},{2,3},{3,2},{4,5},{5,4},{6,7},{7,6},{8,9},{9,8},{10,11... | collective-permute-start | bytes 1966088 | tf_op jit(solution)/shard_map/ppermute | solution.py:25
  78.2 2.0 %collective-permute-start.17 = (s32[64]{0:T(128)S(1)}, s32[64]{0:T(128)S(1)}, u32[]{:S(2)}, u32[]{:S(2)}) collective-permute-start(s32[64]{0:T(128)S(1)} %reshape.31.meta), channel_id=1, source_target_pairs={{0,1},{1,2},{2,3},{3,4},{4,5},{5,6},{6,7},{7,8},{8,9},{9,10},{10,1... | collective-permute-start | bytes 776 | tf_op jit(solution)/shard_map/ppermute | solution.py:21
  80.2 4.4 %collective-permute-start.26 = (f32[2,5,128,128]{3,2,1,0:T(8,128)}, f32[2,5,128,128]{3,2,1,0:T(8,128)S(1)}, u32[]{:S(2)}, u32[]{:S(2)}) collective-permute-start(f32[2,5,128,128]{3,2,1,0:T(8,128)} %get-tuple-element.23), channel_id=1, source_target_pairs={{0,1},{1,0},{2,3},{3,2},{4,5},{5,4},{6,7},{7,6},{8,9},{9,8},{10,11... | collective-permute-start | bytes 1966088 | tf_op jit(solution)/shard_map/ppermute | solution.py:25
  84.6 2.0 %collective-permute-start.16 = (f32[2,8,128,128]{3,2,1,0:T(8,128)}, f32[2,8,128,128]{3,2,1,0:T(8,128)S(1)}, u32[]{:S(2)}, u32[]{:S(2)}) collective-permute-start(f32[2,8,128,128]{3,2,1,0:T(8,128)} %get-tuple-element.14), channel_id=1, source_target_pairs={{0,1},{1,2},{2,3},{3,4},{4,5},{5,6},{6,7},{7,8},{8,9},{9,10},{10,1... | collective-permute-start | bytes 3145736 | tf_op jit(solution)/shard_map/ppermute | solution.py:21
  86.6 1.0 fusion.9
  88.4 1.0 fusion.6
  89.4 1.4 collective-permute-start.21
  91.7 13.5 %collective-permute-done.21 = f32[5,128,128]{2,1,0:T(8,128)S(1)} collective-permute-done((f32[5,128,128]{2,1,0:T(8,128)S(1)}, f32[5,128,128]{2,1,0:T(8,128)S(1)}, u32[]{:S(2)}, u32[]{:S(2)}) %collective-permute-start.21) | collective-permute-done | bytes 327712 | tf_op jit(solution)/shard_map/ppermute | solution.py:25
  106.2 5.5 %collective-permute-done.24 = f32[5,128,128]{2,1,0:T(8,128)S(1)} collective-permute-done((f32[5,128,128]{2,1,0:T(8,128)S(1)}, f32[5,128,128]{2,1,0:T(8,128)S(1)}, u32[]{:S(2)}, u32[]{:S(2)}) %collective-permute-start.24) | collective-permute-done | bytes 327712 | tf_op jit(solution)/shard_map/ppermute | solution.py:25
  111.7 6.5 %collective-permute-start.22 = (f32[5,128,128]{2,1,0:T(8,128)S(1)}, f32[5,128,128]{2,1,0:T(8,128)S(1)}, u32[]{:S(2)}, u32[]{:S(2)}) collective-permute-start(f32[5,128,128]{2,1,0:T(8,128)S(1)} %fusion.8), channel_id=1, source_target_pairs={{0,12},{1,13},{2,14},{3,15},{4,8},{5,9},{6,10},{7,11},{8,4},{9,5},... | collective-permute-start | bytes 983048 | tf_op jit(solution)/shard_map/ppermute | solution.py:25
  118.3 10.2 %collective-permute-start.25 = (f32[5,128,128]{2,1,0:T(8,128)S(1)}, f32[5,128,128]{2,1,0:T(8,128)S(1)}, u32[]{:S(2)}, u32[]{:S(2)}) collective-permute-start(f32[5,128,128]{2,1,0:T(8,128)S(1)} %fusion.5), channel_id=1, source_target_pairs={{0,8},{1,9},{2,10},{3,11},{4,12},{5,13},{6,14},{7,15},{8,0},{9,1},... | collective-permute-start | bytes 983048 | tf_op jit(solution)/shard_map/ppermute | solution.py:25
  128.6 1.8 %collective-permute-start.28 = (f32[5,128,128]{2,1,0:T(8,128)S(1)}, f32[5,128,128]{2,1,0:T(8,128)S(1)}, u32[]{:S(2)}, u32[]{:S(2)}) collective-permute-start(f32[5,128,128]{2,1,0:T(8,128)S(1)} %fusion.2), channel_id=1, source_target_pairs={{0,4},{1,5},{2,6},{3,7},{4,0},{5,1},{6,2},{7,3},{8,12},{9,13},{10,... | collective-permute-start | bytes 983048 | tf_op jit(solution)/shard_map/ppermute | solution.py:25
  130.4 1.8 %density.1 = f32[8,256,128]{2,1,0:T(8,128)S(1)} custom-call(s32[64]{0:T(128)S(1)} %reshape.31.meta, s32[64]{0:T(128)S(1)} %collective-permute-done.17.above, f32[8,128,128]{2,1,0:T(8,128)S(1)} %copy-done.1), custom_call_target="tpu_custom_call" | custom-call | flops 8388608 | bytes 8388608 | tf_op jit(solution)/shard_map/density/pallas_call | solution.py:254
  132.3 3.6 %finish.1 = f32[2,256,1024]{2,1,0:T(8,128)} custom-call(f32[2,256,1024]{2,1,0:T(8,128)S(1)} %copy-done, f32[2,8,256,128]{3,2,1,0:T(8,128)} %get-tuple-element.13.num_top, f32[2,8,128,128]{3,2,1,0:T(8,128)S(1)} %collective-permute-done.16.received, f32[8,256,128]{2,1,0:T(8,128)S(1)} %density.1), custom_call_target="tpu_custom_call" | custom-call | flops 2097152 | bytes 8388608 | tf_op jit(solution)/shard_map/finish/pallas_call | solution.py:279
  135.9 14.0 %collective-permute-done.25 = f32[5,128,128]{2,1,0:T(8,128)S(1)} collective-permute-done((f32[5,128,128]{2,1,0:T(8,128)S(1)}, f32[5,128,128]{2,1,0:T(8,128)S(1)}, u32[]{:S(2)}, u32[]{:S(2)}) %collective-permute-start.25) | collective-permute-done | bytes 327712 | tf_op jit(solution)/shard_map/ppermute | solution.py:25
  (78 shorter events, 7.8 us)
Async XLA Ops:
  0.6 50.4 %copy-start.7 = (s32[16]{0:T(128)S(1)}, s32[16]{0:T(128)}, u32[]{:S(2)}) copy-start(s32[16]{0:T(128)} %constant.22.clone) | copy-start | bytes 196
  0.7 44.4 %copy-start.13 = (s32[16]{0:T(128)S(1)}, s32[16]{0:T(128)}, u32[]{:S(2)}) copy-start(s32[16]{0:T(128)} %param.15) | copy-start | bytes 196
  0.7 50.3 %copy-start.14 = (s32[8]{0:T(128)S(1)}, s32[8]{0:T(128)}, u32[]{:S(2)}) copy-start(s32[8]{0:T(128)} %param.18) | copy-start | bytes 100
  0.7 18.0 %collective-permute-start.3 = (f32[1,4,128,128]{3,2,1,0:T(8,128)}, f32[1,4,128,128]{3,2,1,0:T(8,128)S(1)}, u32[]{:S(2)}, u32[]{:S(2)}) collective-permute-start(f32[1,4,128,128]{3,2,1,0:T(8,128)} %bitcast.39), channel_id=1, source_target_pairs={{0,8},{1,9},{2,10},{3,11},{4,12},{5,13},{6,14},{7,15},{8,0},{9,1},... | collective-permute-start | bytes 786440 | tf_op jit(solution)/shard_map/ppermute | solution.py:25
  4.8 13.9 %collective-permute-start.5 = (f32[1,4,128,128]{3,2,1,0:T(8,128)}, f32[1,4,128,128]{3,2,1,0:T(8,128)S(1)}, u32[]{:S(2)}, u32[]{:S(2)}) collective-permute-start(f32[1,4,128,128]{3,2,1,0:T(8,128)} %bitcast.40), channel_id=1, source_target_pairs={{0,4},{1,5},{2,6},{3,7},{4,0},{5,1},{6,2},{7,3},{8,12},{9,13},{10,... | collective-permute-start | bytes 786440 | tf_op jit(solution)/shard_map/ppermute | solution.py:25
  6.4 18.9 %collective-permute-start.1 = (f32[1,4,128,128]{3,2,1,0:T(8,128)}, f32[1,4,128,128]{3,2,1,0:T(8,128)S(1)}, u32[]{:S(2)}, u32[]{:S(2)}) collective-permute-start(f32[1,4,128,128]{3,2,1,0:T(8,128)} %bitcast.41), channel_id=1, source_target_pairs={{0,12},{1,13},{2,14},{3,15},{4,8},{5,9},{6,10},{7,11},{8,4},{9,5},... | collective-permute-start | bytes 786440 | tf_op jit(solution)/shard_map/ppermute | solution.py:25
  8.7 44.1 %collective-permute-start = (f32[2,128,1024]{2,1,0:T(8,128)}, f32[2,128,1024]{2,1,0:T(8,128)}, u32[]{:S(2)}, u32[]{:S(2)}) collective-permute-start(f32[2,128,1024]{2,1,0:T(8,128)} %slice.65), channel_id=1, source_target_pairs={{1,0},{2,1},{3,2},{4,3},{5,4},{6,5},{7,6},{8,7},{9,8},{10,9},{11,1... | collective-permute-start | bytes 3145736 | tf_op jit(solution)/shard_map/ppermute | solution.py:21
  10.0 24.5 %collective-permute-start.7 = (f32[1,4,128,128]{3,2,1,0:T(8,128)S(1)}, f32[1,4,128,128]{3,2,1,0:T(8,128)S(1)}, u32[]{:S(2)}, u32[]{:S(2)}) collective-permute-start(f32[1,4,128,128]{3,2,1,0:T(8,128)S(1)} %bitcast.42), channel_id=1, source_target_pairs={{0,2},{1,3},{2,0},{3,1},{4,6},{5,7},{6,4},{7,5},{8,10},{9,11},{10,... | collective-permute-start | bytes 786440 | tf_op jit(solution)/shard_map/ppermute | solution.py:25
  18.7 15.9 %collective-permute-start.14 = (f32[1,4,128,128]{3,2,1,0:T(8,128)S(1)}, f32[1,4,128,128]{3,2,1,0:T(8,128)S(1)}, u32[]{:S(2)}, u32[]{:S(2)}) collective-permute-start(f32[1,4,128,128]{3,2,1,0:T(8,128)S(1)} %bitcast.43), channel_id=1, source_target_pairs={{0,1},{1,0},{2,3},{3,2},{4,5},{5,4},{6,7},{7,6},{8,9},{9,8},{10,11... | collective-permute-start | bytes 786440 | tf_op jit(solution)/shard_map/ppermute | solution.py:25
  18.7 20.4 %collective-permute-start.4 = (f32[1,4,128,128]{3,2,1,0:T(8,128)S(1)}, f32[1,4,128,128]{3,2,1,0:T(8,128)S(1)}, u32[]{:S(2)}, u32[]{:S(2)}) collective-permute-start(f32[1,4,128,128]{3,2,1,0:T(8,128)S(1)} %collective-permute-done.3.rest_2_), channel_id=1, source_target_pairs={{0,2},{1,3},{2,0},{3,1},{4,6},{5,7},{6,4},{7,5},{8,10},{9,11},{10,... | collective-permute-start | bytes 786440 | tf_op jit(solution)/shard_map/ppermute | solution.py:25
  25.3 19.0 %collective-permute-start.6 = (f32[1,4,128,128]{3,2,1,0:T(8,128)S(1)}, f32[1,4,128,128]{3,2,1,0:T(8,128)S(1)}, u32[]{:S(2)}, u32[]{:S(2)}) collective-permute-start(f32[1,4,128,128]{3,2,1,0:T(8,128)S(1)} %collective-permute-done.5.rest_4_), channel_id=1, source_target_pairs={{0,2},{1,3},{2,0},{3,1},{4,6},{5,7},{6,4},{7,5},{8,10},{9,11},{10,... | collective-permute-start | bytes 786440 | tf_op jit(solution)/shard_map/ppermute | solution.py:25
  34.5 15.5 %collective-permute-start.10 = (f32[1,4,128,128]{3,2,1,0:T(8,128)S(1)}, f32[1,4,128,128]{3,2,1,0:T(8,128)S(1)}, u32[]{:S(2)}, u32[]{:S(2)}) collective-permute-start(f32[1,4,128,128]{3,2,1,0:T(8,128)S(1)} %collective-permute-done.3.rest_2_), channel_id=1, source_target_pairs={{0,1},{1,0},{2,3},{3,2},{4,5},{5,4},{6,7},{7,6},{8,9},{9,8},{10,11... | collective-permute-start | bytes 786440 | tf_op jit(solution)/shard_map/ppermute | solution.py:25
  34.5 15.9 %collective-permute-start.12 = (f32[1,4,128,128]{3,2,1,0:T(8,128)S(1)}, f32[1,4,128,128]{3,2,1,0:T(8,128)S(1)}, u32[]{:S(2)}, u32[]{:S(2)}) collective-permute-start(f32[1,4,128,128]{3,2,1,0:T(8,128)S(1)} %collective-permute-done.5.rest_4_), channel_id=1, source_target_pairs={{0,1},{1,0},{2,3},{3,2},{4,5},{5,4},{6,7},{7,6},{8,9},{9,8},{10,11... | collective-permute-start | bytes 786440 | tf_op jit(solution)/shard_map/ppermute | solution.py:25
  39.0 10.9 %collective-permute-start.2 = (f32[1,4,128,128]{3,2,1,0:T(8,128)S(1)}, f32[1,4,128,128]{3,2,1,0:T(8,128)S(1)}, u32[]{:S(2)}, u32[]{:S(2)}) collective-permute-start(f32[1,4,128,128]{3,2,1,0:T(8,128)S(1)} %collective-permute-done.1.rest_0_), channel_id=1, source_target_pairs={{0,2},{1,3},{2,0},{3,1},{4,6},{5,7},{6,4},{7,5},{8,10},{9,11},{10,... | collective-permute-start | bytes 786440 | tf_op jit(solution)/shard_map/ppermute | solution.py:25
  44.3 6.2 %collective-permute-start.8 = (f32[1,4,128,128]{3,2,1,0:T(8,128)S(1)}, f32[1,4,128,128]{3,2,1,0:T(8,128)S(1)}, u32[]{:S(2)}, u32[]{:S(2)}) collective-permute-start(f32[1,4,128,128]{3,2,1,0:T(8,128)S(1)} %collective-permute-done.1.rest_0_), channel_id=1, source_target_pairs={{0,1},{1,0},{2,3},{3,2},{4,5},{5,4},{6,7},{7,6},{8,9},{9,8},{10,11... | collective-permute-start | bytes 786440 | tf_op jit(solution)/shard_map/ppermute | solution.py:25
  49.9 1.7 %collective-permute-start.15 = (f32[1,4,128,128]{3,2,1,0:T(8,128)S(1)}, f32[1,4,128,128]{3,2,1,0:T(8,128)S(1)}, u32[]{:S(2)}, u32[]{:S(2)}) collective-permute-start(f32[1,4,128,128]{3,2,1,0:T(8,128)S(1)} %collective-permute-done.7.rest_7_), channel_id=1, source_target_pairs={{0,1},{1,0},{2,3},{3,2},{4,5},{5,4},{6,7},{7,6},{8,9},{9,8},{10,11... | collective-permute-start | bytes 786440 | tf_op jit(solution)/shard_map/ppermute | solution.py:25
  50.0 2.0 %collective-permute-start.11 = (f32[1,4,128,128]{3,2,1,0:T(8,128)S(1)}, f32[1,4,128,128]{3,2,1,0:T(8,128)}, u32[]{:S(2)}, u32[]{:S(2)}) collective-permute-start(f32[1,4,128,128]{3,2,1,0:T(8,128)S(1)} %collective-permute-done.4.rest_3_), channel_id=1, source_target_pairs={{0,1},{1,0},{2,3},{3,2},{4,5},{5,4},{6,7},{7,6},{8,9},{9,8},{10,11... | collective-permute-start | bytes 786440 | tf_op jit(solution)/shard_map/ppermute | solution.py:25
  50.4 1.9 %collective-permute-start.13 = (f32[1,4,128,128]{3,2,1,0:T(8,128)S(1)}, f32[1,4,128,128]{3,2,1,0:T(8,128)}, u32[]{:S(2)}, u32[]{:S(2)}) collective-permute-start(f32[1,4,128,128]{3,2,1,0:T(8,128)S(1)} %collective-permute-done.6.rest_5_), channel_id=1, source_target_pairs={{0,1},{1,0},{2,3},{3,2},{4,5},{5,4},{6,7},{7,6},{8,9},{9,8},{10,11... | collective-permute-start | bytes 786440 | tf_op jit(solution)/shard_map/ppermute | solution.py:25
  50.5 2.2 %collective-permute-start.9 = (f32[1,4,128,128]{3,2,1,0:T(8,128)S(1)}, f32[1,4,128,128]{3,2,1,0:T(8,128)}, u32[]{:S(2)}, u32[]{:S(2)}) collective-permute-start(f32[1,4,128,128]{3,2,1,0:T(8,128)S(1)} %collective-permute-done.2.rest_1_), channel_id=1, source_target_pairs={{0,1},{1,0},{2,3},{3,2},{4,5},{5,4},{6,7},{7,6},{8,9},{9,8},{10,11... | collective-permute-start | bytes 786440 | tf_op jit(solution)/shard_map/ppermute | solution.py:25
  72.1 12.5 %collective-permute-start.18 = (f32[2,5,128,128]{3,2,1,0:T(8,128)}, f32[2,5,128,128]{3,2,1,0:T(8,128)S(1)}, u32[]{:S(2)}, u32[]{:S(2)}) collective-permute-start(f32[2,5,128,128]{3,2,1,0:T(8,128)} %get-tuple-element.17), channel_id=1, source_target_pairs={{0,1},{1,0},{2,3},{3,2},{4,5},{5,4},{6,7},{7,6},{8,9},{9,8},{10,11... | collective-permute-start | bytes 1966088 | tf_op jit(solution)/shard_map/ppermute | solution.py:25
  77.7 9.9 %collective-permute-start.20 = (f32[2,5,128,128]{3,2,1,0:T(8,128)}, f32[2,5,128,128]{3,2,1,0:T(8,128)S(1)}, u32[]{:S(2)}, u32[]{:S(2)}) collective-permute-start(f32[2,5,128,128]{3,2,1,0:T(8,128)} %get-tuple-element.19), channel_id=1, source_target_pairs={{0,1},{1,0},{2,3},{3,2},{4,5},{5,4},{6,7},{7,6},{8,9},{9,8},{10,11... | collective-permute-start | bytes 1966088 | tf_op jit(solution)/shard_map/ppermute | solution.py:25
  77.8 11.6 %collective-permute-start.23 = (f32[2,5,128,128]{3,2,1,0:T(8,128)}, f32[2,5,128,128]{3,2,1,0:T(8,128)S(1)}, u32[]{:S(2)}, u32[]{:S(2)}) collective-permute-start(f32[2,5,128,128]{3,2,1,0:T(8,128)} %get-tuple-element.21), channel_id=1, source_target_pairs={{0,1},{1,0},{2,3},{3,2},{4,5},{5,4},{6,7},{7,6},{8,9},{9,8},{10,11... | collective-permute-start | bytes 1966088 | tf_op jit(solution)/shard_map/ppermute | solution.py:25
  78.2 50.4 %collective-permute-start.17 = (s32[64]{0:T(128)S(1)}, s32[64]{0:T(128)S(1)}, u32[]{:S(2)}, u32[]{:S(2)}) collective-permute-start(s32[64]{0:T(128)S(1)} %reshape.31.meta), channel_id=1, source_target_pairs={{0,1},{1,2},{2,3},{3,4},{4,5},{5,6},{6,7},{7,8},{8,9},{9,10},{10,1... | collective-permute-start | bytes 776 | tf_op jit(solution)/shard_map/ppermute | solution.py:21
  80.2 10.6 %collective-permute-start.26 = (f32[2,5,128,128]{3,2,1,0:T(8,128)}, f32[2,5,128,128]{3,2,1,0:T(8,128)S(1)}, u32[]{:S(2)}, u32[]{:S(2)}) collective-permute-start(f32[2,5,128,128]{3,2,1,0:T(8,128)} %get-tuple-element.23), channel_id=1, source_target_pairs={{0,1},{1,0},{2,3},{3,2},{4,5},{5,4},{6,7},{7,6},{8,9},{9,8},{10,11... | collective-permute-start | bytes 1966088 | tf_op jit(solution)/shard_map/ppermute | solution.py:25
  84.6 47.7 %collective-permute-start.16 = (f32[2,8,128,128]{3,2,1,0:T(8,128)}, f32[2,8,128,128]{3,2,1,0:T(8,128)S(1)}, u32[]{:S(2)}, u32[]{:S(2)}) collective-permute-start(f32[2,8,128,128]{3,2,1,0:T(8,128)} %get-tuple-element.14), channel_id=1, source_target_pairs={{0,1},{1,2},{2,3},{3,4},{4,5},{5,6},{6,7},{7,8},{8,9},{9,10},{10,1... | collective-permute-start | bytes 3145736 | tf_op jit(solution)/shard_map/ppermute | solution.py:21
  87.6 48.3 %collective-permute-start.19 = (f32[5,128,128]{2,1,0:T(8,128)S(1)}, f32[5,128,128]{2,1,0:T(8,128)S(1)}, u32[]{:S(2)}, u32[]{:S(2)}) collective-permute-start(f32[5,128,128]{2,1,0:T(8,128)S(1)} %fusion.9), channel_id=1, source_target_pairs={{0,2},{1,3},{2,0},{3,1},{4,6},{5,7},{6,4},{7,5},{8,10},{9,11},{10,... | collective-permute-start | bytes 983048 | tf_op jit(solution)/shard_map/ppermute | solution.py:25
  89.4 15.8 %collective-permute-start.21 = (f32[5,128,128]{2,1,0:T(8,128)S(1)}, f32[5,128,128]{2,1,0:T(8,128)S(1)}, u32[]{:S(2)}, u32[]{:S(2)}) collective-permute-start(f32[5,128,128]{2,1,0:T(8,128)S(1)} %fusion.6), channel_id=1, source_target_pairs={{0,2},{1,3},{2,0},{3,1},{4,6},{5,7},{6,4},{7,5},{8,10},{9,11},{10,... | collective-permute-start | bytes 983048 | tf_op jit(solution)/shard_map/ppermute | solution.py:25
  90.9 20.8 %collective-permute-start.24 = (f32[5,128,128]{2,1,0:T(8,128)S(1)}, f32[5,128,128]{2,1,0:T(8,128)S(1)}, u32[]{:S(2)}, u32[]{:S(2)}) collective-permute-start(f32[5,128,128]{2,1,0:T(8,128)S(1)} %fusion.3), channel_id=1, source_target_pairs={{0,2},{1,3},{2,0},{3,1},{4,6},{5,7},{6,4},{7,5},{8,10},{9,11},{10,... | collective-permute-start | bytes 983048 | tf_op jit(solution)/shard_map/ppermute | solution.py:25
  105.2 13.1 %collective-permute-start.27 = (f32[5,128,128]{2,1,0:T(8,128)S(1)}, f32[5,128,128]{2,1,0:T(8,128)S(1)}, u32[]{:S(2)}, u32[]{:S(2)}) collective-permute-start(f32[5,128,128]{2,1,0:T(8,128)S(1)} %fusion), channel_id=1, source_target_pairs={{0,2},{1,3},{2,0},{3,1},{4,6},{5,7},{6,4},{7,5},{8,10},{9,11},{10,... | collective-permute-start | bytes 983048 | tf_op jit(solution)/shard_map/ppermute | solution.py:25
  111.7 24.2 %collective-permute-start.22 = (f32[5,128,128]{2,1,0:T(8,128)S(1)}, f32[5,128,128]{2,1,0:T(8,128)S(1)}, u32[]{:S(2)}, u32[]{:S(2)}) collective-permute-start(f32[5,128,128]{2,1,0:T(8,128)S(1)} %fusion.8), channel_id=1, source_target_pairs={{0,12},{1,13},{2,14},{3,15},{4,8},{5,9},{6,10},{7,11},{8,4},{9,5},... | collective-permute-start | bytes 983048 | tf_op jit(solution)/shard_map/ppermute | solution.py:25
  118.3 31.6 %collective-permute-start.25 = (f32[5,128,128]{2,1,0:T(8,128)S(1)}, f32[5,128,128]{2,1,0:T(8,128)S(1)}, u32[]{:S(2)}, u32[]{:S(2)}) collective-permute-start(f32[5,128,128]{2,1,0:T(8,128)S(1)} %fusion.5), channel_id=1, source_target_pairs={{0,8},{1,9},{2,10},{3,11},{4,12},{5,13},{6,14},{7,15},{8,0},{9,1},... | collective-permute-start | bytes 983048 | tf_op jit(solution)/shard_map/ppermute | solution.py:25
  128.6 21.3 %collective-permute-start.28 = (f32[5,128,128]{2,1,0:T(8,128)S(1)}, f32[5,128,128]{2,1,0:T(8,128)S(1)}, u32[]{:S(2)}, u32[]{:S(2)}) collective-permute-start(f32[5,128,128]{2,1,0:T(8,128)S(1)} %fusion.2), channel_id=1, source_target_pairs={{0,4},{1,5},{2,6},{3,7},{4,0},{5,1},{6,2},{7,3},{8,12},{9,13},{10,... | collective-permute-start | bytes 983048 | tf_op jit(solution)/shard_map/ppermute | solution.py:25
  (12 other events, 211.9 us)

commit v2 on v1

--- a/solution.py
+++ b/solution.py
@@ -25,6 +25,30 @@
     return lax.ppermute(block, "row", [(i, i ^ mask) for i in range(lax.axis_size("row"))])
 
 
+FAR, NEAR = (8, 10, 14, 12), (0, 2, 6, 4)
+
+
+def reduced(far, near):
+    half = far[0].shape[2] // 2
+    totals = []
+    for part, (first, second) in enumerate(((2, 4), (4, 2))):
+        rows = slice(part * half, (part + 1) * half)
+        sent, kept = ((1, 2), (0, 3)) if first == 2 else ((3, 2), (0, 1))
+
+        def pick(pair, at):
+            return pair[0][at, :, rows] + pair[1][at, :, rows]
+
+        def once(pair):
+            got = swapped(jnp.stack([pick(pair, at) for at in sent]), first)
+            return pick(pair, kept[0]) + got[0], pick(pair, kept[1]) + got[1]
+
+        outer, across = once(far)
+        inner, beside = once(near)
+        outer = outer + swapped(across, second)
+        totals.append(inner + swapped(beside, second) + swapped(outer, 8))
+    return jnp.concatenate(totals, axis=1)
+
+
 def split(value):
     high = value.astype(jnp.bfloat16)
     low = (value - high.astype(jnp.float32)).astype(jnp.bfloat16)
@@ -57,13 +81,14 @@
     return jnp.dot(table, jnp.concatenate([high, low, high], axis=0), preferred_element_type=jnp.float32)
 
 
-def update_kernel(dims, meta, slot_of, live, amplitudes, obj, rim, right_f, left_f, left_i, right_i, *rest):
+def update_kernel(dims, meta, slot_of, live, amplitudes, obj, rim, *rest):
     piece_sizes, group_sizes, slots = dims
-    pieces = rest[: len(piece_sizes)]
-    rest = rest[len(piece_sizes) :]
+    tables = rest[:4]
+    pieces = rest[4 : 4 + len(piece_sizes)]
+    rest = rest[4 + len(piece_sizes) :]
     num_top, num_low, squares = rest[:3]
     groups = rest[3 : 3 + len(group_sizes)]
-    table, ext, acc, part, piece_sems, out_sems = rest[3 + len(group_sizes) :]
+    table, ext, acc, part, right_f, left_f, left_i, right_i, piece_sems, out_sems = rest[3 + len(group_sizes) :]
     points = LANES
     tile_rows = obj.shape[1]
     blocks = obj.shape[2] // LANES
@@ -74,6 +99,8 @@
     for k, size in enumerate(piece_sizes):
         copies.append(pltpu.make_async_copy(pieces[k], table.at[pl.ds(at, size)], piece_sems.at[k]))
         at += size
+    for k, (source, target) in enumerate(zip(tables, (right_f, left_f, left_i, right_i))):
+        copies.append(pltpu.make_async_copy(source, target, piece_sems.at[len(piece_sizes) + k]))
     for copy in copies:
         copy.start()
     for b in range(blocks):
@@ -197,14 +224,17 @@
             jax.ShapeDtypeStruct((scans, points, points), f32),
         ]
         + [jax.ShapeDtypeStruct((size, channels + 1, points, points), f32) for size in group_sizes],
-        in_specs=[smem] * 3 + [vmem] * 7 + [anywhere] * len(pieces),
+        in_specs=[smem] * 3 + [vmem] * 3 + [anywhere] * (4 + len(pieces)),
         out_specs=[anywhere, anywhere, vmem] + [anywhere] * len(group_sizes),
         scratch_shapes=[
             pltpu.VMEM((slots, channels, points, points), f32),
             pltpu.VMEM((2, blocks + 1, tile_rows + points, LANES), f32),
             pltpu.VMEM((2, blocks + 1, tile_rows + points, LANES), f32),
             pltpu.VMEM((slots, channels + 1, points, points), f32),
-            pltpu.SemaphoreType.DMA((len(pieces),)),
+        ]
+        + [pltpu.VMEM(factor.shape, factor.dtype) for factor in tables]
+        + [
+            pltpu.SemaphoreType.DMA((len(pieces) + 4,)),
             pltpu.SemaphoreType.DMA((len(group_sizes) + 2,)),
         ],
         compiler_params=pltpu.CompilerParams(vmem_limit_bytes=VMEM_BYTES),
@@ -306,18 +336,20 @@
 
     if swaps:
         held = {0: own_probe}
-        for far in (12, 8, 4):
-            held[far] = swapped(own_probe, far)
-        for far in (0, 12, 8, 4):
-            held[far | 2] = swapped(held[far], 2)
-        for far in (0, 2, 12, 14, 8, 10, 4, 6):
-            held[far | 1] = swapped(held[far], 1)
-        order = [far | side | core for core in (0, 1) for far in (12, 8, 4, 0) for side in (0, 2)]
-        pieces = [held[k] for k in order]
+        for key in (8, 4, 2):
+            held[key] = swapped(own_probe, key)
+        held[6] = swapped(held[4], 2)
+        held[12] = swapped(held[8], 4)
+        held[10] = swapped(held[8], 2)
+        held[14] = swapped(held[12], 2)
+        for key in list(held):
+            held[key | 1] = swapped(held[key], 1)
+        order = [key | core for core in (0, 1) for key in FAR + NEAR]
+        pieces = [held[key] for key in order]
         place = np.zeros(size, np.int32)
         place[np.array(order)] = np.arange(size)
         slot_of = jnp.asarray(place)[jnp.bitwise_xor(owner, device)]
-        group_sizes = (2,) * 8
+        group_sizes = (4,) * 4
     else:
         owned = (owner == device)[:, None, None, None]
         pieces = [lax.psum(jnp.where(owned, own_probe, 0.0), "row")]
@@ -329,20 +361,13 @@
         meta, slot_of, counts, amplitudes, object_strip, rim, transform_tables(points), pieces, group_sizes
     )
 
+    received = moved(num_low, 1)
     if swaps:
-        mine, theirs = groups[:4], groups[4:]
-        other = [swapped(block, 1) for block in theirs]
-        near = []
-        for j in range(4):
-            across = swapped(mine[j][1] + other[j][1], 2)
-            near.append(mine[j][0] + other[j][0] + across)
-        total = near[3]
-        for j, far in enumerate((12, 8, 4)):
-            total = total + swapped(near[j], far)
+        mine_far, mine_near, theirs_far, theirs_near = groups
+        total = reduced((mine_far, swapped(theirs_far, 1)), (mine_near, swapped(theirs_near, 1)))
     else:
         summed = lax.psum(groups[0], "row")
         total = jnp.sum(jnp.where(owned, summed, 0.0), axis=0)
-    received = moved(num_low, 1)
     density = density_of(meta, above, squares, tile_rows, blocks)
     new_object = finish(object_strip, num_top, received, density)
     new_probes = own_probe[0] + total[:channels] / (total[channels] + damping)

time: 152 us -> 131 us (0.86)
  waiting for transfers between devices: 61.4 us -> 44.7 us
  starting transfers between devices: 56.6 us -> 44.6 us
  Pallas kernels: 20.7 us -> 29.5 us
    ppermute x26 -> x27, starting transfers between devices: 51.4 us -> 29.7 us  [swapped(): lax.ppermute(block, 'row', [(i, i ^ mask) for i in range(lax.axis_size('r...]
    ppermute x26 -> x27, waiting for transfers between devices: 61.4 us -> 44.7 us  [swapped(): lax.ppermute(block, 'row', [(i, i ^ mask) for i in range(lax.axis_size('r...]
    ppermute x3, starting transfers between devices: 5.24 us -> 14.9 us  [moved(): lax.ppermute(block, 'row', [(i, i + distance) for i in range(size) if 0 <...]
    pallas_call x1, Pallas kernels: 15.3 us -> 23.4 us  [update(): pl.pallas_call(functools.partial(update_kernel, (piece_sizes, group_sizes...]
    unnamed x30 -> x26, local copies, waits for them, and re-layouts: 4.03 us -> 4.02 us
  transfers between devices with their start and end apart: 29 -> 30, of which waited for: 11 -> 11; matrix products, arithmetic and copies ran while one was open for 4% -> 4% of each run, Pallas kernels for 4% -> 5%
where the time goes in v2:
time: 131 us; the launch traced here: 130 us
  waiting for transfers between devices  44.7 us (34%)
  starting transfers between devices  44.6 us (34%)
  Pallas kernels  29.5 us (23%)
  local copies, waits for them, and re-layouts  7.14 us (5%)
  other arithmetic  2.62 us (2%)
  between operations  1.6 us (1%)
    ppermute x27, waiting for transfers between devices, swapped(): lax.ppermute(block, 'row', [(i, i ^ mask) for i in range(lax.axis_size('r...  44.7 us
    ppermute x27, starting transfers between devices, swapped(): lax.ppermute(block, 'row', [(i, i ^ mask) for i in range(lax.axis_size('r...  29.7 us
    pallas_call x1, Pallas kernels, update(): pl.pallas_call(functools.partial(update_kernel, (piece_sizes, group_sizes...  23.4 us
    ppermute x3, starting transfers between devices, moved(): lax.ppermute(block, 'row', [(i, i + distance) for i in range(size) if 0 <...  14.9 us
    unnamed x26, local copies, waits for them, and re-layouts  4.02 us
    pallas_call x1, Pallas kernels, finish(): pl.pallas_call(finish_kernel, out_shape=jax.ShapeDtypeStruct(obj.shape, o...  3.51 us
  transfers between devices with their start and end apart: 30, of which 11 were waited for; matrix products, arithmetic and copies ran while one was open for 4% of the time, Pallas kernels for 5%

profile of v2, /device:TPU:0, one launch (start us, length us, event | category | flops | bytes accessed | tf_op | source)
XLA Modules:
  0.0 130.2 jit_solution(6215181646888275974)
XLA Ops:
  0.7 4.1 %collective-permute-start.1 = (f32[1,4,128,128]{3,2,1,0:T(8,128)}, f32[1,4,128,128]{3,2,1,0:T(8,128)S(1)}, u32[]{:S(2)}, u32[]{:S(2)}) collective-permute-start(f32[1,4,128,128]{3,2,1,0:T(8,128)} %bitcast.37), channel_id=1, source_target_pairs={{0,8},{1,9},{2,10},{3,11},{4,12},{5,13},{6,14},{7,15},{8,0},{9,1},... | collective-permute-start | bytes 786440 | tf_op jit(solution)/shard_map/ppermute | solution.py:25
  4.8 1.6 %collective-permute-start.6 = (f32[1,4,128,128]{3,2,1,0:T(8,128)}, f32[1,4,128,128]{3,2,1,0:T(8,128)S(1)}, u32[]{:S(2)}, u32[]{:S(2)}) collective-permute-start(f32[1,4,128,128]{3,2,1,0:T(8,128)} %bitcast.38), channel_id=1, source_target_pairs={{0,4},{1,5},{2,6},{3,7},{4,0},{5,1},{6,2},{7,3},{8,12},{9,13},{10,... | collective-permute-start | bytes 786440 | tf_op jit(solution)/shard_map/ppermute | solution.py:25
  6.4 1.5 %collective-permute-start.5 = (f32[1,4,128,128]{3,2,1,0:T(8,128)}, f32[1,4,128,128]{3,2,1,0:T(8,128)S(1)}, u32[]{:S(2)}, u32[]{:S(2)}) collective-permute-start(f32[1,4,128,128]{3,2,1,0:T(8,128)} %bitcast.39), channel_id=1, source_target_pairs={{0,2},{1,3},{2,0},{3,1},{4,6},{5,7},{6,4},{7,5},{8,10},{9,11},{10,... | collective-permute-start | bytes 786440 | tf_op jit(solution)/shard_map/ppermute | solution.py:25
  7.9 2.3 %slice.137 = f32[2,128,1024]{2,1,0:T(8,128)} slice(f32[2,256,1024]{2,1,0:T(8,128)} %obj.3), slice={[0:2], [0:128], [0:1024]} | slice | bytes 2097152 | tf_op jit(solution)/shard_map/slice | solution.py:358
  10.2 1.3 collective-permute-start
  11.5 1.2 collective-permute-start.12
  12.7 4.3 %collective-permute-done.1.rest_4_ = f32[1,4,128,128]{3,2,1,0:T(8,128)S(1)} collective-permute-done((f32[1,4,128,128]{3,2,1,0:T(8,128)}, f32[1,4,128,128]{3,2,1,0:T(8,128)S(1)}, u32[]{:S(2)}, u32[]{:S(2)}) %collective-permute-start.1) | collective-permute-done | bytes 262176 | tf_op jit(solution)/shard_map/ppermute | solution.py:25
  17.8 1.5 %collective-permute-start.2 = (f32[1,4,128,128]{3,2,1,0:T(8,128)S(1)}, f32[1,4,128,128]{3,2,1,0:T(8,128)S(1)}, u32[]{:S(2)}, u32[]{:S(2)}) collective-permute-start(f32[1,4,128,128]{3,2,1,0:T(8,128)S(1)} %collective-permute-done.1.rest_4_), channel_id=1, source_target_pairs={{0,2},{1,3},{2,0},{3,1},{4,6},{5,7},{6,4},{7,5},{8,10},{9,11},{10,... | collective-permute-start | bytes 786440 | tf_op jit(solution)/shard_map/ppermute | solution.py:25
  19.8 14.3 %collective-permute-done.3.rest_7_ = f32[1,4,128,128]{3,2,1,0:T(8,128)S(1)} collective-permute-done((f32[1,4,128,128]{3,2,1,0:T(8,128)S(1)}, f32[1,4,128,128]{3,2,1,0:T(8,128)S(1)}, u32[]{:S(2)}, u32[]{:S(2)}) %collective-permute-start.3) | collective-permute-done | bytes 262176 | tf_op jit(solution)/shard_map/ppermute | solution.py:25
  34.6 4.7 %collective-permute-done.7.rest_10_ = f32[1,4,128,128]{3,2,1,0:T(8,128)S(1)} collective-permute-done((f32[1,4,128,128]{3,2,1,0:T(8,128)S(1)}, f32[1,4,128,128]{3,2,1,0:T(8,128)S(1)}, u32[]{:S(2)}, u32[]{:S(2)}) %collective-permute-start.7) | collective-permute-done | bytes 262176 | tf_op jit(solution)/shard_map/ppermute | solution.py:25
  39.3 2.5 %collective-permute-start.4 = (f32[1,4,128,128]{3,2,1,0:T(8,128)S(1)}, f32[1,4,128,128]{3,2,1,0:T(8,128)S(1)}, u32[]{:S(2)}, u32[]{:S(2)}) collective-permute-start(f32[1,4,128,128]{3,2,1,0:T(8,128)S(1)} %collective-permute-done.3.rest_7_), channel_id=1, source_target_pairs={{0,2},{1,3},{2,0},{3,1},{4,6},{5,7},{6,4},{7,5},{8,10},{9,11},{10,... | collective-permute-start | bytes 786440 | tf_op jit(solution)/shard_map/ppermute | solution.py:25
  43.3 4.4 %collective-permute-done.4.rest_6_ = f32[1,4,128,128]{3,2,1,0:T(8,128)S(1)} collective-permute-done((f32[1,4,128,128]{3,2,1,0:T(8,128)S(1)}, f32[1,4,128,128]{3,2,1,0:T(8,128)S(1)}, u32[]{:S(2)}, u32[]{:S(2)}) %collective-permute-start.4) | collective-permute-done | bytes 262176 | tf_op jit(solution)/shard_map/ppermute | solution.py:25
  49.4 1.0 copy-done.3
  50.4 1.0 copy-done.4
  51.4 1.0 copy-done.5
  52.4 1.0 copy-done.6
  53.4 23.4 %update.1 = (f32[2,8,256,128]{3,2,1,0:T(8,128)}, f32[2,8,128,128]{3,2,1,0:T(8,128)}, f32[8,128,128]{2,1,0:T(8,128)}, f32[4,5,128,128]{3,2,1,0:T(8,128)}, f32[4,5...) custom-call(s32[64]{0:T(128)S(1)} %reshape.39.meta, s32[8]{0:T(128)S(1)} %gather_fusion, ...), custom_call_target="tpu_custom_call" | custom-call | flops 6000000000 | bytes 16777216 | tf_op jit(solution)/shard_map/update/pallas_call | solution.py:219
  77.3 2.0 %collective-permute-start.16 = (f32[2,8,128,128]{3,2,1,0:T(8,128)}, f32[2,8,128,128]{3,2,1,0:T(8,128)S(1)}, u32[]{:S(2)}, u32[]{:S(2)}) collective-permute-start(f32[2,8,128,128]{3,2,1,0:T(8,128)} %get-tuple-element.10), channel_id=1, source_target_pairs={{0,1},{1,2},{2,3},{3,4},{4,5},{5,6},{6,7},{7,8},{8,9},{9,10},{10,1... | collective-permute-start | bytes 3145736 | tf_op jit(solution)/shard_map/ppermute | solution.py:21
  80.1 1.3 %slice_add_fusion.4 = (f32[1,5,64,128]{3,2,1,0:T(8,128)S(1)}, f32[1,5,64,128]{3,2,1,0:T(8,128)S(1)}, f32[1,5,64,128]{3,2,1,0:T(8,128)S(1)}, f32[1,5,64,128]{3,2,1,0:T(8,128)S(1)}) fusion(f32[4,5,128,128]{3,2,1,0:T(8,128)S(1)} %collective-permute-done.21, f32[4,5,128,128]{3,2,1,0:T(8,128)} %get-tuple-element.14), kind=kLoop, calls=%fused_computation.17 | loop fusion | flops 163840 | bytes 1966080 | tf_op jit(solution)/shard_map/add | solution.py:39
  81.5 2.0 %collective-permute-start.27 = (f32[2,5,64,128]{3,2,1,0:T(8,128)S(1)}, f32[2,5,64,128]{3,2,1,0:T(8,128)S(1)}, u32[]{:S(2)}, u32[]{:S(2)}) collective-permute-start(f32[2,5,64,128]{3,2,1,0:T(8,128)S(1)} %pad_maximum_fusion.3), channel_id=1, source_target_pairs={{0,4},{1,5},{2,6},{3,7},{4,0},{5,1},{6,2},{7,3},{8,12},{9,13},{10,... | collective-permute-start | bytes 983048 | tf_op jit(solution)/shard_map/ppermute | solution.py:25
  83.9 2.1 %collective-permute-start.25 = (f32[2,5,64,128]{3,2,1,0:T(8,128)S(1)}, f32[2,5,64,128]{3,2,1,0:T(8,128)S(1)}, u32[]{:S(2)}, u32[]{:S(2)}) collective-permute-start(f32[2,5,64,128]{3,2,1,0:T(8,128)S(1)} %pad_maximum_fusion.2), channel_id=1, source_target_pairs={{0,4},{1,5},{2,6},{3,7},{4,0},{5,1},{6,2},{7,3},{8,12},{9,13},{10,... | collective-permute-start | bytes 983048 | tf_op jit(solution)/shard_map/ppermute | solution.py:25
  85.9 6.1 %collective-permute-done.22 = f32[2,5,64,128]{3,2,1,0:T(8,128)S(1)} collective-permute-done((f32[2,5,64,128]{3,2,1,0:T(8,128)S(1)}, f32[2,5,64,128]{3,2,1,0:T(8,128)S(1)}, u32[]{:S(2)}, u32[]{:S(2)}) %collective-permute-start.22) | collective-permute-done | bytes 327712 | tf_op jit(solution)/shard_map/ppermute | solution.py:25
  92.1 11.6 %collective-permute-start.17 = (s32[64]{0:T(128)S(1)}, s32[64]{0:T(128)S(1)}, u32[]{:S(2)}, u32[]{:S(2)}) collective-permute-start(s32[64]{0:T(128)S(1)} %reshape.39.meta), channel_id=1, source_target_pairs={{0,1},{1,2},{2,3},{3,4},{4,5},{5,6},{6,7},{7,8},{8,9},{9,10},{10,1... | collective-permute-start | bytes 776 | tf_op jit(solution)/shard_map/ppermute | solution.py:21
  103.8 2.1 %collective-permute-start.23 = (f32[5,64,128]{2,1,0:T(8,128)S(1)}, f32[5,64,128]{2,1,0:T(8,128)S(1)}, u32[]{:S(2)}, u32[]{:S(2)}) collective-permute-start(f32[5,64,128]{2,1,0:T(8,128)S(1)} %get-tuple-element.27), channel_id=1, source_target_pairs={{0,4},{1,5},{2,6},{3,7},{4,0},{5,1},{6,2},{7,3},{8,12},{9,13},{10,... | collective-permute-start | bytes 491528 | tf_op jit(solution)/shard_map/ppermute | solution.py:25
  105.9 2.2 %collective-permute-start.28 = (f32[5,64,128]{2,1,0:T(8,128)S(1)}, f32[5,64,128]{2,1,0:T(8,128)S(1)}, u32[]{:S(2)}, u32[]{:S(2)}) collective-permute-start(f32[5,64,128]{2,1,0:T(8,128)S(1)} %get-tuple-element.26), channel_id=1, source_target_pairs={{0,2},{1,3},{2,0},{3,1},{4,6},{5,7},{6,4},{7,5},{8,10},{9,11},{10,... | collective-permute-start | bytes 491528 | tf_op jit(solution)/shard_map/ppermute | solution.py:25
  108.3 2.0 %collective-permute-done.23 = f32[5,64,128]{2,1,0:T(8,128)S(1)} collective-permute-done((f32[5,64,128]{2,1,0:T(8,128)S(1)}, f32[5,64,128]{2,1,0:T(8,128)S(1)}, u32[]{:S(2)}, u32[]{:S(2)}) %collective-permute-start.23) | collective-permute-done | bytes 163872 | tf_op jit(solution)/shard_map/ppermute | solution.py:25
  110.2 2.8 %collective-permute-start.26 = (f32[5,64,128]{2,1,0:T(8,128)S(1)}, f32[5,64,128]{2,1,0:T(8,128)S(1)}, u32[]{:S(2)}, u32[]{:S(2)}) collective-permute-start(f32[5,64,128]{2,1,0:T(8,128)S(1)} %get-tuple-element.18), channel_id=1, source_target_pairs={{0,2},{1,3},{2,0},{3,1},{4,6},{5,7},{6,4},{7,5},{8,10},{9,11},{10,... | collective-permute-start | bytes 491528 | tf_op jit(solution)/shard_map/ppermute | solution.py:25
  113.2 2.6 %collective-permute-start.24 = (f32[5,64,128]{2,1,0:T(8,128)S(1)}, f32[5,64,128]{2,1,0:T(8,128)S(1)}, u32[]{:S(2)}, u32[]{:S(2)}) collective-permute-start(f32[5,64,128]{2,1,0:T(8,128)S(1)} %get-tuple-element.25), channel_id=1, source_target_pairs={{0,8},{1,9},{2,10},{3,11},{4,12},{5,13},{6,14},{7,15},{8,0},{9,1},... | collective-permute-start | bytes 491528 | tf_op jit(solution)/shard_map/ppermute | solution.py:25
  116.2 2.6 %density.1 = f32[8,256,128]{2,1,0:T(8,128)S(1)} custom-call(s32[64]{0:T(128)S(1)} %reshape.39.meta, s32[64]{0:T(128)S(1)} %collective-permute-done.17.above, f32[8,128,128]{2,1,0:T(8,128)S(1)} %copy-done.1), custom_call_target="tpu_custom_call" | custom-call | flops 8388608 | bytes 8388608 | tf_op jit(solution)/shard_map/density/pallas_call | solution.py:284
  118.8 3.5 %finish.1 = f32[2,256,1024]{2,1,0:T(8,128)} custom-call(f32[2,256,1024]{2,1,0:T(8,128)S(1)} %copy-done, f32[2,8,256,128]{3,2,1,0:T(8,128)} %get-tuple-element.9.num_top, f32[2,8,128,128]{3,2,1,0:T(8,128)S(1)} %collective-permute-done.16.received, f32[8,256,128]{2,1,0:T(8,128)S(1)} %density.1), custom_call_target="tpu_custom_call" | custom-call | flops 2097152 | bytes 8388608 | tf_op jit(solution)/shard_map/finish/pallas_call | solution.py:309
  122.3 4.8 %collective-permute-done.24 = f32[5,64,128]{2,1,0:T(8,128)S(1)} collective-permute-done((f32[5,64,128]{2,1,0:T(8,128)S(1)}, f32[5,64,128]{2,1,0:T(8,128)S(1)}, u32[]{:S(2)}, u32[]{:S(2)}) %collective-permute-start.24) | collective-permute-done | bytes 163872 | tf_op jit(solution)/shard_map/ppermute | solution.py:25
  127.1 2.2 %collective-permute-done.29 = f32[5,64,128]{2,1,0:T(8,128)S(1)} collective-permute-done((f32[5,64,128]{2,1,0:T(8,128)S(1)}, f32[5,64,128]{2,1,0:T(8,128)S(1)}, u32[]{:S(2)}, u32[]{:S(2)}) %collective-permute-start.29) | collective-permute-done | bytes 163872 | tf_op jit(solution)/shard_map/ppermute | solution.py:25
  (78 shorter events, 7.6 us)
Async XLA Ops:
  0.6 47.1 %copy-start.7 = (s32[16]{0:T(128)S(1)}, s32[16]{0:T(128)}, u32[]{:S(2)}) copy-start(s32[16]{0:T(128)} %constant.22.clone) | copy-start | bytes 196
  0.7 47.0 %copy-start.12 = (s32[8]{0:T(128)S(1)}, s32[8]{0:T(128)}, u32[]{:S(2)}) copy-start(s32[8]{0:T(128)} %param.18) | copy-start | bytes 100
  0.7 16.3 %collective-permute-start.1 = (f32[1,4,128,128]{3,2,1,0:T(8,128)}, f32[1,4,128,128]{3,2,1,0:T(8,128)S(1)}, u32[]{:S(2)}, u32[]{:S(2)}) collective-permute-start(f32[1,4,128,128]{3,2,1,0:T(8,128)} %bitcast.37), channel_id=1, source_target_pairs={{0,8},{1,9},{2,10},{3,11},{4,12},{5,13},{6,14},{7,15},{8,0},{9,1},... | collective-permute-start | bytes 786440 | tf_op jit(solution)/shard_map/ppermute | solution.py:25
  4.8 13.0 %collective-permute-start.6 = (f32[1,4,128,128]{3,2,1,0:T(8,128)}, f32[1,4,128,128]{3,2,1,0:T(8,128)S(1)}, u32[]{:S(2)}, u32[]{:S(2)}) collective-permute-start(f32[1,4,128,128]{3,2,1,0:T(8,128)} %bitcast.38), channel_id=1, source_target_pairs={{0,4},{1,5},{2,6},{3,7},{4,0},{5,1},{6,2},{7,3},{8,12},{9,13},{10,... | collective-permute-start | bytes 786440 | tf_op jit(solution)/shard_map/ppermute | solution.py:25
  6.4 12.9 %collective-permute-start.5 = (f32[1,4,128,128]{3,2,1,0:T(8,128)}, f32[1,4,128,128]{3,2,1,0:T(8,128)S(1)}, u32[]{:S(2)}, u32[]{:S(2)}) collective-permute-start(f32[1,4,128,128]{3,2,1,0:T(8,128)} %bitcast.39), channel_id=1, source_target_pairs={{0,2},{1,3},{2,0},{3,1},{4,6},{5,7},{6,4},{7,5},{8,10},{9,11},{10,... | collective-permute-start | bytes 786440 | tf_op jit(solution)/shard_map/ppermute | solution.py:25
  10.2 39.2 %collective-permute-start = (f32[2,128,1024]{2,1,0:T(8,128)}, f32[2,128,1024]{2,1,0:T(8,128)}, u32[]{:S(2)}, u32[]{:S(2)}) collective-permute-start(f32[2,128,1024]{2,1,0:T(8,128)} %slice.137), channel_id=1, source_target_pairs={{1,0},{2,1},{3,2},{4,3},{5,4},{6,5},{7,6},{8,7},{9,8},{10,9},{11,1... | collective-permute-start | bytes 3145736 | tf_op jit(solution)/shard_map/ppermute | solution.py:21
  11.5 8.3 %collective-permute-start.12 = (f32[1,4,128,128]{3,2,1,0:T(8,128)S(1)}, f32[1,4,128,128]{3,2,1,0:T(8,128)S(1)}, u32[]{:S(2)}, u32[]{:S(2)}) collective-permute-start(f32[1,4,128,128]{3,2,1,0:T(8,128)S(1)} %bitcast.40), channel_id=1, source_target_pairs={{0,1},{1,0},{2,3},{3,2},{4,5},{5,4},{6,7},{7,6},{8,9},{9,8},{10,11... | collective-permute-start | bytes 786440 | tf_op jit(solution)/shard_map/ppermute | solution.py:25
  17.0 17.1 %collective-permute-start.3 = (f32[1,4,128,128]{3,2,1,0:T(8,128)S(1)}, f32[1,4,128,128]{3,2,1,0:T(8,128)S(1)}, u32[]{:S(2)}, u32[]{:S(2)}) collective-permute-start(f32[1,4,128,128]{3,2,1,0:T(8,128)S(1)} %collective-permute-done.1.rest_4_), channel_id=1, source_target_pairs={{0,4},{1,5},{2,6},{3,7},{4,0},{5,1},{6,2},{7,3},{8,12},{9,13},{10,... | collective-permute-start | bytes 786440 | tf_op jit(solution)/shard_map/ppermute | solution.py:25
  17.8 16.6 %collective-permute-start.2 = (f32[1,4,128,128]{3,2,1,0:T(8,128)S(1)}, f32[1,4,128,128]{3,2,1,0:T(8,128)S(1)}, u32[]{:S(2)}, u32[]{:S(2)}) collective-permute-start(f32[1,4,128,128]{3,2,1,0:T(8,128)S(1)} %collective-permute-done.1.rest_4_), channel_id=1, source_target_pairs={{0,2},{1,3},{2,0},{3,1},{4,6},{5,7},{6,4},{7,5},{8,10},{9,11},{10,... | collective-permute-start | bytes 786440 | tf_op jit(solution)/shard_map/ppermute | solution.py:25
  19.3 20.0 %collective-permute-start.7 = (f32[1,4,128,128]{3,2,1,0:T(8,128)S(1)}, f32[1,4,128,128]{3,2,1,0:T(8,128)S(1)}, u32[]{:S(2)}, u32[]{:S(2)}) collective-permute-start(f32[1,4,128,128]{3,2,1,0:T(8,128)S(1)} %collective-permute-done.6.rest_11_), channel_id=1, source_target_pairs={{0,2},{1,3},{2,0},{3,1},{4,6},{5,7},{6,4},{7,5},{8,10},{9,11},{10,... | collective-permute-start | bytes 786440 | tf_op jit(solution)/shard_map/ppermute | solution.py:25
  19.8 22.9 %collective-permute-start.8 = (f32[1,4,128,128]{3,2,1,0:T(8,128)S(1)}, f32[1,4,128,128]{3,2,1,0:T(8,128)S(1)}, u32[]{:S(2)}, u32[]{:S(2)}) collective-permute-start(f32[1,4,128,128]{3,2,1,0:T(8,128)S(1)} %collective-permute-done.1.rest_4_), channel_id=1, source_target_pairs={{0,1},{1,0},{2,3},{3,2},{4,5},{5,4},{6,7},{7,6},{8,9},{9,8},{10,11... | collective-permute-start | bytes 786440 | tf_op jit(solution)/shard_map/ppermute | solution.py:25
  34.1 8.6 %collective-permute-start.15 = (f32[1,4,128,128]{3,2,1,0:T(8,128)S(1)}, f32[1,4,128,128]{3,2,1,0:T(8,128)S(1)}, u32[]{:S(2)}, u32[]{:S(2)}) collective-permute-start(f32[1,4,128,128]{3,2,1,0:T(8,128)S(1)} %collective-permute-done.6.rest_11_), channel_id=1, source_target_pairs={{0,1},{1,0},{2,3},{3,2},{4,5},{5,4},{6,7},{7,6},{8,9},{9,8},{10,11... | collective-permute-start | bytes 786440 | tf_op jit(solution)/shard_map/ppermute | solution.py:25
  34.3 8.9 %collective-permute-start.13 = (f32[1,4,128,128]{3,2,1,0:T(8,128)S(1)}, f32[1,4,128,128]{3,2,1,0:T(8,128)S(1)}, u32[]{:S(2)}, u32[]{:S(2)}) collective-permute-start(f32[1,4,128,128]{3,2,1,0:T(8,128)S(1)} %collective-permute-done.5.rest_9_), channel_id=1, source_target_pairs={{0,1},{1,0},{2,3},{3,2},{4,5},{5,4},{6,7},{7,6},{8,9},{9,8},{10,11... | collective-permute-start | bytes 786440 | tf_op jit(solution)/shard_map/ppermute | solution.py:25
  39.3 8.4 %collective-permute-start.4 = (f32[1,4,128,128]{3,2,1,0:T(8,128)S(1)}, f32[1,4,128,128]{3,2,1,0:T(8,128)S(1)}, u32[]{:S(2)}, u32[]{:S(2)}) collective-permute-start(f32[1,4,128,128]{3,2,1,0:T(8,128)S(1)} %collective-permute-done.3.rest_7_), channel_id=1, source_target_pairs={{0,2},{1,3},{2,0},{3,1},{4,6},{5,7},{6,4},{7,5},{8,10},{9,11},{10,... | collective-permute-start | bytes 786440 | tf_op jit(solution)/shard_map/ppermute | solution.py:25
  42.7 5.7 %collective-permute-start.11 = (f32[1,4,128,128]{3,2,1,0:T(8,128)S(1)}, f32[1,4,128,128]{3,2,1,0:T(8,128)S(1)}, u32[]{:S(2)}, u32[]{:S(2)}) collective-permute-start(f32[1,4,128,128]{3,2,1,0:T(8,128)S(1)} %collective-permute-done.3.rest_7_), channel_id=1, source_target_pairs={{0,1},{1,0},{2,3},{3,2},{4,5},{5,4},{6,7},{7,6},{8,9},{9,8},{10,11... | collective-permute-start | bytes 786440 | tf_op jit(solution)/shard_map/ppermute | solution.py:25
  42.7 5.6 %collective-permute-start.9 = (f32[1,4,128,128]{3,2,1,0:T(8,128)S(1)}, f32[1,4,128,128]{3,2,1,0:T(8,128)}, u32[]{:S(2)}, u32[]{:S(2)}) collective-permute-start(f32[1,4,128,128]{3,2,1,0:T(8,128)S(1)} %collective-permute-done.2.rest_5_), channel_id=1, source_target_pairs={{0,1},{1,0},{2,3},{3,2},{4,5},{5,4},{6,7},{7,6},{8,9},{9,8},{10,11... | collective-permute-start | bytes 786440 | tf_op jit(solution)/shard_map/ppermute | solution.py:25
  43.2 5.2 %collective-permute-start.14 = (f32[1,4,128,128]{3,2,1,0:T(8,128)S(1)}, f32[1,4,128,128]{3,2,1,0:T(8,128)}, u32[]{:S(2)}, u32[]{:S(2)}) collective-permute-start(f32[1,4,128,128]{3,2,1,0:T(8,128)S(1)} %collective-permute-done.7.rest_10_), channel_id=1, source_target_pairs={{0,1},{1,0},{2,3},{3,2},{4,5},{5,4},{6,7},{7,6},{8,9},{9,8},{10,11... | collective-permute-start | bytes 786440 | tf_op jit(solution)/shard_map/ppermute | solution.py:25
  47.7 1.7 %collective-permute-start.10 = (f32[1,4,128,128]{3,2,1,0:T(8,128)S(1)}, f32[1,4,128,128]{3,2,1,0:T(8,128)}, u32[]{:S(2)}, u32[]{:S(2)}) collective-permute-start(f32[1,4,128,128]{3,2,1,0:T(8,128)S(1)} %collective-permute-done.4.rest_6_), channel_id=1, source_target_pairs={{0,1},{1,0},{2,3},{3,2},{4,5},{5,4},{6,7},{7,6},{8,9},{9,8},{10,11... | collective-permute-start | bytes 786440 | tf_op jit(solution)/shard_map/ppermute | solution.py:25
  76.7 3.3 %collective-permute-start.21 = (f32[4,5,128,128]{3,2,1,0:T(8,128)}, f32[4,5,128,128]{3,2,1,0:T(8,128)S(1)}, u32[]{:S(2)}, u32[]{:S(2)}) collective-permute-start(f32[4,5,128,128]{3,2,1,0:T(8,128)} %get-tuple-element.15), channel_id=1, source_target_pairs={{0,1},{1,0},{2,3},{3,2},{4,5},{5,4},{6,7},{7,6},{8,9},{9,8},{10,11... | collective-permute-start | bytes 3932168 | tf_op jit(solution)/shard_map/ppermute | solution.py:25
  76.8 6.8 %collective-permute-start.18 = (f32[4,5,128,128]{3,2,1,0:T(8,128)}, f32[4,5,128,128]{3,2,1,0:T(8,128)S(1)}, u32[]{:S(2)}, u32[]{:S(2)}) collective-permute-start(f32[4,5,128,128]{3,2,1,0:T(8,128)} %get-tuple-element.13), channel_id=1, source_target_pairs={{0,1},{1,0},{2,3},{3,2},{4,5},{5,4},{6,7},{7,6},{8,9},{9,8},{10,11... | collective-permute-start | bytes 3932168 | tf_op jit(solution)/shard_map/ppermute | solution.py:25
  77.3 41.4 %collective-permute-start.16 = (f32[2,8,128,128]{3,2,1,0:T(8,128)}, f32[2,8,128,128]{3,2,1,0:T(8,128)S(1)}, u32[]{:S(2)}, u32[]{:S(2)}) collective-permute-start(f32[2,8,128,128]{3,2,1,0:T(8,128)} %get-tuple-element.10), channel_id=1, source_target_pairs={{0,1},{1,2},{2,3},{3,4},{4,5},{5,6},{6,7},{7,8},{8,9},{9,10},{10,1... | collective-permute-start | bytes 3145736 | tf_op jit(solution)/shard_map/ppermute | solution.py:21
  81.4 10.6 %collective-permute-start.22 = (f32[2,5,64,128]{3,2,1,0:T(8,128)S(1)}, f32[2,5,64,128]{3,2,1,0:T(8,128)S(1)}, u32[]{:S(2)}, u32[]{:S(2)}) collective-permute-start(f32[2,5,64,128]{3,2,1,0:T(8,128)S(1)} %pad_maximum_fusion.1), channel_id=1, source_target_pairs={{0,2},{1,3},{2,0},{3,1},{4,6},{5,7},{6,4},{7,5},{8,10},{9,11},{10,... | collective-permute-start | bytes 983048 | tf_op jit(solution)/shard_map/ppermute | solution.py:25
  81.5 22.1 %collective-permute-start.27 = (f32[2,5,64,128]{3,2,1,0:T(8,128)S(1)}, f32[2,5,64,128]{3,2,1,0:T(8,128)S(1)}, u32[]{:S(2)}, u32[]{:S(2)}) collective-permute-start(f32[2,5,64,128]{3,2,1,0:T(8,128)S(1)} %pad_maximum_fusion.3), channel_id=1, source_target_pairs={{0,4},{1,5},{2,6},{3,7},{4,0},{5,1},{6,2},{7,3},{8,12},{9,13},{10,... | collective-permute-start | bytes 983048 | tf_op jit(solution)/shard_map/ppermute | solution.py:25
  83.7 22.2 %collective-permute-start.19 = (f32[2,5,64,128]{3,2,1,0:T(8,128)S(1)}, f32[2,5,64,128]{3,2,1,0:T(8,128)S(1)}, u32[]{:S(2)}, u32[]{:S(2)}) collective-permute-start(f32[2,5,64,128]{3,2,1,0:T(8,128)S(1)} %pad_maximum_fusion), channel_id=1, source_target_pairs={{0,2},{1,3},{2,0},{3,1},{4,6},{5,7},{6,4},{7,5},{8,10},{9,11},{10,... | collective-permute-start | bytes 983048 | tf_op jit(solution)/shard_map/ppermute | solution.py:25
  83.9 24.2 %collective-permute-start.25 = (f32[2,5,64,128]{3,2,1,0:T(8,128)S(1)}, f32[2,5,64,128]{3,2,1,0:T(8,128)S(1)}, u32[]{:S(2)}, u32[]{:S(2)}) collective-permute-start(f32[2,5,64,128]{3,2,1,0:T(8,128)S(1)} %pad_maximum_fusion.2), channel_id=1, source_target_pairs={{0,4},{1,5},{2,6},{3,7},{4,0},{5,1},{6,2},{7,3},{8,12},{9,13},{10,... | collective-permute-start | bytes 983048 | tf_op jit(solution)/shard_map/ppermute | solution.py:25
  92.1 23.7 %collective-permute-start.17 = (s32[64]{0:T(128)S(1)}, s32[64]{0:T(128)S(1)}, u32[]{:S(2)}, u32[]{:S(2)}) collective-permute-start(s32[64]{0:T(128)S(1)} %reshape.39.meta), channel_id=1, source_target_pairs={{0,1},{1,2},{2,3},{3,4},{4,5},{5,6},{6,7},{7,8},{8,9},{9,10},{10,1... | collective-permute-start | bytes 776 | tf_op jit(solution)/shard_map/ppermute | solution.py:21
  103.8 6.4 %collective-permute-start.23 = (f32[5,64,128]{2,1,0:T(8,128)S(1)}, f32[5,64,128]{2,1,0:T(8,128)S(1)}, u32[]{:S(2)}, u32[]{:S(2)}) collective-permute-start(f32[5,64,128]{2,1,0:T(8,128)S(1)} %get-tuple-element.27), channel_id=1, source_target_pairs={{0,4},{1,5},{2,6},{3,7},{4,0},{5,1},{6,2},{7,3},{8,12},{9,13},{10,... | collective-permute-start | bytes 491528 | tf_op jit(solution)/shard_map/ppermute | solution.py:25
  105.9 7.2 %collective-permute-start.28 = (f32[5,64,128]{2,1,0:T(8,128)S(1)}, f32[5,64,128]{2,1,0:T(8,128)S(1)}, u32[]{:S(2)}, u32[]{:S(2)}) collective-permute-start(f32[5,64,128]{2,1,0:T(8,128)S(1)} %get-tuple-element.26), channel_id=1, source_target_pairs={{0,2},{1,3},{2,0},{3,1},{4,6},{5,7},{6,4},{7,5},{8,10},{9,11},{10,... | collective-permute-start | bytes 491528 | tf_op jit(solution)/shard_map/ppermute | solution.py:25
  108.1 14.2 %collective-permute-start.20 = (f32[5,64,128]{2,1,0:T(8,128)S(1)}, f32[5,64,128]{2,1,0:T(8,128)S(1)}, u32[]{:S(2)}, u32[]{:S(2)}) collective-permute-start(f32[5,64,128]{2,1,0:T(8,128)S(1)} %get-tuple-element.19), channel_id=1, source_target_pairs={{0,4},{1,5},{2,6},{3,7},{4,0},{5,1},{6,2},{7,3},{8,12},{9,13},{10,... | collective-permute-start | bytes 491528 | tf_op jit(solution)/shard_map/ppermute | solution.py:25
  110.2 12.1 %collective-permute-start.26 = (f32[5,64,128]{2,1,0:T(8,128)S(1)}, f32[5,64,128]{2,1,0:T(8,128)S(1)}, u32[]{:S(2)}, u32[]{:S(2)}) collective-permute-start(f32[5,64,128]{2,1,0:T(8,128)S(1)} %get-tuple-element.18), channel_id=1, source_target_pairs={{0,2},{1,3},{2,0},{3,1},{4,6},{5,7},{6,4},{7,5},{8,10},{9,11},{10,... | collective-permute-start | bytes 491528 | tf_op jit(solution)/shard_map/ppermute | solution.py:25
  113.2 13.9 %collective-permute-start.24 = (f32[5,64,128]{2,1,0:T(8,128)S(1)}, f32[5,64,128]{2,1,0:T(8,128)S(1)}, u32[]{:S(2)}, u32[]{:S(2)}) collective-permute-start(f32[5,64,128]{2,1,0:T(8,128)S(1)} %get-tuple-element.25), channel_id=1, source_target_pairs={{0,8},{1,9},{2,10},{3,11},{4,12},{5,13},{6,14},{7,15},{8,0},{9,1},... | collective-permute-start | bytes 491528 | tf_op jit(solution)/shard_map/ppermute | solution.py:25
  115.8 13.6 %collective-permute-start.29 = (f32[5,64,128]{2,1,0:T(8,128)S(1)}, f32[5,64,128]{2,1,0:T(8,128)S(1)}, u32[]{:S(2)}, u32[]{:S(2)}) collective-permute-start(f32[5,64,128]{2,1,0:T(8,128)S(1)} %get-tuple-element.24), channel_id=1, source_target_pairs={{0,8},{1,9},{2,10},{3,11},{4,12},{5,13},{6,14},{7,15},{8,0},{9,1},... | collective-permute-start | bytes 491528 | tf_op jit(solution)/shard_map/ppermute | solution.py:25
  (11 other events, 140.2 us)

commit v3 on v2

--- a/solution.py
+++ b/solution.py
@@ -12,7 +12,7 @@
 damping = 1.0
 floor_level = 0.3
 LANES = 128
-SLOTS_AT_ONCE = 2
+SLOTS_AT_ONCE = 4
 VMEM_BYTES = 48 * 1024 * 1024
 
 
@@ -28,25 +28,39 @@
 FAR, NEAR = (8, 10, 14, 12), (0, 2, 6, 4)
 
 
-def reduced(far, near):
+def reduced(far, theirs_near, mine_near, low, density):
     half = far[0].shape[2] // 2
+    routes = ((slice(0, half), 2, 4, (1, 2), 3), (slice(half, 2 * half), 4, 2, (3, 2), 1))
+
+    def pick(pair, at, rows):
+        return pair[0][at, :, rows] + pair[1][at, :, rows]
+
+    def first_step(pair):
+        return [swapped(jnp.stack([pick(pair, at, rows) for at in sent]), mask) for rows, mask, _, sent, _ in routes]
+
+    got = first_step(far)
+    near = (mine_near, swapped(theirs_near, 1))
+    got_near = first_step(near)
+    low = after(low, *got)
+    received = moved(low, 1)
+    outer, across = [], []
+    for (rows, _, second, _, kept), arrived in zip(routes, got):
+        outer.append(pick(far, 0, rows) + arrived[0])
+        across.append(pick(far, kept, rows) + arrived[1])
+    density, across[0] = lax.optimization_barrier((density, across[0]))
+    across = [swapped(block, route[2]) for block, route in zip(across, routes)]
+    beside = []
+    for (rows, _, second, _, kept), arrived in zip(routes, got_near):
+        beside.append(swapped(pick(near, kept, rows) + arrived[1], second))
     totals = []
-    for part, (first, second) in enumerate(((2, 4), (4, 2))):
-        rows = slice(part * half, (part + 1) * half)
-        sent, kept = ((1, 2), (0, 3)) if first == 2 else ((3, 2), (0, 1))
-
-        def pick(pair, at):
-            return pair[0][at, :, rows] + pair[1][at, :, rows]
-
-        def once(pair):
-            got = swapped(jnp.stack([pick(pair, at) for at in sent]), first)
-            return pick(pair, kept[0]) + got[0], pick(pair, kept[1]) + got[1]
-
-        outer, across = once(far)
-        inner, beside = once(near)
-        outer = outer + swapped(across, second)
-        totals.append(inner + swapped(beside, second) + swapped(outer, 8))
-    return jnp.concatenate(totals, axis=1)
+    for k, (rows, _, _, _, _) in enumerate(routes):
+        ahead = swapped(outer[k] + across[k], 8)
+        totals.append(pick(near, 0, rows) + got_near[k][0] + beside[k] + ahead)
+    return jnp.concatenate(totals, axis=1), received, density
+
+
+def after(value, *others):
+    return lax.optimization_barrier((value,) + others)[0]
 
 
 def split(value):
@@ -62,51 +76,49 @@
     minus = np.block([[cos, -sin], [sin, cos]])
     plus = np.block([[cos, sin], [-sin, cos]])
 
-    def parts(matrix, axis):
-        matrix = matrix.astype(np.float32)
+    parts = []
+    for matrix in (minus.astype(np.float32), plus.astype(np.float32)):
         high = matrix.astype(jnp.bfloat16)
-        low = (matrix - high.astype(np.float32)).astype(jnp.bfloat16)
-        return jnp.asarray(np.concatenate([high, high, low], axis=axis))
-
-    return parts(minus, 0), parts(plus, 1), parts(minus, 1), parts(plus, 0)
-
-
-def right_product(rows, table):
+        parts += [high, (matrix - high.astype(np.float32)).astype(jnp.bfloat16)]
+    return jnp.asarray(np.stack(parts))
+
+
+def right_product(rows, factor, at):
     high, low = split(rows)
+    table = jnp.concatenate([factor[at], factor[at], factor[at + 1]], axis=0)
     return jnp.dot(jnp.concatenate([high, low, high], axis=1), table, preferred_element_type=jnp.float32)
 
 
-def left_product(table, columns):
+def left_product(factor, at, columns):
     high, low = split(columns)
+    table = jnp.concatenate([factor[at], factor[at], factor[at + 1]], axis=1)
     return jnp.dot(table, jnp.concatenate([high, low, high], axis=0), preferred_element_type=jnp.float32)
 
 
-def update_kernel(dims, meta, slot_of, live, amplitudes, obj, rim, *rest):
+def update_kernel(dims, meta, slot_of, live, amplitudes_in, obj, rim, factors_in, *rest):
     piece_sizes, group_sizes, slots = dims
-    tables = rest[:4]
-    pieces = rest[4 : 4 + len(piece_sizes)]
-    rest = rest[4 + len(piece_sizes) :]
+    pieces = rest[: len(piece_sizes)]
+    rest = rest[len(piece_sizes) :]
     num_top, num_low, squares = rest[:3]
     groups = rest[3 : 3 + len(group_sizes)]
-    table, ext, acc, part, right_f, left_f, left_i, right_i, piece_sems, out_sems = rest[3 + len(group_sizes) :]
+    table, ext, acc, part, amplitudes, factors, in_sems, out_sems = rest[3 + len(group_sizes) :]
     points = LANES
     tile_rows = obj.shape[1]
     blocks = obj.shape[2] // LANES
     modes = table.shape[1] // 2
 
-    copies = []
+    moves = [(factors_in, factors), (amplitudes_in, amplitudes)]
+    for b in range(blocks):
+        columns = pl.ds(b * LANES, LANES)
+        moves.append((obj.at[:, :, columns], ext.at[:, b, pl.ds(0, tile_rows), :]))
+        moves.append((rim.at[:, :, columns], ext.at[:, b, pl.ds(tile_rows, points), :]))
     at = 0
     for k, size in enumerate(piece_sizes):
-        copies.append(pltpu.make_async_copy(pieces[k], table.at[pl.ds(at, size)], piece_sems.at[k]))
+        moves.append((pieces[k], table.at[pl.ds(at, size)]))
         at += size
-    for k, (source, target) in enumerate(zip(tables, (right_f, left_f, left_i, right_i))):
-        copies.append(pltpu.make_async_copy(source, target, piece_sems.at[len(piece_sizes) + k]))
+    copies = [pltpu.make_async_copy(*ends, in_sems.at[k]) for k, ends in enumerate(moves)]
     for copy in copies:
         copy.start()
-    for b in range(blocks):
-        ext[:, b, :tile_rows, :] = obj[:, :, b * LANES : (b + 1) * LANES]
-        ext[:, b, tile_rows:, :] = rim[:, :, b * LANES : (b + 1) * LANES]
-    ext[:, blocks] = jnp.zeros_like(ext[:, blocks])
     acc[...] = jnp.zeros_like(acc)
     part[...] = jnp.zeros_like(part)
     for copy in copies:
@@ -127,12 +139,12 @@
             slot = slot_of[scan]
             block, shift = col // LANES, col % LANES
             back = lax.rem(LANES - shift, LANES)
-            keep = lane < LANES - shift
+            keep = lane >= shift
             win = []
             for ch in range(2):
-                first = pltpu.roll(ext[ch, block, pl.ds(row, points), :], back, 1)
-                second = pltpu.roll(ext[ch, block + 1, pl.ds(row, points), :], back, 1)
-                win.append(jnp.where(keep, first, second))
+                first = ext[ch, block, pl.ds(row, points), :]
+                second = ext[ch, block + 1, pl.ds(row, points), :]
+                win.append(pltpu.roll(jnp.where(keep, first, second), back, 1))
             probe = [(table[slot, 2 * m], table[slot, 2 * m + 1]) for m in range(modes)]
             for pr, pi in probe:
                 waves.append(
@@ -141,12 +153,12 @@
             wins.append(win)
             probes.append(probe)
             places.append((p, row, block, shift, slot))
-        half = right_product(jnp.concatenate(waves, axis=0), right_f[...])
+        half = right_product(jnp.concatenate(waves, axis=0), factors, 0)
         columns = []
         for k in range(SLOTS_AT_ONCE * modes):
             rows = half[k * points : (k + 1) * points]
             columns.append(jnp.concatenate([rows[:, :points], rows[:, points:]], axis=0))
-        spec = left_product(left_f[...], jnp.concatenate(columns, axis=1))
+        spec = left_product(factors, 2, jnp.concatenate(columns, axis=1))
         columns = []
         for u in range(SLOTS_AT_ONCE):
             own = [spec[:, (u * modes + m) * points : (u * modes + m + 1) * points] for m in range(modes)]
@@ -156,12 +168,12 @@
             factor = factor * flags[u]
             factor = jnp.concatenate([factor, factor], axis=0)
             columns += [s * factor for s in own]
-        half = left_product(left_i[...], jnp.concatenate(columns, axis=1))
+        half = left_product(factors, 0, jnp.concatenate(columns, axis=1))
         rows = []
         for k in range(SLOTS_AT_ONCE * modes):
             column = half[:, k * points : (k + 1) * points]
             rows.append(jnp.concatenate([column[:points], column[points:]], axis=1))
-        change = right_product(jnp.concatenate(rows, axis=0), right_i[...])
+        change = right_product(jnp.concatenate(rows, axis=0), factors, 2)
         for u in range(SLOTS_AT_ONCE):
             p, row, block, shift, slot = places[u]
             wr, wi = wins[u]
@@ -204,7 +216,7 @@
         copy.wait()
 
 
-def update(meta, slot_of, live, amplitudes, obj, rim, tables, pieces, group_sizes):
+def update(meta, slot_of, live, amplitudes, obj, rim, factors, pieces, group_sizes):
     points = amplitudes.shape[-1]
     tile_rows = obj.shape[1]
     blocks = obj.shape[2] // LANES
@@ -224,23 +236,22 @@
             jax.ShapeDtypeStruct((scans, points, points), f32),
         ]
         + [jax.ShapeDtypeStruct((size, channels + 1, points, points), f32) for size in group_sizes],
-        in_specs=[smem] * 3 + [vmem] * 3 + [anywhere] * (4 + len(pieces)),
+        in_specs=[smem] * 3 + [anywhere] * 3 + [pl.BlockSpec(memory_space=pltpu.HBM)] + [anywhere] * len(pieces),
         out_specs=[anywhere, anywhere, vmem] + [anywhere] * len(group_sizes),
         scratch_shapes=[
             pltpu.VMEM((slots, channels, points, points), f32),
             pltpu.VMEM((2, blocks + 1, tile_rows + points, LANES), f32),
             pltpu.VMEM((2, blocks + 1, tile_rows + points, LANES), f32),
             pltpu.VMEM((slots, channels + 1, points, points), f32),
-        ]
-        + [pltpu.VMEM(factor.shape, factor.dtype) for factor in tables]
-        + [
-            pltpu.SemaphoreType.DMA((len(pieces) + 4,)),
+            pltpu.VMEM(amplitudes.shape, f32),
+            pltpu.VMEM(factors.shape, factors.dtype),
+            pltpu.SemaphoreType.DMA((len(pieces) + 2 * blocks + 2,)),
             pltpu.SemaphoreType.DMA((len(group_sizes) + 2,)),
         ],
         compiler_params=pltpu.CompilerParams(vmem_limit_bytes=VMEM_BYTES),
         cost_estimate=pl.CostEstimate(flops=6 * 10**9, bytes_accessed=16 * 2**20, transcendentals=2**18),
         name="update",
-    )(meta, slot_of, live, amplitudes, obj, rim, *tables, *pieces)
+    )(meta, slot_of, live, amplitudes, obj, rim, factors, *pieces)
 
 
 def density_kernel(tile_rows, meta, above, squares, density, ext):
@@ -342,13 +353,14 @@
         held[12] = swapped(held[8], 4)
         held[10] = swapped(held[8], 2)
         held[14] = swapped(held[12], 2)
+        held[10] = after(held[10], above)
         for key in list(held):
             held[key | 1] = swapped(held[key], 1)
         order = [key | core for core in (0, 1) for key in FAR + NEAR]
         pieces = [held[key] for key in order]
-        place = np.zeros(size, np.int32)
-        place[np.array(order)] = np.arange(size)
-        slot_of = jnp.asarray(place)[jnp.bitwise_xor(owner, device)]
+        key = jnp.bitwise_xor(owner, device)
+        side = key // 2 % 4
+        slot_of = key % 2 * 8 + (1 - key // 8) * 4 + jnp.bitwise_xor(side, side // 2)
         group_sizes = (4,) * 4
     else:
         owned = (owner == device)[:, None, None, None]
@@ -361,14 +373,14 @@
         meta, slot_of, counts, amplitudes, object_strip, rim, transform_tables(points), pieces, group_sizes
     )
 
-    received = moved(num_low, 1)
+    density = density_of(meta, above, squares, tile_rows, blocks)
     if swaps:
         mine_far, mine_near, theirs_far, theirs_near = groups
-        total = reduced((mine_far, swapped(theirs_far, 1)), (mine_near, swapped(theirs_near, 1)))
+        total, received, density = reduced((mine_far, swapped(theirs_far, 1)), theirs_near, mine_near, num_low, density)
     else:
+        received = moved(num_low, 1)
         summed = lax.psum(groups[0], "row")
         total = jnp.sum(jnp.where(owned, summed, 0.0), axis=0)
-    density = density_of(meta, above, squares, tile_rows, blocks)
     new_object = finish(object_strip, num_top, received, density)
     new_probes = own_probe[0] + total[:channels] / (total[channels] + damping)
     return (new_object, new_probes.reshape(probe_store.shape))

time: 131 us -> 121 us (0.924)
  Pallas kernels: 29.5 us -> 20.5 us
  local copies, waits for them, and re-layouts: 7.14 us -> 1.5 us
  waiting for transfers between devices: 44.7 us -> 47.4 us
  starting transfers between devices: 44.6 us -> 46.4 us
    ppermute x27, starting transfers between devices: 29.7 us -> 40.7 us  [swapped(): lax.ppermute(block, 'row', [(i, i ^ mask) for i in range(lax.axis_size('r...]
    ppermute x3, starting transfers between devices: 14.9 us -> 5.67 us  [moved(): lax.ppermute(block, 'row', [(i, i + distance) for i in range(size) if 0 <...]
    pallas_call x1, Pallas kernels: 23.4 us -> 15 us  [update(): pl.pallas_call(functools.partial(update_kernel, (piece_sizes, group_sizes...]
    unnamed x26 -> x18, local copies, waits for them, and re-layouts: 4.02 us -> 0.04 us
    ppermute x27, waiting for transfers between devices: 44.7 us -> 46.6 us  [swapped(): lax.ppermute(block, 'row', [(i, i ^ mask) for i in range(lax.axis_size('r...]
  transfers between devices with their start and end apart: 30 -> 30, of which waited for: 11 -> 14; matrix products, arithmetic and copies ran while one was open for 4% -> 3% of each run, Pallas kernels for 5% -> 2%
where the time goes in v3:
time: 121 us; the launch traced here: 120 us
  waiting for transfers between devices  47.4 us (39%)
  starting transfers between devices  46.4 us (38%)
  Pallas kernels  20.5 us (17%)
  other arithmetic  2.65 us (2%)
  between operations  1.55 us (1%)
  local copies, waits for them, and re-layouts  1.5 us (1%)
    ppermute x27, waiting for transfers between devices, swapped(): lax.ppermute(block, 'row', [(i, i ^ mask) for i in range(lax.axis_size('r...  46.6 us
    ppermute x27, starting transfers between devices, swapped(): lax.ppermute(block, 'row', [(i, i ^ mask) for i in range(lax.axis_size('r...  40.7 us
    pallas_call x1, Pallas kernels, update(): pl.pallas_call(functools.partial(update_kernel, (piece_sizes, group_sizes...  15 us
    ppermute x3, starting transfers between devices, moved(): lax.ppermute(block, 'row', [(i, i + distance) for i in range(size) if 0 <...  5.67 us
    pallas_call x1, Pallas kernels, finish(): pl.pallas_call(finish_kernel, out_shape=jax.ShapeDtypeStruct(obj.shape, o...  3.47 us
  transfers between devices with their start and end apart: 30, of which 14 were waited for; matrix products, arithmetic and copies ran while one was open for 3% of the time, Pallas kernels for 2%

profile of v3, /device:TPU:0, one launch (start us, length us, event | category | flops | bytes accessed | tf_op | source)
XLA Modules:
  0.0 120.0 jit_solution(9283079350292145560)
XLA Ops:
  1.2 2.6 %collective-permute-start.7 = (f32[1,4,128,128]{3,2,1,0:T(8,128)}, f32[1,4,128,128]{3,2,1,0:T(8,128)S(1)}, u32[]{:S(2)}, u32[]{:S(2)}) collective-permute-start(f32[1,4,128,128]{3,2,1,0:T(8,128)} %bitcast.38), channel_id=1, source_target_pairs={{0,4},{1,5},{2,6},{3,7},{4,0},{5,1},{6,2},{7,3},{8,12},{9,13},{10,... | collective-permute-start | bytes 786440 | tf_op jit(solution)/shard_map/ppermute | solution.py:25
  3.9 2.6 %collective-permute-start.1 = (f32[1,4,128,128]{3,2,1,0:T(8,128)}, f32[1,4,128,128]{3,2,1,0:T(8,128)S(1)}, u32[]{:S(2)}, u32[]{:S(2)}) collective-permute-start(f32[1,4,128,128]{3,2,1,0:T(8,128)} %bitcast.39), channel_id=1, source_target_pairs={{0,8},{1,9},{2,10},{3,11},{4,12},{5,13},{6,14},{7,15},{8,0},{9,1},... | collective-permute-start | bytes 786440 | tf_op jit(solution)/shard_map/ppermute | solution.py:25
  6.4 1.3 %slice.137 = f32[2,128,1024]{2,1,0:T(8,128)S(1)} slice(f32[2,256,1024]{2,1,0:T(8,128)} %obj.3), slice={[0:2], [0:128], [0:1024]} | slice | bytes 2097152 | tf_op jit(solution)/shard_map/slice | solution.py:370
  7.7 1.3 %collective-permute-start = (f32[2,128,1024]{2,1,0:T(8,128)S(1)}, f32[2,128,1024]{2,1,0:T(8,128)}, u32[]{:S(2)}, u32[]{:S(2)}) collective-permute-start(f32[2,128,1024]{2,1,0:T(8,128)S(1)} %slice.137), channel_id=1, source_target_pairs={{1,0},{2,1},{3,2},{4,3},{5,4},{6,5},{7,6},{8,7},{9,8},{10,9},{11,1... | collective-permute-start | bytes 3145736 | tf_op jit(solution)/shard_map/ppermute | solution.py:21
  9.9 3.0 %collective-permute-start.3 = (s32[64]{0:T(128)S(1)}, s32[64]{0:T(128)S(1)}, u32[]{:S(2)}, u32[]{:S(2)}) collective-permute-start(s32[64]{0:T(128)S(1)} %reshape.39.meta), channel_id=1, source_target_pairs={{0,1},{1,2},{2,3},{3,4},{4,5},{5,6},{6,7},{7,8},{8,9},{9,10},{10,1... | collective-permute-start | bytes 776 | tf_op jit(solution)/shard_map/ppermute | solution.py:21
  13.8 3.2 %collective-permute-start.6 = (f32[1,4,128,128]{3,2,1,0:T(8,128)S(1)}, f32[1,4,128,128]{3,2,1,0:T(8,128)S(1)}, u32[]{:S(2)}, u32[]{:S(2)}) collective-permute-start(f32[1,4,128,128]{3,2,1,0:T(8,128)S(1)} %bitcast.40), channel_id=1, source_target_pairs={{0,2},{1,3},{2,0},{3,1},{4,6},{5,7},{6,4},{7,5},{8,10},{9,11},{10,... | collective-permute-start | bytes 786440 | tf_op jit(solution)/shard_map/ppermute | solution.py:25
  16.9 2.2 %collective-permute-done.1.rest_0_ = f32[1,4,128,128]{3,2,1,0:T(8,128)S(1)} collective-permute-done((f32[1,4,128,128]{3,2,1,0:T(8,128)}, f32[1,4,128,128]{3,2,1,0:T(8,128)S(1)}, u32[]{:S(2)}, u32[]{:S(2)}) %collective-permute-start.1) | collective-permute-done | bytes 262176 | tf_op jit(solution)/shard_map/ppermute | solution.py:25
  19.5 1.5 %collective-permute-start.2 = (f32[1,4,128,128]{3,2,1,0:T(8,128)S(1)}, f32[1,4,128,128]{3,2,1,0:T(8,128)S(1)}, u32[]{:S(2)}, u32[]{:S(2)}) collective-permute-start(f32[1,4,128,128]{3,2,1,0:T(8,128)S(1)} %collective-permute-done.1.rest_0_), channel_id=1, source_target_pairs={{0,2},{1,3},{2,0},{3,1},{4,6},{5,7},{6,4},{7,5},{8,10},{9,11},{10,... | collective-permute-start | bytes 786440 | tf_op jit(solution)/shard_map/ppermute | solution.py:25
  21.0 11.4 %collective-permute-done.6.rest_5_ = f32[1,4,128,128]{3,2,1,0:T(8,128)S(1)} collective-permute-done((f32[1,4,128,128]{3,2,1,0:T(8,128)S(1)}, f32[1,4,128,128]{3,2,1,0:T(8,128)S(1)}, u32[]{:S(2)}, u32[]{:S(2)}) %collective-permute-start.6) | collective-permute-done | bytes 262176 | tf_op jit(solution)/shard_map/ppermute | solution.py:25
  32.4 2.5 %collective-permute-start.8 = (f32[1,4,128,128]{3,2,1,0:T(8,128)S(1)}, f32[1,4,128,128]{3,2,1,0:T(8,128)S(1)}, u32[]{:S(2)}, u32[]{:S(2)}) collective-permute-start(f32[1,4,128,128]{3,2,1,0:T(8,128)S(1)} %collective-permute-done.7.rest_7_), channel_id=1, source_target_pairs={{0,2},{1,3},{2,0},{3,1},{4,6},{5,7},{6,4},{7,5},{8,10},{9,11},{10,... | collective-permute-start | bytes 786440 | tf_op jit(solution)/shard_map/ppermute | solution.py:25
  35.3 2.6 %collective-permute-done.2.rest_1_ = f32[1,4,128,128]{3,2,1,0:T(8,128)S(1)} collective-permute-done((f32[1,4,128,128]{3,2,1,0:T(8,128)S(1)}, f32[1,4,128,128]{3,2,1,0:T(8,128)S(1)}, u32[]{:S(2)}, u32[]{:S(2)}) %collective-permute-start.2) | collective-permute-done | bytes 262176 | tf_op jit(solution)/shard_map/ppermute | solution.py:25
  38.0 2.5 %collective-permute-start.5 = (f32[1,4,128,128]{3,2,1,0:T(8,128)S(1)}, f32[1,4,128,128]{3,2,1,0:T(8,128)S(1)}, u32[]{:S(2)}, u32[]{:S(2)}) collective-permute-start(f32[1,4,128,128]{3,2,1,0:T(8,128)S(1)} %collective-permute-done.4.rest_3_), channel_id=1, source_target_pairs={{0,2},{1,3},{2,0},{3,1},{4,6},{5,7},{6,4},{7,5},{8,10},{9,11},{10,... | collective-permute-start | bytes 786440 | tf_op jit(solution)/shard_map/ppermute | solution.py:25
  40.4 3.1 %collective-permute-done.8.rest_6_ = f32[1,4,128,128]{3,2,1,0:T(8,128)S(1)} collective-permute-done((f32[1,4,128,128]{3,2,1,0:T(8,128)S(1)}, f32[1,4,128,128]{3,2,1,0:T(8,128)S(1)}, u32[]{:S(2)}, u32[]{:S(2)}) %collective-permute-start.8) | collective-permute-done | bytes 262176 | tf_op jit(solution)/shard_map/ppermute | solution.py:25
  44.2 5.0 %collective-permute-done.5.rest_2_ = f32[1,4,128,128]{3,2,1,0:T(8,128)S(1)} collective-permute-done((f32[1,4,128,128]{3,2,1,0:T(8,128)S(1)}, f32[1,4,128,128]{3,2,1,0:T(8,128)S(1)}, u32[]{:S(2)}, u32[]{:S(2)}) %collective-permute-start.5) | collective-permute-done | bytes 262176 | tf_op jit(solution)/shard_map/ppermute | solution.py:25
  49.2 1.4 %collective-permute-done.11.rest_10_ = f32[1,4,128,128]{3,2,1,0:T(8,128)S(1)} collective-permute-done((f32[1,4,128,128]{3,2,1,0:T(8,128)S(1)}, f32[1,4,128,128]{3,2,1,0:T(8,128)S(1)}, u32[]{:S(2)}, u32[]{:S(2)}) %collective-permute-start.11) | collective-permute-done | bytes 262176 | tf_op jit(solution)/shard_map/ppermute | solution.py:25
  50.7 15.0 %update.1 = (f32[2,8,256,128]{3,2,1,0:T(8,128)}, f32[2,8,128,128]{3,2,1,0:T(8,128)}, f32[8,128,128]{2,1,0:T(8,128)S(1)}, f32[4,5,128,128]{3,2,1,0:T(8,128)}, f32...) custom-call(s32[64]{0:T(128)S(1)} %reshape.39.meta, s32[8]{0:T(128)S(1)} %fusion.22.slot_of, ...), custom_call_target="tpu_custom_call" | custom-call | flops 6000000000 | bytes 16777216 | tf_op jit(solution)/shard_map/update/pallas_call | solution.py:231
  65.7 3.0 %collective-permute-start.17 = (f32[4,5,128,128]{3,2,1,0:T(8,128)}, f32[4,5,128,128]{3,2,1,0:T(8,128)S(1)}, u32[]{:S(2)}, u32[]{:S(2)}) collective-permute-start(f32[4,5,128,128]{3,2,1,0:T(8,128)} %get-tuple-element.17), channel_id=1, source_target_pairs={{0,1},{1,0},{2,3},{3,2},{4,5},{5,4},{6,7},{7,6},{8,9},{9,8},{10,11... | collective-permute-start | bytes 3932168 | tf_op jit(solution)/shard_map/ppermute | solution.py:25
  68.7 2.8 %collective-permute-done.17 = f32[4,5,128,128]{3,2,1,0:T(8,128)S(1)} collective-permute-done((f32[4,5,128,128]{3,2,1,0:T(8,128)}, f32[4,5,128,128]{3,2,1,0:T(8,128)S(1)}, u32[]{:S(2)}, u32[]{:S(2)}) %collective-permute-start.17) | collective-permute-done | bytes 1310752 | tf_op jit(solution)/shard_map/ppermute | solution.py:25
  71.5 1.3 %slice_add_fusion.21 = (f32[1,5,64,128]{3,2,1,0:T(8,128)S(1)}, f32[1,5,64,128]{3,2,1,0:T(8,128)S(1)}, f32[1,5,64,128]{3,2,1,0:T(8,128)S(1)}, f32[1,5,64,128]{3,2,1,0:T(8,128)S(1)}) fusion(f32[4,5,128,128]{3,2,1,0:T(8,128)S(1)} %collective-permute-done.17, f32[4,5,128,128]{3,2,1,0:T(8,128)} %get-tuple-element.16), kind=kLoop, calls=%fused_computation.44 | loop fusion | flops 163840 | bytes 1966080 | tf_op jit(solution)/shard_map/add | solution.py:36
  73.0 5.9 %collective-permute-start.19 = (f32[2,5,64,128]{3,2,1,0:T(8,128)S(1)}, f32[2,5,64,128]{3,2,1,0:T(8,128)S(1)}, u32[]{:S(2)}, u32[]{:S(2)}) collective-permute-start(f32[2,5,64,128]{3,2,1,0:T(8,128)S(1)} %pad_maximum_fusion.1), channel_id=1, source_target_pairs={{0,4},{1,5},{2,6},{3,7},{4,0},{5,1},{6,2},{7,3},{8,12},{9,13},{10,... | collective-permute-start | bytes 983048 | tf_op jit(solution)/shard_map/ppermute | solution.py:25
  79.6 2.1 %density.1 = f32[8,256,128]{2,1,0:T(8,128)S(1)} custom-call(s32[64]{0:T(128)S(1)} %reshape.39.meta, s32[64]{0:T(128)S(1)} %collective-permute-done.3.above, f32[8,128,128]{2,1,0:T(8,128)S(1)} %get-tuple-element.19.squares), custom_call_target="tpu_custom_call" | custom-call | flops 8388608 | bytes 8388608 | tf_op jit(solution)/shard_map/density/pallas_call | solution.py:295
  81.6 1.9 %collective-permute-done.18 = f32[2,5,64,128]{3,2,1,0:T(8,128)S(1)} collective-permute-done((f32[2,5,64,128]{3,2,1,0:T(8,128)S(1)}, f32[2,5,64,128]{3,2,1,0:T(8,128)S(1)}, u32[]{:S(2)}, u32[]{:S(2)}) %collective-permute-start.18) | collective-permute-done | bytes 327712 | tf_op jit(solution)/shard_map/ppermute | solution.py:25
  83.5 3.9 %collective-permute-done.19 = f32[2,5,64,128]{3,2,1,0:T(8,128)S(1)} collective-permute-done((f32[2,5,64,128]{3,2,1,0:T(8,128)S(1)}, f32[2,5,64,128]{3,2,1,0:T(8,128)S(1)}, u32[]{:S(2)}, u32[]{:S(2)}) %collective-permute-start.19) | collective-permute-done | bytes 327712 | tf_op jit(solution)/shard_map/ppermute | solution.py:25
  87.6 2.1 %collective-permute-start.24 = (f32[5,64,128]{2,1,0:T(8,128)S(1)}, f32[5,64,128]{2,1,0:T(8,128)S(1)}, u32[]{:S(2)}, u32[]{:S(2)}) collective-permute-start(f32[5,64,128]{2,1,0:T(8,128)S(1)} %get-tuple-element.23), channel_id=1, source_target_pairs={{0,4},{1,5},{2,6},{3,7},{4,0},{5,1},{6,2},{7,3},{8,12},{9,13},{10,... | collective-permute-start | bytes 491528 | tf_op jit(solution)/shard_map/ppermute | solution.py:25
  89.7 1.3 %collective-permute-start.20 = (f32[2,8,128,128]{3,2,1,0:T(8,128)S(1)}, f32[2,8,128,128]{3,2,1,0:T(8,128)S(1)}, u32[]{:S(2)}, u32[]{:S(2)}) collective-permute-start(f32[2,8,128,128]{3,2,1,0:T(8,128)S(1)} %copy-done.7), channel_id=1, source_target_pairs={{0,1},{1,2},{2,3},{3,4},{4,5},{5,6},{6,7},{7,8},{8,9},{9,10},{10,1... | collective-permute-start | bytes 3145736 | tf_op jit(solution)/shard_map/ppermute | solution.py:21
  91.0 3.4 %collective-permute-done.26 = f32[2,5,64,128]{3,2,1,0:T(8,128)S(1)} collective-permute-done((f32[2,5,64,128]{3,2,1,0:T(8,128)S(1)}, f32[2,5,64,128]{3,2,1,0:T(8,128)S(1)}, u32[]{:S(2)}, u32[]{:S(2)}) %collective-permute-start.26) | collective-permute-done | bytes 327712 | tf_op jit(solution)/shard_map/ppermute | solution.py:25
  94.6 2.1 %collective-permute-start.23 = (f32[5,64,128]{2,1,0:T(8,128)S(1)}, f32[5,64,128]{2,1,0:T(8,128)S(1)}, u32[]{:S(2)}, u32[]{:S(2)}) collective-permute-start(f32[5,64,128]{2,1,0:T(8,128)S(1)} %get-tuple-element.27), channel_id=1, source_target_pairs={{0,4},{1,5},{2,6},{3,7},{4,0},{5,1},{6,2},{7,3},{8,12},{9,13},{10,... | collective-permute-start | bytes 491528 | tf_op jit(solution)/shard_map/ppermute | solution.py:25
  96.8 1.0 collective-permute-done.24
  97.9 10.0 %collective-permute-start.29 = (f32[5,64,128]{2,1,0:T(8,128)S(1)}, f32[5,64,128]{2,1,0:T(8,128)S(1)}, u32[]{:S(2)}, u32[]{:S(2)}) collective-permute-start(f32[5,64,128]{2,1,0:T(8,128)S(1)} %get-tuple-element.32), channel_id=1, source_target_pairs={{0,8},{1,9},{2,10},{3,11},{4,12},{5,13},{6,14},{7,15},{8,0},{9,1},... | collective-permute-start | bytes 491528 | tf_op jit(solution)/shard_map/ppermute | solution.py:25
  108.0 5.0 %collective-permute-done.29 = f32[5,64,128]{2,1,0:T(8,128)S(1)} collective-permute-done((f32[5,64,128]{2,1,0:T(8,128)S(1)}, f32[5,64,128]{2,1,0:T(8,128)S(1)}, u32[]{:S(2)}, u32[]{:S(2)}) %collective-permute-start.29) | collective-permute-done | bytes 163872 | tf_op jit(solution)/shard_map/ppermute | solution.py:25
  113.0 2.7 %collective-permute-done.25 = f32[5,64,128]{2,1,0:T(8,128)S(1)} collective-permute-done((f32[5,64,128]{2,1,0:T(8,128)S(1)}, f32[5,64,128]{2,1,0:T(8,128)S(1)}, u32[]{:S(2)}, u32[]{:S(2)}) %collective-permute-start.25) | collective-permute-done | bytes 163872 | tf_op jit(solution)/shard_map/ppermute | solution.py:25
  116.6 3.5 %finish.1 = f32[2,256,1024]{2,1,0:T(8,128)} custom-call(f32[2,256,1024]{2,1,0:T(8,128)S(1)} %copy-done, f32[2,8,256,128]{3,2,1,0:T(8,128)} %get-tuple-element.14.num_top, f32[2,8,128,128]{3,2,1,0:T(8,128)S(1)} %collective-permute-done.20.received, f32[8,256,128]{2,1,0:T(8,128)S(1)} %density.1), custom_call_target="tpu_custom_call" | custom-call | flops 2097152 | bytes 8388608 | tf_op jit(solution)/shard_map/finish/pallas_call | solution.py:320
  (68 shorter events, 5.1 us)
Async XLA Ops:
  0.6 50.1 %copy-start.2 = (bf16[4,256,256]{2,1,0:T(8,128)(2,1)S(1)}, bf16[4,256,256]{2,1,0:T(8,128)(2,1)}, u32[]{:S(2)}) copy-start(bf16[4,256,256]{2,1,0:T(8,128)(2,1)} %constant.68.clone.factors_in) | copy-start | bytes 1572868
  0.7 48.5 %copy-start.8 = (s32[8]{0:T(128)S(1)}, s32[8]{0:T(128)}, u32[]{:S(2)}) copy-start(s32[8]{0:T(128)} %param.14) | copy-start | bytes 100
  0.7 18.8 %collective-permute-start.13 = (f32[1,4,128,128]{3,2,1,0:T(8,128)}, f32[1,4,128,128]{3,2,1,0:T(8,128)S(1)}, u32[]{:S(2)}, u32[]{:S(2)}) collective-permute-start(f32[1,4,128,128]{3,2,1,0:T(8,128)} %bitcast.37), channel_id=1, source_target_pairs={{0,1},{1,0},{2,3},{3,2},{4,5},{5,4},{6,7},{7,6},{8,9},{9,8},{10,11... | collective-permute-start | bytes 786440 | tf_op jit(solution)/shard_map/ppermute | solution.py:25
  1.2 15.7 %collective-permute-start.7 = (f32[1,4,128,128]{3,2,1,0:T(8,128)}, f32[1,4,128,128]{3,2,1,0:T(8,128)S(1)}, u32[]{:S(2)}, u32[]{:S(2)}) collective-permute-start(f32[1,4,128,128]{3,2,1,0:T(8,128)} %bitcast.38), channel_id=1, source_target_pairs={{0,4},{1,5},{2,6},{3,7},{4,0},{5,1},{6,2},{7,3},{8,12},{9,13},{10,... | collective-permute-start | bytes 786440 | tf_op jit(solution)/shard_map/ppermute | solution.py:25
  3.9 15.3 %collective-permute-start.1 = (f32[1,4,128,128]{3,2,1,0:T(8,128)}, f32[1,4,128,128]{3,2,1,0:T(8,128)S(1)}, u32[]{:S(2)}, u32[]{:S(2)}) collective-permute-start(f32[1,4,128,128]{3,2,1,0:T(8,128)} %bitcast.39), channel_id=1, source_target_pairs={{0,8},{1,9},{2,10},{3,11},{4,12},{5,13},{6,14},{7,15},{8,0},{9,1},... | collective-permute-start | bytes 786440 | tf_op jit(solution)/shard_map/ppermute | solution.py:25
  7.7 42.9 %collective-permute-start = (f32[2,128,1024]{2,1,0:T(8,128)S(1)}, f32[2,128,1024]{2,1,0:T(8,128)}, u32[]{:S(2)}, u32[]{:S(2)}) collective-permute-start(f32[2,128,1024]{2,1,0:T(8,128)S(1)} %slice.137), channel_id=1, source_target_pairs={{1,0},{2,1},{3,2},{4,3},{5,4},{6,5},{7,6},{8,7},{9,8},{10,9},{11,1... | collective-permute-start | bytes 3145736 | tf_op jit(solution)/shard_map/ppermute | solution.py:21
  9.9 3.8 %collective-permute-start.3 = (s32[64]{0:T(128)S(1)}, s32[64]{0:T(128)S(1)}, u32[]{:S(2)}, u32[]{:S(2)}) collective-permute-start(s32[64]{0:T(128)S(1)} %reshape.39.meta), channel_id=1, source_target_pairs={{0,1},{1,2},{2,3},{3,4},{4,5},{5,6},{6,7},{7,8},{8,9},{9,10},{10,1... | collective-permute-start | bytes 776 | tf_op jit(solution)/shard_map/ppermute | solution.py:21
  13.8 18.6 %collective-permute-start.6 = (f32[1,4,128,128]{3,2,1,0:T(8,128)S(1)}, f32[1,4,128,128]{3,2,1,0:T(8,128)S(1)}, u32[]{:S(2)}, u32[]{:S(2)}) collective-permute-start(f32[1,4,128,128]{3,2,1,0:T(8,128)S(1)} %bitcast.40), channel_id=1, source_target_pairs={{0,2},{1,3},{2,0},{3,1},{4,6},{5,7},{6,4},{7,5},{8,10},{9,11},{10,... | collective-permute-start | bytes 786440 | tf_op jit(solution)/shard_map/ppermute | solution.py:25
  16.9 17.9 %collective-permute-start.16 = (f32[1,4,128,128]{3,2,1,0:T(8,128)S(1)}, f32[1,4,128,128]{3,2,1,0:T(8,128)S(1)}, u32[]{:S(2)}, u32[]{:S(2)}) collective-permute-start(f32[1,4,128,128]{3,2,1,0:T(8,128)S(1)} %collective-permute-done.7.rest_7_), channel_id=1, source_target_pairs={{0,1},{1,0},{2,3},{3,2},{4,5},{5,4},{6,7},{7,6},{8,9},{9,8},{10,11... | collective-permute-start | bytes 786440 | tf_op jit(solution)/shard_map/ppermute | solution.py:25
  19.1 15.7 %collective-permute-start.4 = (f32[1,4,128,128]{3,2,1,0:T(8,128)S(1)}, f32[1,4,128,128]{3,2,1,0:T(8,128)S(1)}, u32[]{:S(2)}, u32[]{:S(2)}) collective-permute-start(f32[1,4,128,128]{3,2,1,0:T(8,128)S(1)} %collective-permute-done.1.rest_0_), channel_id=1, source_target_pairs={{0,4},{1,5},{2,6},{3,7},{4,0},{5,1},{6,2},{7,3},{8,12},{9,13},{10,... | collective-permute-start | bytes 786440 | tf_op jit(solution)/shard_map/ppermute | solution.py:25
  19.5 18.5 %collective-permute-start.2 = (f32[1,4,128,128]{3,2,1,0:T(8,128)S(1)}, f32[1,4,128,128]{3,2,1,0:T(8,128)S(1)}, u32[]{:S(2)}, u32[]{:S(2)}) collective-permute-start(f32[1,4,128,128]{3,2,1,0:T(8,128)S(1)} %collective-permute-done.1.rest_0_), channel_id=1, source_target_pairs={{0,2},{1,3},{2,0},{3,1},{4,6},{5,7},{6,4},{7,5},{8,10},{9,11},{10,... | collective-permute-start | bytes 786440 | tf_op jit(solution)/shard_map/ppermute | solution.py:25
  32.4 11.2 %collective-permute-start.8 = (f32[1,4,128,128]{3,2,1,0:T(8,128)S(1)}, f32[1,4,128,128]{3,2,1,0:T(8,128)S(1)}, u32[]{:S(2)}, u32[]{:S(2)}) collective-permute-start(f32[1,4,128,128]{3,2,1,0:T(8,128)S(1)} %collective-permute-done.7.rest_7_), channel_id=1, source_target_pairs={{0,2},{1,3},{2,0},{3,1},{4,6},{5,7},{6,4},{7,5},{8,10},{9,11},{10,... | collective-permute-start | bytes 786440 | tf_op jit(solution)/shard_map/ppermute | solution.py:25
  34.8 8.8 %collective-permute-start.14 = (f32[1,4,128,128]{3,2,1,0:T(8,128)S(1)}, f32[1,4,128,128]{3,2,1,0:T(8,128)S(1)}, u32[]{:S(2)}, u32[]{:S(2)}) collective-permute-start(f32[1,4,128,128]{3,2,1,0:T(8,128)S(1)} %collective-permute-done.6.rest_5_), channel_id=1, source_target_pairs={{0,1},{1,0},{2,3},{3,2},{4,5},{5,4},{6,7},{7,6},{8,9},{9,8},{10,11... | collective-permute-start | bytes 786440 | tf_op jit(solution)/shard_map/ppermute | solution.py:25
  34.8 9.3 %collective-permute-start.9 = (f32[1,4,128,128]{3,2,1,0:T(8,128)S(1)}, f32[1,4,128,128]{3,2,1,0:T(8,128)S(1)}, u32[]{:S(2)}, u32[]{:S(2)}) collective-permute-start(f32[1,4,128,128]{3,2,1,0:T(8,128)S(1)} %collective-permute-done.1.rest_0_), channel_id=1, source_target_pairs={{0,1},{1,0},{2,3},{3,2},{4,5},{5,4},{6,7},{7,6},{8,9},{9,8},{10,11... | collective-permute-start | bytes 786440 | tf_op jit(solution)/shard_map/ppermute | solution.py:25
  38.0 11.2 %collective-permute-start.5 = (f32[1,4,128,128]{3,2,1,0:T(8,128)S(1)}, f32[1,4,128,128]{3,2,1,0:T(8,128)S(1)}, u32[]{:S(2)}, u32[]{:S(2)}) collective-permute-start(f32[1,4,128,128]{3,2,1,0:T(8,128)S(1)} %collective-permute-done.4.rest_3_), channel_id=1, source_target_pairs={{0,2},{1,3},{2,0},{3,1},{4,6},{5,7},{6,4},{7,5},{8,10},{9,11},{10,... | collective-permute-start | bytes 786440 | tf_op jit(solution)/shard_map/ppermute | solution.py:25
  43.6 5.7 %collective-permute-start.10 = (f32[1,4,128,128]{3,2,1,0:T(8,128)S(1)}, f32[1,4,128,128]{3,2,1,0:T(8,128)S(1)}, u32[]{:S(2)}, u32[]{:S(2)}) collective-permute-start(f32[1,4,128,128]{3,2,1,0:T(8,128)S(1)} %collective-permute-done.2.rest_1_), channel_id=1, source_target_pairs={{0,1},{1,0},{2,3},{3,2},{4,5},{5,4},{6,7},{7,6},{8,9},{9,8},{10,11... | collective-permute-start | bytes 786440 | tf_op jit(solution)/shard_map/ppermute | solution.py:25
  43.6 5.6 %collective-permute-start.15 = (f32[1,4,128,128]{3,2,1,0:T(8,128)S(1)}, f32[1,4,128,128]{3,2,1,0:T(8,128)S(1)}, u32[]{:S(2)}, u32[]{:S(2)}) collective-permute-start(f32[1,4,128,128]{3,2,1,0:T(8,128)S(1)} %collective-permute-done.8.rest_6_), channel_id=1, source_target_pairs={{0,1},{1,0},{2,3},{3,2},{4,5},{5,4},{6,7},{7,6},{8,9},{9,8},{10,11... | collective-permute-start | bytes 786440 | tf_op jit(solution)/shard_map/ppermute | solution.py:25
  44.1 5.1 %collective-permute-start.12 = (f32[1,4,128,128]{3,2,1,0:T(8,128)S(1)}, f32[1,4,128,128]{3,2,1,0:T(8,128)S(1)}, u32[]{:S(2)}, u32[]{:S(2)}) collective-permute-start(f32[1,4,128,128]{3,2,1,0:T(8,128)S(1)} %collective-permute-done.4.rest_3_), channel_id=1, source_target_pairs={{0,1},{1,0},{2,3},{3,2},{4,5},{5,4},{6,7},{7,6},{8,9},{9,8},{10,11... | collective-permute-start | bytes 786440 | tf_op jit(solution)/shard_map/ppermute | solution.py:25
  49.1 1.5 %collective-permute-start.11 = (f32[1,4,128,128]{3,2,1,0:T(8,128)S(1)}, f32[1,4,128,128]{3,2,1,0:T(8,128)S(1)}, u32[]{:S(2)}, u32[]{:S(2)}) collective-permute-start(f32[1,4,128,128]{3,2,1,0:T(8,128)S(1)} %collective-permute-done.5.rest_2_), channel_id=1, source_target_pairs={{0,1},{1,0},{2,3},{3,2},{4,5},{5,4},{6,7},{7,6},{8,9},{9,8},{10,11... | collective-permute-start | bytes 786440 | tf_op jit(solution)/shard_map/ppermute | solution.py:25
  65.7 5.8 %collective-permute-start.17 = (f32[4,5,128,128]{3,2,1,0:T(8,128)}, f32[4,5,128,128]{3,2,1,0:T(8,128)S(1)}, u32[]{:S(2)}, u32[]{:S(2)}) collective-permute-start(f32[4,5,128,128]{3,2,1,0:T(8,128)} %get-tuple-element.17), channel_id=1, source_target_pairs={{0,1},{1,0},{2,3},{3,2},{4,5},{5,4},{6,7},{7,6},{8,9},{9,8},{10,11... | collective-permute-start | bytes 3932168 | tf_op jit(solution)/shard_map/ppermute | solution.py:25
  68.7 10.3 %collective-permute-start.21 = (f32[4,5,128,128]{3,2,1,0:T(8,128)}, f32[4,5,128,128]{3,2,1,0:T(8,128)S(1)}, u32[]{:S(2)}, u32[]{:S(2)}) collective-permute-start(f32[4,5,128,128]{3,2,1,0:T(8,128)} %get-tuple-element.22), channel_id=1, source_target_pairs={{0,1},{1,0},{2,3},{3,2},{4,5},{5,4},{6,7},{7,6},{8,9},{9,8},{10,11... | collective-permute-start | bytes 3932168 | tf_op jit(solution)/shard_map/ppermute | solution.py:25
  72.9 10.6 %collective-permute-start.18 = (f32[2,5,64,128]{3,2,1,0:T(8,128)S(1)}, f32[2,5,64,128]{3,2,1,0:T(8,128)S(1)}, u32[]{:S(2)}, u32[]{:S(2)}) collective-permute-start(f32[2,5,64,128]{3,2,1,0:T(8,128)S(1)} %pad_maximum_fusion), channel_id=1, source_target_pairs={{0,2},{1,3},{2,0},{3,1},{4,6},{5,7},{6,4},{7,5},{8,10},{9,11},{10,... | collective-permute-start | bytes 983048 | tf_op jit(solution)/shard_map/ppermute | solution.py:25
  73.0 14.4 %collective-permute-start.19 = (f32[2,5,64,128]{3,2,1,0:T(8,128)S(1)}, f32[2,5,64,128]{3,2,1,0:T(8,128)S(1)}, u32[]{:S(2)}, u32[]{:S(2)}) collective-permute-start(f32[2,5,64,128]{3,2,1,0:T(8,128)S(1)} %pad_maximum_fusion.1), channel_id=1, source_target_pairs={{0,4},{1,5},{2,6},{3,7},{4,0},{5,1},{6,2},{7,3},{8,12},{9,13},{10,... | collective-permute-start | bytes 983048 | tf_op jit(solution)/shard_map/ppermute | solution.py:25
  79.1 12.0 %collective-permute-start.22 = (f32[2,5,64,128]{3,2,1,0:T(8,128)S(1)}, f32[2,5,64,128]{3,2,1,0:T(8,128)S(1)}, u32[]{:S(2)}, u32[]{:S(2)}) collective-permute-start(f32[2,5,64,128]{3,2,1,0:T(8,128)S(1)} %pad_maximum_fusion.2), channel_id=1, source_target_pairs={{0,2},{1,3},{2,0},{3,1},{4,6},{5,7},{6,4},{7,5},{8,10},{9,11},{10,... | collective-permute-start | bytes 983048 | tf_op jit(solution)/shard_map/ppermute | solution.py:25
  79.2 15.3 %collective-permute-start.26 = (f32[2,5,64,128]{3,2,1,0:T(8,128)S(1)}, f32[2,5,64,128]{3,2,1,0:T(8,128)S(1)}, u32[]{:S(2)}, u32[]{:S(2)}) collective-permute-start(f32[2,5,64,128]{3,2,1,0:T(8,128)S(1)} %pad_maximum_fusion.3), channel_id=1, source_target_pairs={{0,4},{1,5},{2,6},{3,7},{4,0},{5,1},{6,2},{7,3},{8,12},{9,13},{10,... | collective-permute-start | bytes 983048 | tf_op jit(solution)/shard_map/ppermute | solution.py:25
  87.6 10.2 %collective-permute-start.24 = (f32[5,64,128]{2,1,0:T(8,128)S(1)}, f32[5,64,128]{2,1,0:T(8,128)S(1)}, u32[]{:S(2)}, u32[]{:S(2)}) collective-permute-start(f32[5,64,128]{2,1,0:T(8,128)S(1)} %get-tuple-element.23), channel_id=1, source_target_pairs={{0,4},{1,5},{2,6},{3,7},{4,0},{5,1},{6,2},{7,3},{8,12},{9,13},{10,... | collective-permute-start | bytes 491528 | tf_op jit(solution)/shard_map/ppermute | solution.py:25
  89.7 8.1 %collective-permute-start.28 = (f32[5,64,128]{2,1,0:T(8,128)S(1)}, f32[5,64,128]{2,1,0:T(8,128)S(1)}, u32[]{:S(2)}, u32[]{:S(2)}) collective-permute-start(f32[5,64,128]{2,1,0:T(8,128)S(1)} %get-tuple-element.34), channel_id=1, source_target_pairs={{0,2},{1,3},{2,0},{3,1},{4,6},{5,7},{6,4},{7,5},{8,10},{9,11},{10,... | collective-permute-start | bytes 491528 | tf_op jit(solution)/shard_map/ppermute | solution.py:25
  89.7 26.9 %collective-permute-start.20 = (f32[2,8,128,128]{3,2,1,0:T(8,128)S(1)}, f32[2,8,128,128]{3,2,1,0:T(8,128)S(1)}, u32[]{:S(2)}, u32[]{:S(2)}) collective-permute-start(f32[2,8,128,128]{3,2,1,0:T(8,128)S(1)} %copy-done.7), channel_id=1, source_target_pairs={{0,1},{1,2},{2,3},{3,4},{4,5},{5,6},{6,7},{7,8},{8,9},{9,10},{10,1... | collective-permute-start | bytes 3145736 | tf_op jit(solution)/shard_map/ppermute | solution.py:21
  94.5 13.4 %collective-permute-start.27 = (f32[5,64,128]{2,1,0:T(8,128)S(1)}, f32[5,64,128]{2,1,0:T(8,128)S(1)}, u32[]{:S(2)}, u32[]{:S(2)}) collective-permute-start(f32[5,64,128]{2,1,0:T(8,128)S(1)} %get-tuple-element.26), channel_id=1, source_target_pairs={{0,2},{1,3},{2,0},{3,1},{4,6},{5,7},{6,4},{7,5},{8,10},{9,11},{10,... | collective-permute-start | bytes 491528 | tf_op jit(solution)/shard_map/ppermute | solution.py:25
  94.6 13.3 %collective-permute-start.23 = (f32[5,64,128]{2,1,0:T(8,128)S(1)}, f32[5,64,128]{2,1,0:T(8,128)S(1)}, u32[]{:S(2)}, u32[]{:S(2)}) collective-permute-start(f32[5,64,128]{2,1,0:T(8,128)S(1)} %get-tuple-element.27), channel_id=1, source_target_pairs={{0,4},{1,5},{2,6},{3,7},{4,0},{5,1},{6,2},{7,3},{8,12},{9,13},{10,... | collective-permute-start | bytes 491528 | tf_op jit(solution)/shard_map/ppermute | solution.py:25
  97.9 15.1 %collective-permute-start.29 = (f32[5,64,128]{2,1,0:T(8,128)S(1)}, f32[5,64,128]{2,1,0:T(8,128)S(1)}, u32[]{:S(2)}, u32[]{:S(2)}) collective-permute-start(f32[5,64,128]{2,1,0:T(8,128)S(1)} %get-tuple-element.32), channel_id=1, source_target_pairs={{0,8},{1,9},{2,10},{3,11},{4,12},{5,13},{6,14},{7,15},{8,0},{9,1},... | collective-permute-start | bytes 491528 | tf_op jit(solution)/shard_map/ppermute | solution.py:25
  107.9 7.8 %collective-permute-start.25 = (f32[5,64,128]{2,1,0:T(8,128)S(1)}, f32[5,64,128]{2,1,0:T(8,128)S(1)}, u32[]{:S(2)}, u32[]{:S(2)}) collective-permute-start(f32[5,64,128]{2,1,0:T(8,128)S(1)} %get-tuple-element.33), channel_id=1, source_target_pairs={{0,8},{1,9},{2,10},{3,11},{4,12},{5,13},{6,14},{7,15},{8,0},{9,1},... | collective-permute-start | bytes 491528 | tf_op jit(solution)/shard_map/ppermute | solution.py:25
  (7 other events, 65.3 us)

commit v4 on v3

--- a/solution.py
+++ b/solution.py
@@ -13,7 +13,7 @@
 floor_level = 0.3
 LANES = 128
 SLOTS_AT_ONCE = 4
-VMEM_BYTES = 48 * 1024 * 1024
+VMEM_BYTES = 26 * 1024 * 1024
 
 
 def moved(block, distance):
@@ -95,19 +95,19 @@
     return jnp.dot(table, jnp.concatenate([high, low, high], axis=0), preferred_element_type=jnp.float32)
 
 
-def update_kernel(dims, meta, slot_of, live, amplitudes_in, obj, rim, factors_in, *rest):
+def update_kernel(dims, meta, slot_of, live, amplitudes, obj, rim, factors, *rest):
     piece_sizes, group_sizes, slots = dims
     pieces = rest[: len(piece_sizes)]
     rest = rest[len(piece_sizes) :]
     num_top, num_low, squares = rest[:3]
     groups = rest[3 : 3 + len(group_sizes)]
-    table, ext, acc, part, amplitudes, factors, in_sems, out_sems = rest[3 + len(group_sizes) :]
+    table, ext, acc, part, in_sems, out_sems = rest[3 + len(group_sizes) :]
     points = LANES
     tile_rows = obj.shape[1]
     blocks = obj.shape[2] // LANES
     modes = table.shape[1] // 2
 
-    moves = [(factors_in, factors), (amplitudes_in, amplitudes)]
+    moves = []
     for b in range(blocks):
         columns = pl.ds(b * LANES, LANES)
         moves.append((obj.at[:, :, columns], ext.at[:, b, pl.ds(0, tile_rows), :]))
@@ -133,8 +133,9 @@
     def step(i, carry):
         wins, probes, places, waves, flags = [], [], [], [], []
         for u in range(SLOTS_AT_ONCE):
-            p = i * SLOTS_AT_ONCE + u
-            flags.append((p < count).astype(jnp.float32))
+            at = i * SLOTS_AT_ONCE + u
+            flags.append((at < count).astype(jnp.float32))
+            p = jnp.minimum(at, count - 1)
             row, col, scan = meta[4 * p], meta[4 * p + 1], meta[4 * p + 2]
             slot = slot_of[scan]
             block, shift = col // LANES, col % LANES
@@ -236,16 +237,14 @@
             jax.ShapeDtypeStruct((scans, points, points), f32),
         ]
         + [jax.ShapeDtypeStruct((size, channels + 1, points, points), f32) for size in group_sizes],
-        in_specs=[smem] * 3 + [anywhere] * 3 + [pl.BlockSpec(memory_space=pltpu.HBM)] + [anywhere] * len(pieces),
+        in_specs=[smem] * 3 + [vmem, anywhere, anywhere, vmem] + [anywhere] * len(pieces),
         out_specs=[anywhere, anywhere, vmem] + [anywhere] * len(group_sizes),
         scratch_shapes=[
             pltpu.VMEM((slots, channels, points, points), f32),
             pltpu.VMEM((2, blocks + 1, tile_rows + points, LANES), f32),
             pltpu.VMEM((2, blocks + 1, tile_rows + points, LANES), f32),
             pltpu.VMEM((slots, channels + 1, points, points), f32),
-            pltpu.VMEM(amplitudes.shape, f32),
-            pltpu.VMEM(factors.shape, factors.dtype),
-            pltpu.SemaphoreType.DMA((len(pieces) + 2 * blocks + 2,)),
+            pltpu.SemaphoreType.DMA((len(pieces) + 2 * blocks,)),
             pltpu.SemaphoreType.DMA((len(group_sizes) + 2,)),
         ],
         compiler_params=pltpu.CompilerParams(vmem_limit_bytes=VMEM_BYTES),
@@ -328,6 +327,27 @@
     )(obj, num_top, received, density)
 
 
+def staged_kernel(*refs):
+    half = (len(refs) - 1) // 2
+    copies = [pltpu.make_async_copy(refs[k], refs[half + k], refs[-1].at[k]) for k in range(half)]
+    for copy in copies:
+        copy.start()
+    for copy in copies:
+        copy.wait()
+
+
+def staged(*arrays):
+    return pl.pallas_call(
+        staged_kernel,
+        out_shape=[jax.ShapeDtypeStruct(array.shape, array.dtype) for array in arrays],
+        in_specs=[pl.BlockSpec(memory_space=pl.ANY)] * len(arrays),
+        out_specs=[pl.BlockSpec(memory_space=pltpu.VMEM)] * len(arrays),
+        scratch_shapes=[pltpu.SemaphoreType.DMA((len(arrays),))],
+        compiler_params=pltpu.CompilerParams(vmem_limit_bytes=VMEM_BYTES),
+        name="staged",
+    )(*arrays)
+
+
 def local(object_strip, probe_store, amplitudes, scan_of, offsets, counts, owner):
     device = lax.axis_index("row")
     size = lax.axis_size("row")
@@ -343,20 +363,20 @@
 
     is_live = (jnp.arange(slot_count, dtype=jnp.int32) < counts[0]).astype(jnp.int32)
     meta = jnp.stack([offsets[:, 0] - device * tile_rows, offsets[:, 1], scan_of, is_live], axis=1).reshape(-1)
-    above = moved(meta, 1)
 
     if swaps:
         held = {0: own_probe}
         for key in (8, 4, 2):
             held[key] = swapped(own_probe, key)
+        held[8], held[4], held[2] = lax.optimization_barrier((held[8], held[4], held[2]))
         held[6] = swapped(held[4], 2)
         held[12] = swapped(held[8], 4)
         held[10] = swapped(held[8], 2)
         held[14] = swapped(held[12], 2)
-        held[10] = after(held[10], above)
         for key in list(held):
             held[key | 1] = swapped(held[key], 1)
         order = [key | core for core in (0, 1) for key in FAR + NEAR]
+        amplitudes, factors, held[0] = staged(amplitudes, after(transform_tables(points), held[12]), own_probe)
         pieces = [held[key] for key in order]
         key = jnp.bitwise_xor(owner, device)
         side = key // 2 % 4
@@ -367,10 +387,13 @@
         pieces = [lax.psum(jnp.where(owned, own_probe, 0.0), "row")]
         slot_of = jnp.arange(scan_count, dtype=jnp.int32)
         group_sizes = (scan_count,)
-    rim = moved(object_strip[:, :points, :], -1)
-
+        factors = transform_tables(points)
+
+    rim = moved(after(object_strip[:, :points, :], slot_of), -1)
+    above = moved(after(meta, held[7]) if swaps else meta, 1)
+    rim = after(rim, above)
     num_top, num_low, squares, *groups = update(
-        meta, slot_of, counts, amplitudes, object_strip, rim, transform_tables(points), pieces, group_sizes
+        meta, slot_of, counts, amplitudes, object_strip, rim, factors, pieces, group_sizes
     )
 
     density = density_of(meta, above, squares, tile_rows, blocks)

time: 121 us -> 115 us (0.950); the launches traced: 120 us -> 112 us
  starting transfers between devices: 46.4 us -> 37.2 us
  Pallas kernels: 20.5 us -> 16.3 us
  waiting for transfers between devices: 47.4 us -> 50.2 us
  local copies, waits for them, and re-layouts: 1.5 us -> 3.68 us
    ppermute x27, starting transfers between devices: 40.7 us -> 32.8 us  [swapped(): lax.ppermute(block, 'row', [(i, i ^ mask) for i in range(lax.axis_size('r...]
    ppermute x27, waiting for transfers between devices: 46.6 us -> 50.2 us  [swapped(): lax.ppermute(block, 'row', [(i, i ^ mask) for i in range(lax.axis_size('r...]
    pallas_call x1, Pallas kernels: 15 us -> 12.2 us  [update(): pl.pallas_call(functools.partial(update_kernel, (piece_sizes, group_sizes...]
    pallas_call x1, Pallas kernels: 3.47 us -> 1.8 us  [finish(): pl.pallas_call(finish_kernel, out_shape=jax.ShapeDtypeStruct(obj.shape, o...]
    ppermute x3, starting transfers between devices: 5.67 us -> 4.4 us  [moved(): lax.ppermute(block, 'row', [(i, i + distance) for i in range(size) if 0 <...]
    add x2, other arithmetic: 1.43 us -> 0.19 us  [pick(): return pair[0][at, :, rows] + pair[1][at, :, rows]]
  transfers between devices with their start and end apart: 30 -> 30, of which waited for: 14 -> 15; matrix products, arithmetic and copies ran while one was open for 3% -> 5% of each run, Pallas kernels for 2% -> 2%
where the time goes in v4:
time: 115 us; the launch traced here: 112 us
  waiting for transfers between devices  50.2 us (44%)
  starting transfers between devices  37.2 us (32%)
  Pallas kernels  16.3 us (14%)
  local copies, waits for them, and re-layouts  3.68 us (3%)
  other arithmetic  3.54 us (3%)
  between operations  1.5 us (1%)
    ppermute x27, waiting for transfers between devices, swapped(): lax.ppermute(block, 'row', [(i, i ^ mask) for i in range(lax.axis_size('r...  50.2 us
    ppermute x27, starting transfers between devices, swapped(): lax.ppermute(block, 'row', [(i, i ^ mask) for i in range(lax.axis_size('r...  32.8 us
    pallas_call x1, Pallas kernels, update(): pl.pallas_call(functools.partial(update_kernel, (piece_sizes, group_sizes...  12.2 us
    ppermute x3, starting transfers between devices, moved(): lax.ppermute(block, 'row', [(i, i + distance) for i in range(size) if 0 <...  4.4 us
    slice x1, local copies, waits for them, and re-layouts, local(): rim = moved(after(object_strip[:, :points, :], slot_of), -1)  2.46 us
  transfers between devices with their start and end apart: 30, of which 15 were waited for; matrix products, arithmetic and copies ran while one was open for 5% of the time, Pallas kernels for 2%

profile of v4, /device:TPU:0, one launch (start us, length us, event | category | flops | bytes accessed | tf_op | source)
XLA Modules:
  0.0 112.4 jit_solution(17990039789834706874)
XLA Ops:
  0.6 3.0 %collective-permute-start.2 = (f32[1,4,128,128]{3,2,1,0:T(8,128)}, f32[1,4,128,128]{3,2,1,0:T(8,128)}, u32[]{:S(2)}, u32[]{:S(2)}) collective-permute-start(f32[1,4,128,128]{3,2,1,0:T(8,128)} %bitcast.37), channel_id=1, source_target_pairs={{0,2},{1,3},{2,0},{3,1},{4,6},{5,7},{6,4},{7,5},{8,10},{9,11},{10,... | collective-permute-start | bytes 786440 | tf_op jit(solution)/shard_map/ppermute | solution.py:25
  3.7 1.6 %collective-permute-start.1 = (f32[1,4,128,128]{3,2,1,0:T(8,128)}, f32[1,4,128,128]{3,2,1,0:T(8,128)}, u32[]{:S(2)}, u32[]{:S(2)}) collective-permute-start(f32[1,4,128,128]{3,2,1,0:T(8,128)} %bitcast.38), channel_id=1, source_target_pairs={{0,4},{1,5},{2,6},{3,7},{4,0},{5,1},{6,2},{7,3},{8,12},{9,13},{10,... | collective-permute-start | bytes 786440 | tf_op jit(solution)/shard_map/ppermute | solution.py:25
  5.3 2.6 %collective-permute-start = (f32[1,4,128,128]{3,2,1,0:T(8,128)}, f32[1,4,128,128]{3,2,1,0:T(8,128)}, u32[]{:S(2)}, u32[]{:S(2)}) collective-permute-start(f32[1,4,128,128]{3,2,1,0:T(8,128)} %bitcast.39), channel_id=1, source_target_pairs={{0,8},{1,9},{2,10},{3,11},{4,12},{5,13},{6,14},{7,15},{8,0},{9,1},... | collective-permute-start | bytes 786440 | tf_op jit(solution)/shard_map/ppermute | solution.py:25
  7.9 2.5 %slice.137 = f32[2,128,1024]{2,1,0:T(8,128)} slice(f32[2,256,1024]{2,1,0:T(8,128)} %obj.3), slice={[0:2], [0:128], [0:1024]} | slice | bytes 2097152 | tf_op jit(solution)/shard_map/slice | solution.py:392
  11.0 1.3 %collective-permute-start.4 = (f32[2,128,1024]{2,1,0:T(8,128)}, f32[2,128,1024]{2,1,0:T(8,128)}, u32[]{:S(2)}, u32[]{:S(2)}) collective-permute-start(f32[2,128,1024]{2,1,0:T(8,128)} %slice.137), channel_id=1, source_target_pairs={{1,0},{2,1},{3,2},{4,3},{5,4},{6,5},{7,6},{8,7},{9,8},{10,9},{11,1... | collective-permute-start | bytes 3145736 | tf_op jit(solution)/shard_map/ppermute | solution.py:21
  12.3 5.0 %collective-permute-done.1.rest_7_ = f32[1,4,128,128]{3,2,1,0:T(8,128)} collective-permute-done((f32[1,4,128,128]{3,2,1,0:T(8,128)}, f32[1,4,128,128]{3,2,1,0:T(8,128)}, u32[]{:S(2)}, u32[]{:S(2)}) %collective-permute-start.1) | collective-permute-done | bytes 262176 | tf_op jit(solution)/shard_map/ppermute | solution.py:25
  17.3 2.5 %collective-permute-done.rest_0_ = f32[1,4,128,128]{3,2,1,0:T(8,128)} collective-permute-done((f32[1,4,128,128]{3,2,1,0:T(8,128)}, f32[1,4,128,128]{3,2,1,0:T(8,128)}, u32[]{:S(2)}, u32[]{:S(2)}) %collective-permute-start) | collective-permute-done | bytes 262176 | tf_op jit(solution)/shard_map/ppermute | solution.py:25
  20.6 12.5 %collective-permute-done.5.rest_6_ = f32[1,4,128,128]{3,2,1,0:T(8,128)} collective-permute-done((f32[1,4,128,128]{3,2,1,0:T(8,128)}, f32[1,4,128,128]{3,2,1,0:T(8,128)}, u32[]{:S(2)}, u32[]{:S(2)}) %collective-permute-start.5) | collective-permute-done | bytes 262176 | tf_op jit(solution)/shard_map/ppermute | solution.py:25
  33.6 2.5 %collective-permute-start.8 = (f32[1,4,128,128]{3,2,1,0:T(8,128)}, f32[1,4,128,128]{3,2,1,0:T(8,128)}, u32[]{:S(2)}, u32[]{:S(2)}) collective-permute-start(f32[1,4,128,128]{3,2,1,0:T(8,128)} %collective-permute-done.rest_0_), channel_id=1, source_target_pairs={{0,2},{1,3},{2,0},{3,1},{4,6},{5,7},{6,4},{7,5},{8,10},{9,11},{10,... | collective-permute-start | bytes 786440 | tf_op jit(solution)/shard_map/ppermute | solution.py:25
  36.1 1.7 %collective-permute-start.9 = (f32[1,4,128,128]{3,2,1,0:T(8,128)}, f32[1,4,128,128]{3,2,1,0:T(8,128)}, u32[]{:S(2)}, u32[]{:S(2)}) collective-permute-start(f32[1,4,128,128]{3,2,1,0:T(8,128)} %collective-permute-done.3.rest_3_), channel_id=1, source_target_pairs={{0,2},{1,3},{2,0},{3,1},{4,6},{5,7},{6,4},{7,5},{8,10},{9,11},{10,... | collective-permute-start | bytes 786440 | tf_op jit(solution)/shard_map/ppermute | solution.py:25
  37.7 0.8 slice_subtract_fusion
  40.0 1.8 %collective-permute-start.7 = (s32[64]{0:T(128)S(1)}, s32[64]{0:T(128)S(1)}, u32[]{:S(2)}, u32[]{:S(2)}) collective-permute-start(s32[64]{0:T(128)S(1)} %reshape.39.meta), channel_id=1, source_target_pairs={{0,1},{1,2},{2,3},{3,4},{4,5},{5,6},{6,7},{7,8},{8,9},{9,10},{10,1... | collective-permute-start | bytes 776 | tf_op jit(solution)/shard_map/ppermute | solution.py:21
  41.8 0.8 collective-permute-start.16
  42.6 0.9 collective-permute-done.8.rest_1_
  43.5 5.0 %collective-permute-done.9.rest_2_ = f32[1,4,128,128]{3,2,1,0:T(8,128)} collective-permute-done((f32[1,4,128,128]{3,2,1,0:T(8,128)}, f32[1,4,128,128]{3,2,1,0:T(8,128)}, u32[]{:S(2)}, u32[]{:S(2)}) %collective-permute-start.9) | collective-permute-done | bytes 262176 | tf_op jit(solution)/shard_map/ppermute | solution.py:25
  49.1 1.0 copy-done.3
  51.0 12.2 %update.1 = (f32[2,8,256,128]{3,2,1,0:T(8,128)S(1)}, f32[2,8,128,128]{3,2,1,0:T(8,128)S(1)}, f32[8,128,128]{2,1,0:T(8,128)S(1)}, f32[4,5,128,128]{3,2,1,0:T(8,12...) custom-call(s32[64]{0:T(128)S(1)} %reshape.39.meta, ...), custom_call_target="tpu_custom_call" | custom-call | flops 6000000000 | bytes 16777216 | tf_op jit(solution)/shard_map/update/pallas_call | solution.py:232
  63.7 2.5 %collective-permute-done.17 = f32[4,5,128,128]{3,2,1,0:T(8,128)S(1)} collective-permute-done((f32[4,5,128,128]{3,2,1,0:T(8,128)S(1)}, f32[4,5,128,128]{3,2,1,0:T(8,128)S(1)}, u32[]{:S(2)}, u32[]{:S(2)}) %collective-permute-start.17) | collective-permute-done | bytes 1310752 | tf_op jit(solution)/shard_map/ppermute | solution.py:25
  66.4 4.7 %collective-permute-start.18 = (f32[2,5,64,128]{3,2,1,0:T(8,128)S(1)}, f32[2,5,64,128]{3,2,1,0:T(8,128)S(1)}, u32[]{:S(2)}, u32[]{:S(2)}) collective-permute-start(f32[2,5,64,128]{3,2,1,0:T(8,128)S(1)} %pad_maximum_fusion), channel_id=1, source_target_pairs={{0,2},{1,3},{2,0},{3,1},{4,6},{5,7},{6,4},{7,5},{8,10},{9,11},{10,... | collective-permute-start | bytes 983048 | tf_op jit(solution)/shard_map/ppermute | solution.py:25
  71.3 1.6 %collective-permute-start.22 = (f32[2,5,64,128]{3,2,1,0:T(8,128)S(1)}, f32[2,5,64,128]{3,2,1,0:T(8,128)S(1)}, u32[]{:S(2)}, u32[]{:S(2)}) collective-permute-start(f32[2,5,64,128]{3,2,1,0:T(8,128)S(1)} %pad_maximum_fusion.2), channel_id=1, source_target_pairs={{0,2},{1,3},{2,0},{3,1},{4,6},{5,7},{6,4},{7,5},{8,10},{9,11},{10,... | collective-permute-start | bytes 983048 | tf_op jit(solution)/shard_map/ppermute | solution.py:25
  73.5 2.2 %density.1 = f32[8,256,128]{2,1,0:T(8,128)S(1)} custom-call(s32[64]{0:T(128)S(1)} %reshape.39.meta, s32[64]{0:T(128)S(1)} %collective-permute-done.7.above, f32[8,128,128]{2,1,0:T(8,128)S(1)} %get-tuple-element.37.squares), custom_call_target="tpu_custom_call" | custom-call | flops 8388608 | bytes 8388608 | tf_op jit(solution)/shard_map/density/pallas_call | solution.py:294
  75.6 3.9 %collective-permute-done.18 = f32[2,5,64,128]{3,2,1,0:T(8,128)S(1)} collective-permute-done((f32[2,5,64,128]{3,2,1,0:T(8,128)S(1)}, f32[2,5,64,128]{3,2,1,0:T(8,128)S(1)}, u32[]{:S(2)}, u32[]{:S(2)}) %collective-permute-start.18) | collective-permute-done | bytes 327712 | tf_op jit(solution)/shard_map/ppermute | solution.py:25
  79.5 2.2 %collective-permute-done.19 = f32[2,5,64,128]{3,2,1,0:T(8,128)S(1)} collective-permute-done((f32[2,5,64,128]{3,2,1,0:T(8,128)S(1)}, f32[2,5,64,128]{3,2,1,0:T(8,128)S(1)}, u32[]{:S(2)}, u32[]{:S(2)}) %collective-permute-start.19) | collective-permute-done | bytes 327712 | tf_op jit(solution)/shard_map/ppermute | solution.py:25
  82.3 1.3 %collective-permute-start.20 = (f32[2,8,128,128]{3,2,1,0:T(8,128)S(1)}, f32[2,8,128,128]{3,2,1,0:T(8,128)S(1)}, u32[]{:S(2)}, u32[]{:S(2)}) collective-permute-start(f32[2,8,128,128]{3,2,1,0:T(8,128)S(1)} %get-tuple-element.36), channel_id=1, source_target_pairs={{0,1},{1,2},{2,3},{3,4},{4,5},{5,6},{6,7},{7,8},{8,9},{9,10},{10,1... | collective-permute-start | bytes 3145736 | tf_op jit(solution)/shard_map/ppermute | solution.py:21
  83.7 2.9 %collective-permute-done.22 = f32[2,5,64,128]{3,2,1,0:T(8,128)S(1)} collective-permute-done((f32[2,5,64,128]{3,2,1,0:T(8,128)S(1)}, f32[2,5,64,128]{3,2,1,0:T(8,128)S(1)}, u32[]{:S(2)}, u32[]{:S(2)}) %collective-permute-start.22) | collective-permute-done | bytes 327712 | tf_op jit(solution)/shard_map/ppermute | solution.py:25
  86.5 2.2 %collective-permute-done.26 = f32[2,5,64,128]{3,2,1,0:T(8,128)S(1)} collective-permute-done((f32[2,5,64,128]{3,2,1,0:T(8,128)S(1)}, f32[2,5,64,128]{3,2,1,0:T(8,128)S(1)}, u32[]{:S(2)}, u32[]{:S(2)}) %collective-permute-start.26) | collective-permute-done | bytes 327712 | tf_op jit(solution)/shard_map/ppermute | solution.py:25
  89.3 2.9 %collective-permute-done.24 = f32[5,64,128]{2,1,0:T(8,128)S(1)} collective-permute-done((f32[5,64,128]{2,1,0:T(8,128)S(1)}, f32[5,64,128]{2,1,0:T(8,128)S(1)}, u32[]{:S(2)}, u32[]{:S(2)}) %collective-permute-start.24) | collective-permute-done | bytes 163872 | tf_op jit(solution)/shard_map/ppermute | solution.py:25
  92.4 10.2 %collective-permute-start.29 = (f32[5,64,128]{2,1,0:T(8,128)S(1)}, f32[5,64,128]{2,1,0:T(8,128)S(1)}, u32[]{:S(2)}, u32[]{:S(2)}) collective-permute-start(f32[5,64,128]{2,1,0:T(8,128)S(1)} %get-tuple-element.50), channel_id=1, source_target_pairs={{0,8},{1,9},{2,10},{3,11},{4,12},{5,13},{6,14},{7,15},{8,0},{9,1},... | collective-permute-start | bytes 491528 | tf_op jit(solution)/shard_map/ppermute | solution.py:25
  102.7 5.0 %collective-permute-done.29 = f32[5,64,128]{2,1,0:T(8,128)S(1)} collective-permute-done((f32[5,64,128]{2,1,0:T(8,128)S(1)}, f32[5,64,128]{2,1,0:T(8,128)S(1)}, u32[]{:S(2)}, u32[]{:S(2)}) %collective-permute-start.29) | collective-permute-done | bytes 163872 | tf_op jit(solution)/shard_map/ppermute | solution.py:25
  107.7 2.0 %collective-permute-done.25 = f32[5,64,128]{2,1,0:T(8,128)S(1)} collective-permute-done((f32[5,64,128]{2,1,0:T(8,128)S(1)}, f32[5,64,128]{2,1,0:T(8,128)S(1)}, u32[]{:S(2)}, u32[]{:S(2)}) %collective-permute-start.25) | collective-permute-done | bytes 163872 | tf_op jit(solution)/shard_map/ppermute | solution.py:25
  109.8 0.7 fusion.2
  110.6 1.8 %finish.1 = f32[2,256,1024]{2,1,0:T(8,128)} custom-call(f32[2,256,1024]{2,1,0:T(8,128)S(1)} %copy-done, f32[2,8,256,128]{3,2,1,0:T(8,128)S(1)} %get-tuple-element.32.num_top, f32[2,8,128,128]{3,2,1,0:T(8,128)S(1)} %collective-permute-done.20.received, f32[8,256,128]{2,1,0:T(8,128)S(1)} %density.1), custom_call_target="tpu_custom_call" | custom-call | flops 2097152 | bytes 8388608 | tf_op jit(solution)/shard_map/finish/pallas_call | solution.py:319
  (59 shorter events, 7.3 us)
Async XLA Ops:
  0.6 48.4 %copy-start.2 = (f32[16,128,128]{2,1,0:T(8,128)S(1)}, f32[16,128,128]{2,1,0:T(8,128)}, u32[]{:S(2)}) copy-start(f32[16,128,128]{2,1,0:T(8,128)} %refs_0_.1) | copy-start | bytes 3145732
  0.6 11.6 %collective-permute-start.2 = (f32[1,4,128,128]{3,2,1,0:T(8,128)}, f32[1,4,128,128]{3,2,1,0:T(8,128)}, u32[]{:S(2)}, u32[]{:S(2)}) collective-permute-start(f32[1,4,128,128]{3,2,1,0:T(8,128)} %bitcast.37), channel_id=1, source_target_pairs={{0,2},{1,3},{2,0},{3,1},{4,6},{5,7},{6,4},{7,5},{8,10},{9,11},{10,... | collective-permute-start | bytes 786440 | tf_op jit(solution)/shard_map/ppermute | solution.py:25
  3.7 13.6 %collective-permute-start.1 = (f32[1,4,128,128]{3,2,1,0:T(8,128)}, f32[1,4,128,128]{3,2,1,0:T(8,128)}, u32[]{:S(2)}, u32[]{:S(2)}) collective-permute-start(f32[1,4,128,128]{3,2,1,0:T(8,128)} %bitcast.38), channel_id=1, source_target_pairs={{0,4},{1,5},{2,6},{3,7},{4,0},{5,1},{6,2},{7,3},{8,12},{9,13},{10,... | collective-permute-start | bytes 786440 | tf_op jit(solution)/shard_map/ppermute | solution.py:25
  5.3 14.5 %collective-permute-start = (f32[1,4,128,128]{3,2,1,0:T(8,128)}, f32[1,4,128,128]{3,2,1,0:T(8,128)}, u32[]{:S(2)}, u32[]{:S(2)}) collective-permute-start(f32[1,4,128,128]{3,2,1,0:T(8,128)} %bitcast.39), channel_id=1, source_target_pairs={{0,8},{1,9},{2,10},{3,11},{4,12},{5,13},{6,14},{7,15},{8,0},{9,1},... | collective-permute-start | bytes 786440 | tf_op jit(solution)/shard_map/ppermute | solution.py:25
  7.8 43.1 %copy-start = (f32[2,256,1024]{2,1,0:T(8,128)S(1)}, f32[2,256,1024]{2,1,0:T(8,128)}, u32[]{:S(2)}) copy-start(f32[2,256,1024]{2,1,0:T(8,128)} %obj.3) | copy-start | bytes 6291460
  11.0 38.0 %collective-permute-start.4 = (f32[2,128,1024]{2,1,0:T(8,128)}, f32[2,128,1024]{2,1,0:T(8,128)}, u32[]{:S(2)}, u32[]{:S(2)}) collective-permute-start(f32[2,128,1024]{2,1,0:T(8,128)} %slice.137), channel_id=1, source_target_pairs={{1,0},{2,1},{3,2},{4,3},{5,4},{6,5},{7,6},{8,7},{9,8},{10,9},{11,1... | collective-permute-start | bytes 3145736 | tf_op jit(solution)/shard_map/ppermute | solution.py:21
  19.7 13.3 %collective-permute-start.5 = (f32[1,4,128,128]{3,2,1,0:T(8,128)}, f32[1,4,128,128]{3,2,1,0:T(8,128)}, u32[]{:S(2)}, u32[]{:S(2)}) collective-permute-start(f32[1,4,128,128]{3,2,1,0:T(8,128)} %collective-permute-done.1.rest_7_), channel_id=1, source_target_pairs={{0,2},{1,3},{2,0},{3,1},{4,6},{5,7},{6,4},{7,5},{8,10},{9,11},{10,... | collective-permute-start | bytes 786440 | tf_op jit(solution)/shard_map/ppermute | solution.py:25
  20.1 15.9 %collective-permute-start.3 = (f32[1,4,128,128]{3,2,1,0:T(8,128)}, f32[1,4,128,128]{3,2,1,0:T(8,128)}, u32[]{:S(2)}, u32[]{:S(2)}) collective-permute-start(f32[1,4,128,128]{3,2,1,0:T(8,128)} %collective-permute-done.rest_0_), channel_id=1, source_target_pairs={{0,4},{1,5},{2,6},{3,7},{4,0},{5,1},{6,2},{7,3},{8,12},{9,13},{10,... | collective-permute-start | bytes 786440 | tf_op jit(solution)/shard_map/ppermute | solution.py:25
  33.1 3.0 %collective-permute-start.6 = (f32[1,4,128,128]{3,2,1,0:T(8,128)}, f32[1,4,128,128]{3,2,1,0:T(8,128)}, u32[]{:S(2)}, u32[]{:S(2)}) collective-permute-start(f32[1,4,128,128]{3,2,1,0:T(8,128)} %collective-permute-done.5.rest_6_), channel_id=1, source_target_pairs={{0,1},{1,0},{2,3},{3,2},{4,5},{5,4},{6,7},{7,6},{8,9},{9,8},{10,11... | collective-permute-start | bytes 786440 | tf_op jit(solution)/shard_map/ppermute | solution.py:25
  33.1 6.9 %collective-permute-start.14 = (f32[1,4,128,128]{3,2,1,0:T(8,128)S(1)}, f32[1,4,128,128]{3,2,1,0:T(8,128)}, u32[]{:S(2)}, u32[]{:S(2)}) collective-permute-start(f32[1,4,128,128]{3,2,1,0:T(8,128)S(1)} %bitcast.40), channel_id=1, source_target_pairs={{0,1},{1,0},{2,3},{3,2},{4,5},{5,4},{6,7},{7,6},{8,9},{9,8},{10,11... | collective-permute-start | bytes 786440 | tf_op jit(solution)/shard_map/ppermute | solution.py:25
  33.6 9.9 %collective-permute-start.8 = (f32[1,4,128,128]{3,2,1,0:T(8,128)}, f32[1,4,128,128]{3,2,1,0:T(8,128)}, u32[]{:S(2)}, u32[]{:S(2)}) collective-permute-start(f32[1,4,128,128]{3,2,1,0:T(8,128)} %collective-permute-done.rest_0_), channel_id=1, source_target_pairs={{0,2},{1,3},{2,0},{3,1},{4,6},{5,7},{6,4},{7,5},{8,10},{9,11},{10,... | collective-permute-start | bytes 786440 | tf_op jit(solution)/shard_map/ppermute | solution.py:25
  36.1 5.7 %collective-permute-start.15 = (f32[1,4,128,128]{3,2,1,0:T(8,128)}, f32[1,4,128,128]{3,2,1,0:T(8,128)}, u32[]{:S(2)}, u32[]{:S(2)}) collective-permute-start(f32[1,4,128,128]{3,2,1,0:T(8,128)} %collective-permute-done.2.rest_5_), channel_id=1, source_target_pairs={{0,1},{1,0},{2,3},{3,2},{4,5},{5,4},{6,7},{7,6},{8,9},{9,8},{10,11... | collective-permute-start | bytes 786440 | tf_op jit(solution)/shard_map/ppermute | solution.py:25
  36.1 12.4 %collective-permute-start.9 = (f32[1,4,128,128]{3,2,1,0:T(8,128)}, f32[1,4,128,128]{3,2,1,0:T(8,128)}, u32[]{:S(2)}, u32[]{:S(2)}) collective-permute-start(f32[1,4,128,128]{3,2,1,0:T(8,128)} %collective-permute-done.3.rest_3_), channel_id=1, source_target_pairs={{0,2},{1,3},{2,0},{3,1},{4,6},{5,7},{6,4},{7,5},{8,10},{9,11},{10,... | collective-permute-start | bytes 786440 | tf_op jit(solution)/shard_map/ppermute | solution.py:25
  40.0 8.5 %collective-permute-start.7 = (s32[64]{0:T(128)S(1)}, s32[64]{0:T(128)S(1)}, u32[]{:S(2)}, u32[]{:S(2)}) collective-permute-start(s32[64]{0:T(128)S(1)} %reshape.39.meta), channel_id=1, source_target_pairs={{0,1},{1,2},{2,3},{3,4},{4,5},{5,6},{6,7},{7,8},{8,9},{9,10},{10,1... | collective-permute-start | bytes 776 | tf_op jit(solution)/shard_map/ppermute | solution.py:21
  41.8 8.5 %collective-permute-start.16 = (f32[1,4,128,128]{3,2,1,0:T(8,128)}, f32[1,4,128,128]{3,2,1,0:T(8,128)S(1)}, u32[]{:S(2)}, u32[]{:S(2)}) collective-permute-start(f32[1,4,128,128]{3,2,1,0:T(8,128)} %collective-permute-done.1.rest_7_), channel_id=1, source_target_pairs={{0,1},{1,0},{2,3},{3,2},{4,5},{5,4},{6,7},{7,6},{8,9},{9,8},{10,11... | collective-permute-start | bytes 786440 | tf_op jit(solution)/shard_map/ppermute | solution.py:25
  43.5 6.8 %collective-permute-start.10 = (f32[1,4,128,128]{3,2,1,0:T(8,128)}, f32[1,4,128,128]{3,2,1,0:T(8,128)S(1)}, u32[]{:S(2)}, u32[]{:S(2)}) collective-permute-start(f32[1,4,128,128]{3,2,1,0:T(8,128)} %collective-permute-done.rest_0_), channel_id=1, source_target_pairs={{0,1},{1,0},{2,3},{3,2},{4,5},{5,4},{6,7},{7,6},{8,9},{9,8},{10,11... | collective-permute-start | bytes 786440 | tf_op jit(solution)/shard_map/ppermute | solution.py:25
  48.5 2.1 %collective-permute-start.13 = (f32[1,4,128,128]{3,2,1,0:T(8,128)}, f32[1,4,128,128]{3,2,1,0:T(8,128)S(1)}, u32[]{:S(2)}, u32[]{:S(2)}) collective-permute-start(f32[1,4,128,128]{3,2,1,0:T(8,128)} %collective-permute-done.3.rest_3_), channel_id=1, source_target_pairs={{0,1},{1,0},{2,3},{3,2},{4,5},{5,4},{6,7},{7,6},{8,9},{9,8},{10,11... | collective-permute-start | bytes 786440 | tf_op jit(solution)/shard_map/ppermute | solution.py:25
  48.5 2.1 %collective-permute-start.11 = (f32[1,4,128,128]{3,2,1,0:T(8,128)}, f32[1,4,128,128]{3,2,1,0:T(8,128)S(1)}, u32[]{:S(2)}, u32[]{:S(2)}) collective-permute-start(f32[1,4,128,128]{3,2,1,0:T(8,128)} %collective-permute-done.8.rest_1_), channel_id=1, source_target_pairs={{0,1},{1,0},{2,3},{3,2},{4,5},{5,4},{6,7},{7,6},{8,9},{9,8},{10,11... | collective-permute-start | bytes 786440 | tf_op jit(solution)/shard_map/ppermute | solution.py:25
  49.0 2.0 %collective-permute-start.12 = (f32[1,4,128,128]{3,2,1,0:T(8,128)}, f32[1,4,128,128]{3,2,1,0:T(8,128)S(1)}, u32[]{:S(2)}, u32[]{:S(2)}) collective-permute-start(f32[1,4,128,128]{3,2,1,0:T(8,128)} %collective-permute-done.9.rest_2_), channel_id=1, source_target_pairs={{0,1},{1,0},{2,3},{3,2},{4,5},{5,4},{6,7},{7,6},{8,9},{9,8},{10,11... | collective-permute-start | bytes 786440 | tf_op jit(solution)/shard_map/ppermute | solution.py:25
  63.1 3.1 %collective-permute-start.17 = (f32[4,5,128,128]{3,2,1,0:T(8,128)S(1)}, f32[4,5,128,128]{3,2,1,0:T(8,128)S(1)}, u32[]{:S(2)}, u32[]{:S(2)}) collective-permute-start(f32[4,5,128,128]{3,2,1,0:T(8,128)S(1)} %get-tuple-element.35), channel_id=1, source_target_pairs={{0,1},{1,0},{2,3},{3,2},{4,5},{5,4},{6,7},{7,6},{8,9},{9,8},{10,11... | collective-permute-start | bytes 3932168 | tf_op jit(solution)/shard_map/ppermute | solution.py:25
  63.2 7.9 %collective-permute-start.21 = (f32[4,5,128,128]{3,2,1,0:T(8,128)S(1)}, f32[4,5,128,128]{3,2,1,0:T(8,128)S(1)}, u32[]{:S(2)}, u32[]{:S(2)}) collective-permute-start(f32[4,5,128,128]{3,2,1,0:T(8,128)S(1)} %get-tuple-element.40), channel_id=1, source_target_pairs={{0,1},{1,0},{2,3},{3,2},{4,5},{5,4},{6,7},{7,6},{8,9},{9,8},{10,11... | collective-permute-start | bytes 3932168 | tf_op jit(solution)/shard_map/ppermute | solution.py:25
  66.4 13.2 %collective-permute-start.18 = (f32[2,5,64,128]{3,2,1,0:T(8,128)S(1)}, f32[2,5,64,128]{3,2,1,0:T(8,128)S(1)}, u32[]{:S(2)}, u32[]{:S(2)}) collective-permute-start(f32[2,5,64,128]{3,2,1,0:T(8,128)S(1)} %pad_maximum_fusion), channel_id=1, source_target_pairs={{0,2},{1,3},{2,0},{3,1},{4,6},{5,7},{6,4},{7,5},{8,10},{9,11},{10,... | collective-permute-start | bytes 983048 | tf_op jit(solution)/shard_map/ppermute | solution.py:25
  71.1 10.7 %collective-permute-start.19 = (f32[2,5,64,128]{3,2,1,0:T(8,128)S(1)}, f32[2,5,64,128]{3,2,1,0:T(8,128)S(1)}, u32[]{:S(2)}, u32[]{:S(2)}) collective-permute-start(f32[2,5,64,128]{3,2,1,0:T(8,128)S(1)} %pad_maximum_fusion.1), channel_id=1, source_target_pairs={{0,4},{1,5},{2,6},{3,7},{4,0},{5,1},{6,2},{7,3},{8,12},{9,13},{10,... | collective-permute-start | bytes 983048 | tf_op jit(solution)/shard_map/ppermute | solution.py:25
  71.3 15.3 %collective-permute-start.22 = (f32[2,5,64,128]{3,2,1,0:T(8,128)S(1)}, f32[2,5,64,128]{3,2,1,0:T(8,128)S(1)}, u32[]{:S(2)}, u32[]{:S(2)}) collective-permute-start(f32[2,5,64,128]{3,2,1,0:T(8,128)S(1)} %pad_maximum_fusion.2), channel_id=1, source_target_pairs={{0,2},{1,3},{2,0},{3,1},{4,6},{5,7},{6,4},{7,5},{8,10},{9,11},{10,... | collective-permute-start | bytes 983048 | tf_op jit(solution)/shard_map/ppermute | solution.py:25
  72.9 15.8 %collective-permute-start.26 = (f32[2,5,64,128]{3,2,1,0:T(8,128)S(1)}, f32[2,5,64,128]{3,2,1,0:T(8,128)S(1)}, u32[]{:S(2)}, u32[]{:S(2)}) collective-permute-start(f32[2,5,64,128]{3,2,1,0:T(8,128)S(1)} %pad_maximum_fusion.3), channel_id=1, source_target_pairs={{0,4},{1,5},{2,6},{3,7},{4,0},{5,1},{6,2},{7,3},{8,12},{9,13},{10,... | collective-permute-start | bytes 983048 | tf_op jit(solution)/shard_map/ppermute | solution.py:25
  81.8 10.5 %collective-permute-start.24 = (f32[5,64,128]{2,1,0:T(8,128)S(1)}, f32[5,64,128]{2,1,0:T(8,128)S(1)}, u32[]{:S(2)}, u32[]{:S(2)}) collective-permute-start(f32[5,64,128]{2,1,0:T(8,128)S(1)} %get-tuple-element.41), channel_id=1, source_target_pairs={{0,4},{1,5},{2,6},{3,7},{4,0},{5,1},{6,2},{7,3},{8,12},{9,13},{10,... | collective-permute-start | bytes 491528 | tf_op jit(solution)/shard_map/ppermute | solution.py:25
  81.9 10.4 %collective-permute-start.28 = (f32[5,64,128]{2,1,0:T(8,128)S(1)}, f32[5,64,128]{2,1,0:T(8,128)S(1)}, u32[]{:S(2)}, u32[]{:S(2)}) collective-permute-start(f32[5,64,128]{2,1,0:T(8,128)S(1)} %get-tuple-element.52), channel_id=1, source_target_pairs={{0,2},{1,3},{2,0},{3,1},{4,6},{5,7},{6,4},{7,5},{8,10},{9,11},{10,... | collective-permute-start | bytes 491528 | tf_op jit(solution)/shard_map/ppermute | solution.py:25
  82.3 28.3 %collective-permute-start.20 = (f32[2,8,128,128]{3,2,1,0:T(8,128)S(1)}, f32[2,8,128,128]{3,2,1,0:T(8,128)S(1)}, u32[]{:S(2)}, u32[]{:S(2)}) collective-permute-start(f32[2,8,128,128]{3,2,1,0:T(8,128)S(1)} %get-tuple-element.36), channel_id=1, source_target_pairs={{0,1},{1,2},{2,3},{3,4},{4,5},{5,6},{6,7},{7,8},{8,9},{9,10},{10,1... | collective-permute-start | bytes 3145736 | tf_op jit(solution)/shard_map/ppermute | solution.py:21
  88.8 13.9 %collective-permute-start.27 = (f32[5,64,128]{2,1,0:T(8,128)S(1)}, f32[5,64,128]{2,1,0:T(8,128)S(1)}, u32[]{:S(2)}, u32[]{:S(2)}) collective-permute-start(f32[5,64,128]{2,1,0:T(8,128)S(1)} %get-tuple-element.44), channel_id=1, source_target_pairs={{0,2},{1,3},{2,0},{3,1},{4,6},{5,7},{6,4},{7,5},{8,10},{9,11},{10,... | collective-permute-start | bytes 491528 | tf_op jit(solution)/shard_map/ppermute | solution.py:25
  88.9 13.8 %collective-permute-start.23 = (f32[5,64,128]{2,1,0:T(8,128)S(1)}, f32[5,64,128]{2,1,0:T(8,128)S(1)}, u32[]{:S(2)}, u32[]{:S(2)}) collective-permute-start(f32[5,64,128]{2,1,0:T(8,128)S(1)} %get-tuple-element.45), channel_id=1, source_target_pairs={{0,4},{1,5},{2,6},{3,7},{4,0},{5,1},{6,2},{7,3},{8,12},{9,13},{10,... | collective-permute-start | bytes 491528 | tf_op jit(solution)/shard_map/ppermute | solution.py:25
  92.4 15.3 %collective-permute-start.29 = (f32[5,64,128]{2,1,0:T(8,128)S(1)}, f32[5,64,128]{2,1,0:T(8,128)S(1)}, u32[]{:S(2)}, u32[]{:S(2)}) collective-permute-start(f32[5,64,128]{2,1,0:T(8,128)S(1)} %get-tuple-element.50), channel_id=1, source_target_pairs={{0,8},{1,9},{2,10},{3,11},{4,12},{5,13},{6,14},{7,15},{8,0},{9,1},... | collective-permute-start | bytes 491528 | tf_op jit(solution)/shard_map/ppermute | solution.py:25
  102.6 7.1 %collective-permute-start.25 = (f32[5,64,128]{2,1,0:T(8,128)S(1)}, f32[5,64,128]{2,1,0:T(8,128)S(1)}, u32[]{:S(2)}, u32[]{:S(2)}) collective-permute-start(f32[5,64,128]{2,1,0:T(8,128)S(1)} %get-tuple-element.51), channel_id=1, source_target_pairs={{0,8},{1,9},{2,10},{3,11},{4,12},{5,13},{6,14},{7,15},{8,0},{9,1},... | collective-permute-start | bytes 491528 | tf_op jit(solution)/shard_map/ppermute | solution.py:25
  (2 other events, 33.5 us)

commit v5 on v4

--- a/solution.py
+++ b/solution.py
@@ -12,7 +12,7 @@
 damping = 1.0
 floor_level = 0.3
 LANES = 128
-SLOTS_AT_ONCE = 4
+SLOTS_AT_ONCE = 8
 VMEM_BYTES = 26 * 1024 * 1024
 
 
@@ -369,10 +369,10 @@
         for key in (8, 4, 2):
             held[key] = swapped(own_probe, key)
         held[8], held[4], held[2] = lax.optimization_barrier((held[8], held[4], held[2]))
-        held[6] = swapped(held[4], 2)
+        held[6] = swapped(held[2], 4)
         held[12] = swapped(held[8], 4)
         held[10] = swapped(held[8], 2)
-        held[14] = swapped(held[12], 2)
+        held[14] = swapped(held[10], 4)
         for key in list(held):
             held[key | 1] = swapped(held[key], 1)
         order = [key | core for core in (0, 1) for key in FAR + NEAR]

time: 115 us -> 114 us (level)
  Pallas kernels: 16.3 us -> 18.4 us
    pallas_call x1, Pallas kernels: 12.2 us -> 14.4 us  [update(): pl.pallas_call(functools.partial(update_kernel, (piece_sizes, group_sizes...]
    ppermute x27, starting transfers between devices: 32.8 us -> 31.5 us  [swapped(): lax.ppermute(block, 'row', [(i, i ^ mask) for i in range(lax.axis_size('r...]
  transfers between devices with their start and end apart: 30 -> 30, of which waited for: 15 -> 18; matrix products, arithmetic and copies ran while one was open for 5% -> 5% of each run, Pallas kernels for 2% -> 2%
where the time goes in v5:
time: 114 us; the launch traced here: 112 us
  waiting for transfers between devices  49.1 us (43%)
  starting transfers between devices  36.2 us (32%)
  Pallas kernels  18.4 us (16%)
  local copies, waits for them, and re-layouts  3.68 us (3%)
  other arithmetic  3.54 us (3%)
  between operations  1.48 us (1%)
    ppermute x27, waiting for transfers between devices, swapped(): lax.ppermute(block, 'row', [(i, i ^ mask) for i in range(lax.axis_size('r...  49.1 us
    ppermute x27, starting transfers between devices, swapped(): lax.ppermute(block, 'row', [(i, i ^ mask) for i in range(lax.axis_size('r...  31.5 us
    pallas_call x1, Pallas kernels, update(): pl.pallas_call(functools.partial(update_kernel, (piece_sizes, group_sizes...  14.4 us
    ppermute x3, starting transfers between devices, moved(): lax.ppermute(block, 'row', [(i, i + distance) for i in range(size) if 0 <...  4.7 us
    slice x1, local copies, waits for them, and re-layouts, local(): rim = moved(after(object_strip[:, :points, :], slot_of), -1)  2.46 us
  transfers between devices with their start and end apart: 30, of which 18 were waited for; matrix products, arithmetic and copies ran while one was open for 5% of the time, Pallas kernels for 2%

profile of v5, /device:TPU:0, one launch (start us, length us, event | category | flops | bytes accessed | tf_op | source)
XLA Modules:
  0.0 112.4 jit_solution(6005728705825741614)
XLA Ops:
  0.6 3.0 %collective-permute-start.2 = (f32[1,4,128,128]{3,2,1,0:T(8,128)}, f32[1,4,128,128]{3,2,1,0:T(8,128)}, u32[]{:S(2)}, u32[]{:S(2)}) collective-permute-start(f32[1,4,128,128]{3,2,1,0:T(8,128)} %bitcast.37), channel_id=1, source_target_pairs={{0,2},{1,3},{2,0},{3,1},{4,6},{5,7},{6,4},{7,5},{8,10},{9,11},{10,... | collective-permute-start | bytes 786440 | tf_op jit(solution)/shard_map/ppermute | solution.py:25
  3.7 1.6 %collective-permute-start.1 = (f32[1,4,128,128]{3,2,1,0:T(8,128)}, f32[1,4,128,128]{3,2,1,0:T(8,128)}, u32[]{:S(2)}, u32[]{:S(2)}) collective-permute-start(f32[1,4,128,128]{3,2,1,0:T(8,128)} %bitcast.38), channel_id=1, source_target_pairs={{0,4},{1,5},{2,6},{3,7},{4,0},{5,1},{6,2},{7,3},{8,12},{9,13},{10,... | collective-permute-start | bytes 786440 | tf_op jit(solution)/shard_map/ppermute | solution.py:25
  5.3 2.6 %collective-permute-start = (f32[1,4,128,128]{3,2,1,0:T(8,128)}, f32[1,4,128,128]{3,2,1,0:T(8,128)}, u32[]{:S(2)}, u32[]{:S(2)}) collective-permute-start(f32[1,4,128,128]{3,2,1,0:T(8,128)} %bitcast.39), channel_id=1, source_target_pairs={{0,8},{1,9},{2,10},{3,11},{4,12},{5,13},{6,14},{7,15},{8,0},{9,1},... | collective-permute-start | bytes 786440 | tf_op jit(solution)/shard_map/ppermute | solution.py:25
  7.9 2.5 %slice.137 = f32[2,128,1024]{2,1,0:T(8,128)} slice(f32[2,256,1024]{2,1,0:T(8,128)} %obj.3), slice={[0:2], [0:128], [0:1024]} | slice | bytes 2097152 | tf_op jit(solution)/shard_map/slice | solution.py:392
  10.3 0.7 fusion.22.slot_of
  11.0 1.3 %collective-permute-start.4 = (f32[2,128,1024]{2,1,0:T(8,128)}, f32[2,128,1024]{2,1,0:T(8,128)}, u32[]{:S(2)}, u32[]{:S(2)}) collective-permute-start(f32[2,128,1024]{2,1,0:T(8,128)} %slice.137), channel_id=1, source_target_pairs={{1,0},{2,1},{3,2},{4,3},{5,4},{6,5},{7,6},{8,7},{9,8},{10,9},{11,1... | collective-permute-start | bytes 3145736 | tf_op jit(solution)/shard_map/ppermute | solution.py:21
  12.3 5.0 %collective-permute-done.1.rest_7_ = f32[1,4,128,128]{3,2,1,0:T(8,128)} collective-permute-done((f32[1,4,128,128]{3,2,1,0:T(8,128)}, f32[1,4,128,128]{3,2,1,0:T(8,128)}, u32[]{:S(2)}, u32[]{:S(2)}) %collective-permute-start.1) | collective-permute-done | bytes 262176 | tf_op jit(solution)/shard_map/ppermute | solution.py:25
  17.3 2.5 %collective-permute-done.rest_0_ = f32[1,4,128,128]{3,2,1,0:T(8,128)} collective-permute-done((f32[1,4,128,128]{3,2,1,0:T(8,128)}, f32[1,4,128,128]{3,2,1,0:T(8,128)}, u32[]{:S(2)}, u32[]{:S(2)}) %collective-permute-start) | collective-permute-done | bytes 262176 | tf_op jit(solution)/shard_map/ppermute | solution.py:25
  20.6 13.7 %collective-permute-done.5.rest_6_ = f32[1,4,128,128]{3,2,1,0:T(8,128)} collective-permute-done((f32[1,4,128,128]{3,2,1,0:T(8,128)}, f32[1,4,128,128]{3,2,1,0:T(8,128)}, u32[]{:S(2)}, u32[]{:S(2)}) %collective-permute-start.5) | collective-permute-done | bytes 262176 | tf_op jit(solution)/shard_map/ppermute | solution.py:25
  34.9 1.6 %collective-permute-done.6.rest_14_ = f32[1,4,128,128]{3,2,1,0:T(8,128)} collective-permute-done((f32[1,4,128,128]{3,2,1,0:T(8,128)}, f32[1,4,128,128]{3,2,1,0:T(8,128)}, u32[]{:S(2)}, u32[]{:S(2)}) %collective-permute-start.6) | collective-permute-done | bytes 262176 | tf_op jit(solution)/shard_map/ppermute | solution.py:25
  36.9 0.8 slice_subtract_fusion
  39.2 2.1 %collective-permute-start.7 = (s32[64]{0:T(128)S(1)}, s32[64]{0:T(128)S(1)}, u32[]{:S(2)}, u32[]{:S(2)}) collective-permute-start(s32[64]{0:T(128)S(1)} %reshape.39.meta), channel_id=1, source_target_pairs={{0,1},{1,2},{2,3},{3,4},{4,5},{5,6},{6,7},{7,8},{8,9},{9,10},{10,1... | collective-permute-start | bytes 776 | tf_op jit(solution)/shard_map/ppermute | solution.py:21
  41.3 1.7 %collective-permute-start.15 = (f32[1,4,128,128]{3,2,1,0:T(8,128)}, f32[1,4,128,128]{3,2,1,0:T(8,128)S(1)}, u32[]{:S(2)}, u32[]{:S(2)}) collective-permute-start(f32[1,4,128,128]{3,2,1,0:T(8,128)} %collective-permute-done.2.rest_5_), channel_id=1, source_target_pairs={{0,1},{1,0},{2,3},{3,2},{4,5},{5,4},{6,7},{7,6},{8,9},{9,8},{10,11... | collective-permute-start | bytes 786440 | tf_op jit(solution)/shard_map/ppermute | solution.py:25
  42.9 1.4 %collective-permute-done.3.rest_3_ = f32[1,4,128,128]{3,2,1,0:T(8,128)} collective-permute-done((f32[1,4,128,128]{3,2,1,0:T(8,128)}, f32[1,4,128,128]{3,2,1,0:T(8,128)}, u32[]{:S(2)}, u32[]{:S(2)}) %collective-permute-start.3) | collective-permute-done | bytes 262176 | tf_op jit(solution)/shard_map/ppermute | solution.py:25
  44.3 4.7 %collective-permute-done.9.rest_2_ = f32[1,4,128,128]{3,2,1,0:T(8,128)} collective-permute-done((f32[1,4,128,128]{3,2,1,0:T(8,128)}, f32[1,4,128,128]{3,2,1,0:T(8,128)}, u32[]{:S(2)}, u32[]{:S(2)}) %collective-permute-start.9) | collective-permute-done | bytes 262176 | tf_op jit(solution)/shard_map/ppermute | solution.py:25
  49.5 1.0 copy-done.3
  51.4 14.4 %update.1 = (f32[2,8,256,128]{3,2,1,0:T(8,128)S(1)}, f32[2,8,128,128]{3,2,1,0:T(8,128)S(1)}, f32[8,128,128]{2,1,0:T(8,128)S(1)}, f32[4,5,128,128]{3,2,1,0:T(8,12...) custom-call(s32[64]{0:T(128)S(1)} %reshape.39.meta, ...), custom_call_target="tpu_custom_call" | custom-call | flops 6000000000 | bytes 16777216 | tf_op jit(solution)/shard_map/update/pallas_call | solution.py:232
  66.5 2.5 %collective-permute-done.17 = f32[4,5,128,128]{3,2,1,0:T(8,128)S(1)} collective-permute-done((f32[4,5,128,128]{3,2,1,0:T(8,128)S(1)}, f32[4,5,128,128]{3,2,1,0:T(8,128)S(1)}, u32[]{:S(2)}, u32[]{:S(2)}) %collective-permute-start.17) | collective-permute-done | bytes 1310752 | tf_op jit(solution)/shard_map/ppermute | solution.py:25
  69.4 1.4 %collective-permute-done.21 = f32[4,5,128,128]{3,2,1,0:T(8,128)S(1)} collective-permute-done((f32[4,5,128,128]{3,2,1,0:T(8,128)S(1)}, f32[4,5,128,128]{3,2,1,0:T(8,128)S(1)}, u32[]{:S(2)}, u32[]{:S(2)}) %collective-permute-start.21) | collective-permute-done | bytes 1310752 | tf_op jit(solution)/shard_map/ppermute | solution.py:25
  71.7 2.0 %collective-permute-start.26 = (f32[2,5,64,128]{3,2,1,0:T(8,128)S(1)}, f32[2,5,64,128]{3,2,1,0:T(8,128)S(1)}, u32[]{:S(2)}, u32[]{:S(2)}) collective-permute-start(f32[2,5,64,128]{3,2,1,0:T(8,128)S(1)} %pad_maximum_fusion.3), channel_id=1, source_target_pairs={{0,4},{1,5},{2,6},{3,7},{4,0},{5,1},{6,2},{7,3},{8,12},{9,13},{10,... | collective-permute-start | bytes 983048 | tf_op jit(solution)/shard_map/ppermute | solution.py:25
  73.6 2.0 %density.1 = f32[8,256,128]{2,1,0:T(8,128)S(1)} custom-call(s32[64]{0:T(128)S(1)} %reshape.39.meta, s32[64]{0:T(128)S(1)} %collective-permute-done.7.above, f32[8,128,128]{2,1,0:T(8,128)S(1)} %get-tuple-element.37.squares), custom_call_target="tpu_custom_call" | custom-call | flops 8388608 | bytes 8388608 | tf_op jit(solution)/shard_map/density/pallas_call | solution.py:294
  75.6 4.1 %collective-permute-done.18 = f32[2,5,64,128]{3,2,1,0:T(8,128)S(1)} collective-permute-done((f32[2,5,64,128]{3,2,1,0:T(8,128)S(1)}, f32[2,5,64,128]{3,2,1,0:T(8,128)S(1)}, u32[]{:S(2)}, u32[]{:S(2)}) %collective-permute-start.18) | collective-permute-done | bytes 327712 | tf_op jit(solution)/shard_map/ppermute | solution.py:25
  80.1 2.0 %collective-permute-start.28 = (f32[5,64,128]{2,1,0:T(8,128)S(1)}, f32[5,64,128]{2,1,0:T(8,128)S(1)}, u32[]{:S(2)}, u32[]{:S(2)}) collective-permute-start(f32[5,64,128]{2,1,0:T(8,128)S(1)} %get-tuple-element.52), channel_id=1, source_target_pairs={{0,2},{1,3},{2,0},{3,1},{4,6},{5,7},{6,4},{7,5},{8,10},{9,11},{10,... | collective-permute-start | bytes 491528 | tf_op jit(solution)/shard_map/ppermute | solution.py:25
  82.2 1.3 %collective-permute-start.20 = (f32[2,8,128,128]{3,2,1,0:T(8,128)S(1)}, f32[2,8,128,128]{3,2,1,0:T(8,128)S(1)}, u32[]{:S(2)}, u32[]{:S(2)}) collective-permute-start(f32[2,8,128,128]{3,2,1,0:T(8,128)S(1)} %get-tuple-element.36), channel_id=1, source_target_pairs={{0,1},{1,2},{2,3},{3,4},{4,5},{5,6},{6,7},{7,8},{8,9},{9,10},{10,1... | collective-permute-start | bytes 3145736 | tf_op jit(solution)/shard_map/ppermute | solution.py:21
  83.5 3.2 %collective-permute-done.22 = f32[2,5,64,128]{3,2,1,0:T(8,128)S(1)} collective-permute-done((f32[2,5,64,128]{3,2,1,0:T(8,128)S(1)}, f32[2,5,64,128]{3,2,1,0:T(8,128)S(1)}, u32[]{:S(2)}, u32[]{:S(2)}) %collective-permute-start.22) | collective-permute-done | bytes 327712 | tf_op jit(solution)/shard_map/ppermute | solution.py:25
  86.9 2.1 %collective-permute-start.27 = (f32[5,64,128]{2,1,0:T(8,128)S(1)}, f32[5,64,128]{2,1,0:T(8,128)S(1)}, u32[]{:S(2)}, u32[]{:S(2)}) collective-permute-start(f32[5,64,128]{2,1,0:T(8,128)S(1)} %get-tuple-element.44), channel_id=1, source_target_pairs={{0,2},{1,3},{2,0},{3,1},{4,6},{5,7},{6,4},{7,5},{8,10},{9,11},{10,... | collective-permute-start | bytes 491528 | tf_op jit(solution)/shard_map/ppermute | solution.py:25
  89.6 0.7 collective-permute-done.28
  90.4 12.2 %collective-permute-start.29 = (f32[5,64,128]{2,1,0:T(8,128)S(1)}, f32[5,64,128]{2,1,0:T(8,128)S(1)}, u32[]{:S(2)}, u32[]{:S(2)}) collective-permute-start(f32[5,64,128]{2,1,0:T(8,128)S(1)} %get-tuple-element.50), channel_id=1, source_target_pairs={{0,8},{1,9},{2,10},{3,11},{4,12},{5,13},{6,14},{7,15},{8,0},{9,1},... | collective-permute-start | bytes 491528 | tf_op jit(solution)/shard_map/ppermute | solution.py:25
  102.7 5.0 %collective-permute-done.29 = f32[5,64,128]{2,1,0:T(8,128)S(1)} collective-permute-done((f32[5,64,128]{2,1,0:T(8,128)S(1)}, f32[5,64,128]{2,1,0:T(8,128)S(1)}, u32[]{:S(2)}, u32[]{:S(2)}) %collective-permute-start.29) | collective-permute-done | bytes 163872 | tf_op jit(solution)/shard_map/ppermute | solution.py:25
  107.7 2.0 %collective-permute-done.25 = f32[5,64,128]{2,1,0:T(8,128)S(1)} collective-permute-done((f32[5,64,128]{2,1,0:T(8,128)S(1)}, f32[5,64,128]{2,1,0:T(8,128)S(1)}, u32[]{:S(2)}, u32[]{:S(2)}) %collective-permute-start.25) | collective-permute-done | bytes 163872 | tf_op jit(solution)/shard_map/ppermute | solution.py:25
  109.9 0.7 fusion.2
  110.6 1.8 %finish.1 = f32[2,256,1024]{2,1,0:T(8,128)} custom-call(f32[2,256,1024]{2,1,0:T(8,128)S(1)} %copy-done, f32[2,8,256,128]{3,2,1,0:T(8,128)S(1)} %get-tuple-element.32.num_top, f32[2,8,128,128]{3,2,1,0:T(8,128)S(1)} %collective-permute-done.20.received, f32[8,256,128]{2,1,0:T(8,128)S(1)} %density.1), custom_call_target="tpu_custom_call" | custom-call | flops 2097152 | bytes 8388608 | tf_op jit(solution)/shard_map/finish/pallas_call | solution.py:319
  (59 shorter events, 7.3 us)
Async XLA Ops:
  0.6 48.9 %copy-start.2 = (f32[16,128,128]{2,1,0:T(8,128)S(1)}, f32[16,128,128]{2,1,0:T(8,128)}, u32[]{:S(2)}) copy-start(f32[16,128,128]{2,1,0:T(8,128)} %refs_0_.1) | copy-start | bytes 3145732
  0.6 11.6 %collective-permute-start.2 = (f32[1,4,128,128]{3,2,1,0:T(8,128)}, f32[1,4,128,128]{3,2,1,0:T(8,128)}, u32[]{:S(2)}, u32[]{:S(2)}) collective-permute-start(f32[1,4,128,128]{3,2,1,0:T(8,128)} %bitcast.37), channel_id=1, source_target_pairs={{0,2},{1,3},{2,0},{3,1},{4,6},{5,7},{6,4},{7,5},{8,10},{9,11},{10,... | collective-permute-start | bytes 786440 | tf_op jit(solution)/shard_map/ppermute | solution.py:25
  3.7 13.6 %collective-permute-start.1 = (f32[1,4,128,128]{3,2,1,0:T(8,128)}, f32[1,4,128,128]{3,2,1,0:T(8,128)}, u32[]{:S(2)}, u32[]{:S(2)}) collective-permute-start(f32[1,4,128,128]{3,2,1,0:T(8,128)} %bitcast.38), channel_id=1, source_target_pairs={{0,4},{1,5},{2,6},{3,7},{4,0},{5,1},{6,2},{7,3},{8,12},{9,13},{10,... | collective-permute-start | bytes 786440 | tf_op jit(solution)/shard_map/ppermute | solution.py:25
  5.3 14.5 %collective-permute-start = (f32[1,4,128,128]{3,2,1,0:T(8,128)}, f32[1,4,128,128]{3,2,1,0:T(8,128)}, u32[]{:S(2)}, u32[]{:S(2)}) collective-permute-start(f32[1,4,128,128]{3,2,1,0:T(8,128)} %bitcast.39), channel_id=1, source_target_pairs={{0,8},{1,9},{2,10},{3,11},{4,12},{5,13},{6,14},{7,15},{8,0},{9,1},... | collective-permute-start | bytes 786440 | tf_op jit(solution)/shard_map/ppermute | solution.py:25
  7.8 43.6 %copy-start = (f32[2,256,1024]{2,1,0:T(8,128)S(1)}, f32[2,256,1024]{2,1,0:T(8,128)}, u32[]{:S(2)}) copy-start(f32[2,256,1024]{2,1,0:T(8,128)} %obj.3) | copy-start | bytes 6291460
  11.0 38.5 %collective-permute-start.4 = (f32[2,128,1024]{2,1,0:T(8,128)}, f32[2,128,1024]{2,1,0:T(8,128)}, u32[]{:S(2)}, u32[]{:S(2)}) collective-permute-start(f32[2,128,1024]{2,1,0:T(8,128)} %slice.137), channel_id=1, source_target_pairs={{1,0},{2,1},{3,2},{4,3},{5,4},{6,5},{7,6},{8,7},{9,8},{10,9},{11,1... | collective-permute-start | bytes 3145736 | tf_op jit(solution)/shard_map/ppermute | solution.py:21
  19.7 14.5 %collective-permute-start.5 = (f32[1,4,128,128]{3,2,1,0:T(8,128)}, f32[1,4,128,128]{3,2,1,0:T(8,128)}, u32[]{:S(2)}, u32[]{:S(2)}) collective-permute-start(f32[1,4,128,128]{3,2,1,0:T(8,128)} %collective-permute-done.2.rest_5_), channel_id=1, source_target_pairs={{0,4},{1,5},{2,6},{3,7},{4,0},{5,1},{6,2},{7,3},{8,12},{9,13},{10,... | collective-permute-start | bytes 786440 | tf_op jit(solution)/shard_map/ppermute | solution.py:25
  20.1 14.7 %collective-permute-start.8 = (f32[1,4,128,128]{3,2,1,0:T(8,128)}, f32[1,4,128,128]{3,2,1,0:T(8,128)}, u32[]{:S(2)}, u32[]{:S(2)}) collective-permute-start(f32[1,4,128,128]{3,2,1,0:T(8,128)} %collective-permute-done.rest_0_), channel_id=1, source_target_pairs={{0,2},{1,3},{2,0},{3,1},{4,6},{5,7},{6,4},{7,5},{8,10},{9,11},{10,... | collective-permute-start | bytes 786440 | tf_op jit(solution)/shard_map/ppermute | solution.py:25
  34.3 2.2 %collective-permute-start.6 = (f32[1,4,128,128]{3,2,1,0:T(8,128)}, f32[1,4,128,128]{3,2,1,0:T(8,128)}, u32[]{:S(2)}, u32[]{:S(2)}) collective-permute-start(f32[1,4,128,128]{3,2,1,0:T(8,128)} %collective-permute-done.5.rest_6_), channel_id=1, source_target_pairs={{0,1},{1,0},{2,3},{3,2},{4,5},{5,4},{6,7},{7,6},{8,9},{9,8},{10,11... | collective-permute-start | bytes 786440 | tf_op jit(solution)/shard_map/ppermute | solution.py:25
  34.3 4.9 %collective-permute-start.14 = (f32[1,4,128,128]{3,2,1,0:T(8,128)S(1)}, f32[1,4,128,128]{3,2,1,0:T(8,128)}, u32[]{:S(2)}, u32[]{:S(2)}) collective-permute-start(f32[1,4,128,128]{3,2,1,0:T(8,128)S(1)} %bitcast.40), channel_id=1, source_target_pairs={{0,1},{1,0},{2,3},{3,2},{4,5},{5,4},{6,7},{7,6},{8,9},{9,8},{10,11... | collective-permute-start | bytes 786440 | tf_op jit(solution)/shard_map/ppermute | solution.py:25
  34.8 9.5 %collective-permute-start.3 = (f32[1,4,128,128]{3,2,1,0:T(8,128)}, f32[1,4,128,128]{3,2,1,0:T(8,128)}, u32[]{:S(2)}, u32[]{:S(2)}) collective-permute-start(f32[1,4,128,128]{3,2,1,0:T(8,128)} %collective-permute-done.rest_0_), channel_id=1, source_target_pairs={{0,4},{1,5},{2,6},{3,7},{4,0},{5,1},{6,2},{7,3},{8,12},{9,13},{10,... | collective-permute-start | bytes 786440 | tf_op jit(solution)/shard_map/ppermute | solution.py:25
  34.8 6.5 %collective-permute-start.16 = (f32[1,4,128,128]{3,2,1,0:T(8,128)}, f32[1,4,128,128]{3,2,1,0:T(8,128)}, u32[]{:S(2)}, u32[]{:S(2)}) collective-permute-start(f32[1,4,128,128]{3,2,1,0:T(8,128)} %collective-permute-done.1.rest_7_), channel_id=1, source_target_pairs={{0,1},{1,0},{2,3},{3,2},{4,5},{5,4},{6,7},{7,6},{8,9},{9,8},{10,11... | collective-permute-start | bytes 786440 | tf_op jit(solution)/shard_map/ppermute | solution.py:25
  36.5 12.5 %collective-permute-start.9 = (f32[1,4,128,128]{3,2,1,0:T(8,128)}, f32[1,4,128,128]{3,2,1,0:T(8,128)}, u32[]{:S(2)}, u32[]{:S(2)}) collective-permute-start(f32[1,4,128,128]{3,2,1,0:T(8,128)} %collective-permute-done.8.rest_1_), channel_id=1, source_target_pairs={{0,4},{1,5},{2,6},{3,7},{4,0},{5,1},{6,2},{7,3},{8,12},{9,13},{10,... | collective-permute-start | bytes 786440 | tf_op jit(solution)/shard_map/ppermute | solution.py:25
  39.2 9.8 %collective-permute-start.7 = (s32[64]{0:T(128)S(1)}, s32[64]{0:T(128)S(1)}, u32[]{:S(2)}, u32[]{:S(2)}) collective-permute-start(s32[64]{0:T(128)S(1)} %reshape.39.meta), channel_id=1, source_target_pairs={{0,1},{1,2},{2,3},{3,4},{4,5},{5,6},{6,7},{7,8},{8,9},{9,10},{10,1... | collective-permute-start | bytes 776 | tf_op jit(solution)/shard_map/ppermute | solution.py:21
  41.3 9.5 %collective-permute-start.15 = (f32[1,4,128,128]{3,2,1,0:T(8,128)}, f32[1,4,128,128]{3,2,1,0:T(8,128)S(1)}, u32[]{:S(2)}, u32[]{:S(2)}) collective-permute-start(f32[1,4,128,128]{3,2,1,0:T(8,128)} %collective-permute-done.2.rest_5_), channel_id=1, source_target_pairs={{0,1},{1,0},{2,3},{3,2},{4,5},{5,4},{6,7},{7,6},{8,9},{9,8},{10,11... | collective-permute-start | bytes 786440 | tf_op jit(solution)/shard_map/ppermute | solution.py:25
  44.3 6.5 %collective-permute-start.10 = (f32[1,4,128,128]{3,2,1,0:T(8,128)}, f32[1,4,128,128]{3,2,1,0:T(8,128)S(1)}, u32[]{:S(2)}, u32[]{:S(2)}) collective-permute-start(f32[1,4,128,128]{3,2,1,0:T(8,128)} %collective-permute-done.rest_0_), channel_id=1, source_target_pairs={{0,1},{1,0},{2,3},{3,2},{4,5},{5,4},{6,7},{7,6},{8,9},{9,8},{10,11... | collective-permute-start | bytes 786440 | tf_op jit(solution)/shard_map/ppermute | solution.py:25
  48.9 1.8 %collective-permute-start.11 = (f32[1,4,128,128]{3,2,1,0:T(8,128)}, f32[1,4,128,128]{3,2,1,0:T(8,128)S(1)}, u32[]{:S(2)}, u32[]{:S(2)}) collective-permute-start(f32[1,4,128,128]{3,2,1,0:T(8,128)} %collective-permute-done.8.rest_1_), channel_id=1, source_target_pairs={{0,1},{1,0},{2,3},{3,2},{4,5},{5,4},{6,7},{7,6},{8,9},{9,8},{10,11... | collective-permute-start | bytes 786440 | tf_op jit(solution)/shard_map/ppermute | solution.py:25
  48.9 2.1 %collective-permute-start.13 = (f32[1,4,128,128]{3,2,1,0:T(8,128)}, f32[1,4,128,128]{3,2,1,0:T(8,128)S(1)}, u32[]{:S(2)}, u32[]{:S(2)}) collective-permute-start(f32[1,4,128,128]{3,2,1,0:T(8,128)} %collective-permute-done.3.rest_3_), channel_id=1, source_target_pairs={{0,1},{1,0},{2,3},{3,2},{4,5},{5,4},{6,7},{7,6},{8,9},{9,8},{10,11... | collective-permute-start | bytes 786440 | tf_op jit(solution)/shard_map/ppermute | solution.py:25
  49.5 2.0 %collective-permute-start.12 = (f32[1,4,128,128]{3,2,1,0:T(8,128)}, f32[1,4,128,128]{3,2,1,0:T(8,128)S(1)}, u32[]{:S(2)}, u32[]{:S(2)}) collective-permute-start(f32[1,4,128,128]{3,2,1,0:T(8,128)} %collective-permute-done.9.rest_2_), channel_id=1, source_target_pairs={{0,1},{1,0},{2,3},{3,2},{4,5},{5,4},{6,7},{7,6},{8,9},{9,8},{10,11... | collective-permute-start | bytes 786440 | tf_op jit(solution)/shard_map/ppermute | solution.py:25
  65.9 3.1 %collective-permute-start.17 = (f32[4,5,128,128]{3,2,1,0:T(8,128)S(1)}, f32[4,5,128,128]{3,2,1,0:T(8,128)S(1)}, u32[]{:S(2)}, u32[]{:S(2)}) collective-permute-start(f32[4,5,128,128]{3,2,1,0:T(8,128)S(1)} %get-tuple-element.35), channel_id=1, source_target_pairs={{0,1},{1,0},{2,3},{3,2},{4,5},{5,4},{6,7},{7,6},{8,9},{9,8},{10,11... | collective-permute-start | bytes 3932168 | tf_op jit(solution)/shard_map/ppermute | solution.py:25
  66.1 4.8 %collective-permute-start.21 = (f32[4,5,128,128]{3,2,1,0:T(8,128)S(1)}, f32[4,5,128,128]{3,2,1,0:T(8,128)S(1)}, u32[]{:S(2)}, u32[]{:S(2)}) collective-permute-start(f32[4,5,128,128]{3,2,1,0:T(8,128)S(1)} %get-tuple-element.40), channel_id=1, source_target_pairs={{0,1},{1,0},{2,3},{3,2},{4,5},{5,4},{6,7},{7,6},{8,9},{9,8},{10,11... | collective-permute-start | bytes 3932168 | tf_op jit(solution)/shard_map/ppermute | solution.py:25
  69.1 10.6 %collective-permute-start.18 = (f32[2,5,64,128]{3,2,1,0:T(8,128)S(1)}, f32[2,5,64,128]{3,2,1,0:T(8,128)S(1)}, u32[]{:S(2)}, u32[]{:S(2)}) collective-permute-start(f32[2,5,64,128]{3,2,1,0:T(8,128)S(1)} %pad_maximum_fusion), channel_id=1, source_target_pairs={{0,2},{1,3},{2,0},{3,1},{4,6},{5,7},{6,4},{7,5},{8,10},{9,11},{10,... | collective-permute-start | bytes 983048 | tf_op jit(solution)/shard_map/ppermute | solution.py:25
  69.2 10.6 %collective-permute-start.19 = (f32[2,5,64,128]{3,2,1,0:T(8,128)S(1)}, f32[2,5,64,128]{3,2,1,0:T(8,128)S(1)}, u32[]{:S(2)}, u32[]{:S(2)}) collective-permute-start(f32[2,5,64,128]{3,2,1,0:T(8,128)S(1)} %pad_maximum_fusion.1), channel_id=1, source_target_pairs={{0,4},{1,5},{2,6},{3,7},{4,0},{5,1},{6,2},{7,3},{8,12},{9,13},{10,... | collective-permute-start | bytes 983048 | tf_op jit(solution)/shard_map/ppermute | solution.py:25
  71.0 15.8 %collective-permute-start.22 = (f32[2,5,64,128]{3,2,1,0:T(8,128)S(1)}, f32[2,5,64,128]{3,2,1,0:T(8,128)S(1)}, u32[]{:S(2)}, u32[]{:S(2)}) collective-permute-start(f32[2,5,64,128]{3,2,1,0:T(8,128)S(1)} %pad_maximum_fusion.2), channel_id=1, source_target_pairs={{0,2},{1,3},{2,0},{3,1},{4,6},{5,7},{6,4},{7,5},{8,10},{9,11},{10,... | collective-permute-start | bytes 983048 | tf_op jit(solution)/shard_map/ppermute | solution.py:25
  71.7 15.2 %collective-permute-start.26 = (f32[2,5,64,128]{3,2,1,0:T(8,128)S(1)}, f32[2,5,64,128]{3,2,1,0:T(8,128)S(1)}, u32[]{:S(2)}, u32[]{:S(2)}) collective-permute-start(f32[2,5,64,128]{3,2,1,0:T(8,128)S(1)} %pad_maximum_fusion.3), channel_id=1, source_target_pairs={{0,4},{1,5},{2,6},{3,7},{4,0},{5,1},{6,2},{7,3},{8,12},{9,13},{10,... | collective-permute-start | bytes 983048 | tf_op jit(solution)/shard_map/ppermute | solution.py:25
  79.9 9.7 %collective-permute-start.24 = (f32[5,64,128]{2,1,0:T(8,128)S(1)}, f32[5,64,128]{2,1,0:T(8,128)S(1)}, u32[]{:S(2)}, u32[]{:S(2)}) collective-permute-start(f32[5,64,128]{2,1,0:T(8,128)S(1)} %get-tuple-element.41), channel_id=1, source_target_pairs={{0,4},{1,5},{2,6},{3,7},{4,0},{5,1},{6,2},{7,3},{8,12},{9,13},{10,... | collective-permute-start | bytes 491528 | tf_op jit(solution)/shard_map/ppermute | solution.py:25
  80.1 10.2 %collective-permute-start.28 = (f32[5,64,128]{2,1,0:T(8,128)S(1)}, f32[5,64,128]{2,1,0:T(8,128)S(1)}, u32[]{:S(2)}, u32[]{:S(2)}) collective-permute-start(f32[5,64,128]{2,1,0:T(8,128)S(1)} %get-tuple-element.52), channel_id=1, source_target_pairs={{0,2},{1,3},{2,0},{3,1},{4,6},{5,7},{6,4},{7,5},{8,10},{9,11},{10,... | collective-permute-start | bytes 491528 | tf_op jit(solution)/shard_map/ppermute | solution.py:25
  82.2 28.4 %collective-permute-start.20 = (f32[2,8,128,128]{3,2,1,0:T(8,128)S(1)}, f32[2,8,128,128]{3,2,1,0:T(8,128)S(1)}, u32[]{:S(2)}, u32[]{:S(2)}) collective-permute-start(f32[2,8,128,128]{3,2,1,0:T(8,128)S(1)} %get-tuple-element.36), channel_id=1, source_target_pairs={{0,1},{1,2},{2,3},{3,4},{4,5},{5,6},{6,7},{7,8},{8,9},{9,10},{10,1... | collective-permute-start | bytes 3145736 | tf_op jit(solution)/shard_map/ppermute | solution.py:21
  86.9 15.7 %collective-permute-start.27 = (f32[5,64,128]{2,1,0:T(8,128)S(1)}, f32[5,64,128]{2,1,0:T(8,128)S(1)}, u32[]{:S(2)}, u32[]{:S(2)}) collective-permute-start(f32[5,64,128]{2,1,0:T(8,128)S(1)} %get-tuple-element.44), channel_id=1, source_target_pairs={{0,2},{1,3},{2,0},{3,1},{4,6},{5,7},{6,4},{7,5},{8,10},{9,11},{10,... | collective-permute-start | bytes 491528 | tf_op jit(solution)/shard_map/ppermute | solution.py:25
  89.1 13.6 %collective-permute-start.23 = (f32[5,64,128]{2,1,0:T(8,128)S(1)}, f32[5,64,128]{2,1,0:T(8,128)S(1)}, u32[]{:S(2)}, u32[]{:S(2)}) collective-permute-start(f32[5,64,128]{2,1,0:T(8,128)S(1)} %get-tuple-element.45), channel_id=1, source_target_pairs={{0,4},{1,5},{2,6},{3,7},{4,0},{5,1},{6,2},{7,3},{8,12},{9,13},{10,... | collective-permute-start | bytes 491528 | tf_op jit(solution)/shard_map/ppermute | solution.py:25
  90.4 17.3 %collective-permute-start.29 = (f32[5,64,128]{2,1,0:T(8,128)S(1)}, f32[5,64,128]{2,1,0:T(8,128)S(1)}, u32[]{:S(2)}, u32[]{:S(2)}) collective-permute-start(f32[5,64,128]{2,1,0:T(8,128)S(1)} %get-tuple-element.50), channel_id=1, source_target_pairs={{0,8},{1,9},{2,10},{3,11},{4,12},{5,13},{6,14},{7,15},{8,0},{9,1},... | collective-permute-start | bytes 491528 | tf_op jit(solution)/shard_map/ppermute | solution.py:25
  102.6 7.1 %collective-permute-start.25 = (f32[5,64,128]{2,1,0:T(8,128)S(1)}, f32[5,64,128]{2,1,0:T(8,128)S(1)}, u32[]{:S(2)}, u32[]{:S(2)}) collective-permute-start(f32[5,64,128]{2,1,0:T(8,128)S(1)} %get-tuple-element.51), channel_id=1, source_target_pairs={{0,8},{1,9},{2,10},{3,11},{4,12},{5,13},{6,14},{7,15},{8,0},{9,1},... | collective-permute-start | bytes 491528 | tf_op jit(solution)/shard_map/ppermute | solution.py:25
  (2 other events, 34.7 us)

commit v6 on v5

--- a/solution.py
+++ b/solution.py
@@ -253,9 +253,10 @@
     )(meta, slot_of, live, amplitudes, obj, rim, factors, *pieces)
 
 
-def density_kernel(tile_rows, meta, above, squares, density, ext):
+def density_kernel(meta, above, squares, obj, num_top, out, scale, ext):
     points = LANES
-    blocks = density.shape[0]
+    tile_rows = obj.shape[1]
+    blocks = scale.shape[0]
     ext[...] = jnp.zeros_like(ext)
     lane = lax.broadcasted_iota(jnp.int32, (points, LANES), 1)
 
@@ -284,47 +285,58 @@
 
     lax.fori_loop(0, meta.shape[0] // 4, own, 0)
     lax.fori_loop(0, above.shape[0] // 4, upper, 0)
-    density[...] = ext[:blocks, points : points + tile_rows, :]
-
-
-def density_of(meta, above, squares, tile_rows, blocks):
+    for b in range(blocks):
+        columns = slice(b * LANES, (b + 1) * LANES)
+        scale[b] = 1.0 / (ext[b, points : 2 * points, :] + damping)
+        lower = 1.0 / (ext[b, 2 * points : points + tile_rows, :] + damping)
+        for ch in range(2):
+            out[ch, points:, columns] = obj[ch, points:, columns] + num_top[ch, b, points:] * lower
+            out[ch, :points, columns] = obj[ch, :points, columns]
+
+
+def density_of(meta, above, squares, obj, num_top):
     points = squares.shape[-1]
+    blocks, tile_rows = num_top.shape[1:3]
     smem = pl.BlockSpec(memory_space=pltpu.SMEM)
     vmem = pl.BlockSpec(memory_space=pltpu.VMEM)
     return pl.pallas_call(
-        functools.partial(density_kernel, tile_rows),
-        out_shape=jax.ShapeDtypeStruct((blocks, tile_rows, LANES), jnp.float32),
-        in_specs=[smem, smem, vmem],
-        out_specs=vmem,
+        density_kernel,
+        out_shape=[
+            jax.ShapeDtypeStruct(obj.shape, jnp.float32),
+            jax.ShapeDtypeStruct((blocks, points, LANES), jnp.float32),
+        ],
+        in_specs=[smem, smem, vmem, vmem, vmem],
+        out_specs=[vmem, vmem],
         scratch_shapes=[pltpu.VMEM((blocks + 1, points + tile_rows + points, LANES), jnp.float32)],
         compiler_params=pltpu.CompilerParams(vmem_limit_bytes=VMEM_BYTES),
         cost_estimate=pl.CostEstimate(flops=2**23, bytes_accessed=8 * 2**20, transcendentals=0),
         name="density",
-    )(meta, above, squares)
-
-
-def finish_kernel(obj, num_top, received, density, out):
-    points = received.shape[2]
-    for b in range(density.shape[0]):
+    )(meta, above, squares, obj, num_top)
+
+
+def finish_kernel(begun, num_top, received, scale, out):
+    for b in range(scale.shape[0]):
         columns = slice(b * LANES, (b + 1) * LANES)
-        scale = 1.0 / (density[b] + damping)
         for ch in range(2):
-            head = num_top[ch, b, :points] + received[ch, b]
-            out[ch, :points, columns] = obj[ch, :points, columns] + head * scale[:points]
-            out[ch, points:, columns] = obj[ch, points:, columns] + num_top[ch, b, points:] * scale[points:]
-
-
-def finish(obj, num_top, received, density):
-    vmem = pl.BlockSpec(memory_space=pltpu.VMEM)
+            out[ch, :, columns] = begun[ch, :, columns] + (num_top[ch, b] + received[ch, b]) * scale[b]
+
+
+def finish(begun, num_top, received, scale):
+    blocks, points = scale.shape[:2]
+    whole = pl.BlockSpec(memory_space=pltpu.VMEM)
+    rows = pl.BlockSpec((2, points, begun.shape[2]), lambda i: (0, 0, 0))
+    head = pl.BlockSpec((2, blocks, points, LANES), lambda i: (0, 0, 0, 0))
     return pl.pallas_call(
         finish_kernel,
-        out_shape=jax.ShapeDtypeStruct(obj.shape, obj.dtype),
-        in_specs=[vmem] * 4,
-        out_specs=vmem,
+        grid=(1,),
+        out_shape=jax.ShapeDtypeStruct(begun.shape, begun.dtype),
+        in_specs=[rows, head, head, pl.BlockSpec((blocks, points, LANES), lambda i: (0, 0, 0))],
+        out_specs=rows,
+        input_output_aliases={0: 0},
         compiler_params=pltpu.CompilerParams(vmem_limit_bytes=VMEM_BYTES),
-        cost_estimate=pl.CostEstimate(flops=2**21, bytes_accessed=8 * 2**20, transcendentals=0),
+        cost_estimate=pl.CostEstimate(flops=2**20, bytes_accessed=5 * 2**20, transcendentals=0),
         name="finish",
-    )(obj, num_top, received, density)
+    )(begun, num_top, received, scale)
 
 
 def staged_kernel(*refs):
@@ -352,7 +364,6 @@
     device = lax.axis_index("row")
     size = lax.axis_size("row")
     tile_rows = object_strip.shape[1]
-    blocks = object_strip.shape[2] // LANES
     points = probe_store.shape[-1]
     modes = probe_store.shape[1]
     slot_count = amplitudes.shape[0]
@@ -396,15 +407,15 @@
         meta, slot_of, counts, amplitudes, object_strip, rim, factors, pieces, group_sizes
     )
 
-    density = density_of(meta, above, squares, tile_rows, blocks)
+    begun, scale = density_of(meta, above, squares, object_strip, num_top)
     if swaps:
         mine_far, mine_near, theirs_far, theirs_near = groups
-        total, received, density = reduced((mine_far, swapped(theirs_far, 1)), theirs_near, mine_near, num_low, density)
+        total, received, scale = reduced((mine_far, swapped(theirs_far, 1)), theirs_near, mine_near, num_low, scale)
     else:
         received = moved(num_low, 1)
         summed = lax.psum(groups[0], "row")
         total = jnp.sum(jnp.where(owned, summed, 0.0), axis=0)
-    new_object = finish(object_strip, num_top, received, density)
+    new_object = finish(begun, num_top, received, scale)
     new_probes = own_probe[0] + total[:channels] / (total[channels] + damping)
     return (new_object, new_probes.reshape(probe_store.shape))
 

time: 114 us -> 117 us (1.026)
  the two profiles are of different devices: /device:TPU:0 before, /device:TPU:5 now
where the time goes in v6:
time: 117 us
  starting transfers between devices  51.8 us (44%)
  waiting for transfers between devices  40.9 us (35%)
  Pallas kernels  15.3 us (13%)
  local copies, waits for them, and re-layouts  3.68 us (3%)
  other arithmetic  3.47 us (3%)
  between operations  1.52 us (1%)
    ppermute x27, waiting for transfers between devices, swapped(): lax.ppermute(block, 'row', [(i, i ^ mask) for i in range(lax.axis_size('r...  40.9 us
    ppermute x27, starting transfers between devices, swapped(): lax.ppermute(block, 'row', [(i, i ^ mask) for i in range(lax.axis_size('r...  39.8 us
    ppermute x3, starting transfers between devices, moved(): lax.ppermute(block, 'row', [(i, i + distance) for i in range(size) if 0 <...  12 us
    pallas_call x1, Pallas kernels, update(): pl.pallas_call(functools.partial(update_kernel, (piece_sizes, group_sizes...  9.06 us
    pallas_call x1, Pallas kernels, density_of(): pl.pallas_call(density_kernel, out_shape=[jax.ShapeDtypeStruct(obj.shape,...  3.67 us
    slice x1, local copies, waits for them, and re-layouts, local(): rim = moved(after(object_strip[:, :points, :], slot_of), -1)  2.46 us
    pallas_call x1, Pallas kernels, finish(): pl.pallas_call(finish_kernel, grid=(1,), out_shape=jax.ShapeDtypeStruct(b...  2.45 us
  transfers between devices with their start and end apart: 30, of which 12 were waited for; matrix products, arithmetic and copies ran while one was open for 5% of the time, Pallas kernels for 3%

profile of v6, /device:TPU:5, one launch (start us, length us, event | category | flops | bytes accessed | tf_op | source)
XLA Modules:
  0.0 116.7 jit_solution(14372668329829608327)
XLA Ops:
  0.7 1.5 %collective-permute-start.1 = (f32[1,4,128,128]{3,2,1,0:T(8,128)}, f32[1,4,128,128]{3,2,1,0:T(8,128)}, u32[]{:S(2)}, u32[]{:S(2)}) collective-permute-start(f32[1,4,128,128]{3,2,1,0:T(8,128)} %bitcast.38), channel_id=1, source_target_pairs={{0,4},{1,5},{2,6},{3,7},{4,0},{5,1},{6,2},{7,3},{8,12},{9,13},{10,... | collective-permute-start | bytes 786440 | tf_op jit(solution)/shard_map/ppermute | solution.py:25
  2.2 2.3 %collective-permute-start = (f32[1,4,128,128]{3,2,1,0:T(8,128)}, f32[1,4,128,128]{3,2,1,0:T(8,128)}, u32[]{:S(2)}, u32[]{:S(2)}) collective-permute-start(f32[1,4,128,128]{3,2,1,0:T(8,128)} %bitcast.39), channel_id=1, source_target_pairs={{0,8},{1,9},{2,10},{3,11},{4,12},{5,13},{6,14},{7,15},{8,0},{9,1},... | collective-permute-start | bytes 786440 | tf_op jit(solution)/shard_map/ppermute | solution.py:25
  4.5 2.5 %slice.137 = f32[2,128,1024]{2,1,0:T(8,128)} slice(f32[2,256,1024]{2,1,0:T(8,128)} %obj.3), slice={[0:2], [0:128], [0:1024]} | slice | bytes 2097152 | tf_op jit(solution)/shard_map/slice | solution.py:403
  7.7 3.4 %collective-permute-start.7 = (f32[2,128,1024]{2,1,0:T(8,128)}, f32[2,128,1024]{2,1,0:T(8,128)}, u32[]{:S(2)}, u32[]{:S(2)}) collective-permute-start(f32[2,128,1024]{2,1,0:T(8,128)} %slice.137), channel_id=1, source_target_pairs={{1,0},{2,1},{3,2},{4,3},{5,4},{6,5},{7,6},{8,7},{9,8},{10,9},{11,1... | collective-permute-start | bytes 3145736 | tf_op jit(solution)/shard_map/ppermute | solution.py:21
  11.1 2.7 %collective-permute-done.1.rest_7_ = f32[1,4,128,128]{3,2,1,0:T(8,128)} collective-permute-done((f32[1,4,128,128]{3,2,1,0:T(8,128)}, f32[1,4,128,128]{3,2,1,0:T(8,128)}, u32[]{:S(2)}, u32[]{:S(2)}) %collective-permute-start.1) | collective-permute-done | bytes 262176 | tf_op jit(solution)/shard_map/ppermute | solution.py:25
  13.8 2.3 %collective-permute-start.3 = (f32[1,4,128,128]{3,2,1,0:T(8,128)}, f32[1,4,128,128]{3,2,1,0:T(8,128)}, u32[]{:S(2)}, u32[]{:S(2)}) collective-permute-start(f32[1,4,128,128]{3,2,1,0:T(8,128)} %collective-permute-done.2.rest_5_), channel_id=1, source_target_pairs={{0,4},{1,5},{2,6},{3,7},{4,0},{5,1},{6,2},{7,3},{8,12},{9,13},{10,... | collective-permute-start | bytes 786440 | tf_op jit(solution)/shard_map/ppermute | solution.py:25
  16.1 1.2 %collective-permute-start.8 = (f32[1,4,128,128]{3,2,1,0:T(8,128)}, f32[1,4,128,128]{3,2,1,0:T(8,128)}, u32[]{:S(2)}, u32[]{:S(2)}) collective-permute-start(f32[1,4,128,128]{3,2,1,0:T(8,128)} %collective-permute-done.rest_0_), channel_id=1, source_target_pairs={{0,2},{1,3},{2,0},{3,1},{4,6},{5,7},{6,4},{7,5},{8,10},{9,11},{10,... | collective-permute-start | bytes 786440 | tf_op jit(solution)/shard_map/ppermute | solution.py:25
  17.3 2.8 %collective-permute-done.3.rest_6_ = f32[1,4,128,128]{3,2,1,0:T(8,128)} collective-permute-done((f32[1,4,128,128]{3,2,1,0:T(8,128)}, f32[1,4,128,128]{3,2,1,0:T(8,128)}, u32[]{:S(2)}, u32[]{:S(2)}) %collective-permute-start.3) | collective-permute-done | bytes 262176 | tf_op jit(solution)/shard_map/ppermute | solution.py:25
  20.2 4.4 %collective-permute-start.4 = (f32[1,4,128,128]{3,2,1,0:T(8,128)}, f32[1,4,128,128]{3,2,1,0:T(8,128)}, u32[]{:S(2)}, u32[]{:S(2)}) collective-permute-start(f32[1,4,128,128]{3,2,1,0:T(8,128)} %collective-permute-done.3.rest_6_), channel_id=1, source_target_pairs={{0,1},{1,0},{2,3},{3,2},{4,5},{5,4},{6,7},{7,6},{8,9},{9,8},{10,11... | collective-permute-start | bytes 786440 | tf_op jit(solution)/shard_map/ppermute | solution.py:25
  25.1 6.7 %collective-permute-done.8.rest_1_ = f32[1,4,128,128]{3,2,1,0:T(8,128)} collective-permute-done((f32[1,4,128,128]{3,2,1,0:T(8,128)}, f32[1,4,128,128]{3,2,1,0:T(8,128)}, u32[]{:S(2)}, u32[]{:S(2)}) %collective-permute-start.8) | collective-permute-done | bytes 262176 | tf_op jit(solution)/shard_map/ppermute | solution.py:25
  31.8 1.8 %collective-permute-start.16 = (f32[1,4,128,128]{3,2,1,0:T(8,128)}, f32[1,4,128,128]{3,2,1,0:T(8,128)}, u32[]{:S(2)}, u32[]{:S(2)}) collective-permute-start(f32[1,4,128,128]{3,2,1,0:T(8,128)} %collective-permute-done.1.rest_7_), channel_id=1, source_target_pairs={{0,1},{1,0},{2,3},{3,2},{4,5},{5,4},{6,7},{7,6},{8,9},{9,8},{10,11... | collective-permute-start | bytes 786440 | tf_op jit(solution)/shard_map/ppermute | solution.py:25
  33.6 2.3 %collective-permute-start.9 = (f32[1,4,128,128]{3,2,1,0:T(8,128)}, f32[1,4,128,128]{3,2,1,0:T(8,128)}, u32[]{:S(2)}, u32[]{:S(2)}) collective-permute-start(f32[1,4,128,128]{3,2,1,0:T(8,128)} %collective-permute-done.8.rest_1_), channel_id=1, source_target_pairs={{0,4},{1,5},{2,6},{3,7},{4,0},{5,1},{6,2},{7,3},{8,12},{9,13},{10,... | collective-permute-start | bytes 786440 | tf_op jit(solution)/shard_map/ppermute | solution.py:25
  36.0 0.8 slice_subtract_fusion
  38.2 3.2 %collective-permute-start.5 = (s32[64]{0:T(128)S(1)}, s32[64]{0:T(128)S(1)}, u32[]{:S(2)}, u32[]{:S(2)}) collective-permute-start(s32[64]{0:T(128)S(1)} %reshape.39.meta), channel_id=1, source_target_pairs={{0,1},{1,2},{2,3},{3,4},{4,5},{5,6},{6,7},{7,8},{8,9},{9,10},{10,1... | collective-permute-start | bytes 776 | tf_op jit(solution)/shard_map/ppermute | solution.py:21
  42.0 0.9 collective-permute-done.9.rest_2_
  44.1 1.0 copy-done.3
  45.7 9.1 %update.1 = (f32[2,8,256,128]{3,2,1,0:T(8,128)S(1)}, f32[2,8,128,128]{3,2,1,0:T(8,128)S(1)}, f32[8,128,128]{2,1,0:T(8,128)S(1)}, f32[4,5,128,128]{3,2,1,0:T(8,12...) custom-call(s32[64]{0:T(128)S(1)} %reshape.39.meta, ...), custom_call_target="tpu_custom_call" | custom-call | flops 6000000000 | bytes 16777216 | tf_op jit(solution)/shard_map/update/pallas_call | solution.py:232
  54.7 5.7 %collective-permute-start.17 = (f32[4,5,128,128]{3,2,1,0:T(8,128)S(1)}, f32[4,5,128,128]{3,2,1,0:T(8,128)S(1)}, u32[]{:S(2)}, u32[]{:S(2)}) collective-permute-start(f32[4,5,128,128]{3,2,1,0:T(8,128)S(1)} %get-tuple-element.39), channel_id=1, source_target_pairs={{0,1},{1,0},{2,3},{3,2},{4,5},{5,4},{6,7},{7,6},{8,9},{9,8},{10,11... | collective-permute-start | bytes 3932168 | tf_op jit(solution)/shard_map/ppermute | solution.py:25
  60.5 2.6 %collective-permute-done.17 = f32[4,5,128,128]{3,2,1,0:T(8,128)S(1)} collective-permute-done((f32[4,5,128,128]{3,2,1,0:T(8,128)S(1)}, f32[4,5,128,128]{3,2,1,0:T(8,128)S(1)}, u32[]{:S(2)}, u32[]{:S(2)}) %collective-permute-start.17) | collective-permute-done | bytes 1310752 | tf_op jit(solution)/shard_map/ppermute | solution.py:25
  63.2 4.9 %collective-permute-start.18 = (f32[2,5,64,128]{3,2,1,0:T(8,128)S(1)}, f32[2,5,64,128]{3,2,1,0:T(8,128)S(1)}, u32[]{:S(2)}, u32[]{:S(2)}) collective-permute-start(f32[2,5,64,128]{3,2,1,0:T(8,128)S(1)} %pad_maximum_fusion), channel_id=1, source_target_pairs={{0,2},{1,3},{2,0},{3,1},{4,6},{5,7},{6,4},{7,5},{8,10},{9,11},{10,... | collective-permute-start | bytes 983048 | tf_op jit(solution)/shard_map/ppermute | solution.py:25
  68.4 1.6 %collective-permute-start.22 = (f32[2,5,64,128]{3,2,1,0:T(8,128)S(1)}, f32[2,5,64,128]{3,2,1,0:T(8,128)S(1)}, u32[]{:S(2)}, u32[]{:S(2)}) collective-permute-start(f32[2,5,64,128]{3,2,1,0:T(8,128)S(1)} %pad_maximum_fusion.2), channel_id=1, source_target_pairs={{0,2},{1,3},{2,0},{3,1},{4,6},{5,7},{6,4},{7,5},{8,10},{9,11},{10,... | collective-permute-start | bytes 983048 | tf_op jit(solution)/shard_map/ppermute | solution.py:25
  70.2 3.7 %density.1 = (f32[2,256,1024]{2,1,0:T(8,128)}, f32[8,128,128]{2,1,0:T(8,128)S(1)}) custom-call(s32[64]{0:T(128)S(1)} %reshape.39.meta, s32[64]{0:T(128)S(1)} %collective-permute-done.5.above, f32[8,128,128]{2,1,0:T(8,128)S(1)} %get-tuple-element.34.squares, f32[2,256,1024]{2,1,0:T(8,128)S(1)} %copy-done, f32[2,8,256,128]{3,2,1,0:T(8,128)S(1)} %get-tuple-element.35.num_top), custom_call_target="tpu_custom_call" | custom-call | flops 8388608 | bytes 8388608 | tf_op jit(solution)/shard_map/density/pallas_call | solution.py:302
  73.8 2.1 %collective-permute-done.18 = f32[2,5,64,128]{3,2,1,0:T(8,128)S(1)} collective-permute-done((f32[2,5,64,128]{3,2,1,0:T(8,128)S(1)}, f32[2,5,64,128]{3,2,1,0:T(8,128)S(1)}, u32[]{:S(2)}, u32[]{:S(2)}) %collective-permute-start.18) | collective-permute-done | bytes 327712 | tf_op jit(solution)/shard_map/ppermute | solution.py:25
  75.9 0.9 collective-permute-done.19
  77.3 5.4 %collective-permute-start.20 = (f32[2,8,128,128]{3,2,1,0:T(8,128)S(1)}, f32[2,8,128,128]{3,2,1,0:T(8,128)S(1)}, u32[]{:S(2)}, u32[]{:S(2)}) collective-permute-start(f32[2,8,128,128]{3,2,1,0:T(8,128)S(1)} %get-tuple-element.40), channel_id=1, source_target_pairs={{0,1},{1,2},{2,3},{3,4},{4,5},{5,6},{6,7},{7,8},{8,9},{9,10},{10,1... | collective-permute-start | bytes 3145736 | tf_op jit(solution)/shard_map/ppermute | solution.py:21
  82.7 2.9 %collective-permute-start.24 = (f32[5,64,128]{2,1,0:T(8,128)S(1)}, f32[5,64,128]{2,1,0:T(8,128)S(1)}, u32[]{:S(2)}, u32[]{:S(2)}) collective-permute-start(f32[5,64,128]{2,1,0:T(8,128)S(1)} %get-tuple-element.45), channel_id=1, source_target_pairs={{0,4},{1,5},{2,6},{3,7},{4,0},{5,1},{6,2},{7,3},{8,12},{9,13},{10,... | collective-permute-start | bytes 491528 | tf_op jit(solution)/shard_map/ppermute | solution.py:25
  86.5 13.3 %collective-permute-done.24 = f32[5,64,128]{2,1,0:T(8,128)S(1)} collective-permute-done((f32[5,64,128]{2,1,0:T(8,128)S(1)}, f32[5,64,128]{2,1,0:T(8,128)S(1)}, u32[]{:S(2)}, u32[]{:S(2)}) %collective-permute-start.24) | collective-permute-done | bytes 163872 | tf_op jit(solution)/shard_map/ppermute | solution.py:25
  99.9 5.5 %collective-permute-start.29 = (f32[5,64,128]{2,1,0:T(8,128)S(1)}, f32[5,64,128]{2,1,0:T(8,128)S(1)}, u32[]{:S(2)}, u32[]{:S(2)}) collective-permute-start(f32[5,64,128]{2,1,0:T(8,128)S(1)} %get-tuple-element.54), channel_id=1, source_target_pairs={{0,8},{1,9},{2,10},{3,11},{4,12},{5,13},{6,14},{7,15},{8,0},{9,1},... | collective-permute-start | bytes 491528 | tf_op jit(solution)/shard_map/ppermute | solution.py:25
  105.5 4.4 %collective-permute-done.29 = f32[5,64,128]{2,1,0:T(8,128)S(1)} collective-permute-done((f32[5,64,128]{2,1,0:T(8,128)S(1)}, f32[5,64,128]{2,1,0:T(8,128)S(1)}, u32[]{:S(2)}, u32[]{:S(2)}) %collective-permute-start.29) | collective-permute-done | bytes 163872 | tf_op jit(solution)/shard_map/ppermute | solution.py:25
  109.8 3.5 %collective-permute-done.25 = f32[5,64,128]{2,1,0:T(8,128)S(1)} collective-permute-done((f32[5,64,128]{2,1,0:T(8,128)S(1)}, f32[5,64,128]{2,1,0:T(8,128)S(1)}, u32[]{:S(2)}, u32[]{:S(2)}) %collective-permute-start.25) | collective-permute-done | bytes 163872 | tf_op jit(solution)/shard_map/ppermute | solution.py:25
  113.5 0.7 fusion.2
  114.2 2.5 %finish.1 = f32[2,256,1024]{2,1,0:T(8,128)} custom-call(f32[2,256,1024]{2,1,0:T(8,128)} %get-tuple-element.36.begun, f32[2,8,256,128]{3,2,1,0:T(8,128)S(1)} %get-tuple-element.35.num_top, f32[2,8,128,128]{3,2,1,0:T(8,128)S(1)} %collective-permute-done.20.received, f32[8,128,128]{2,1,0:T(8,128)S(1)} %get-tuple-element.42.scale), custom_call_target="tpu_custom_call", output_to_operand_aliasing={{}: (0, {})} | custom-call | flops 1048576 | bytes 5242880 | tf_op jit(solution)/shard_map/finish/pallas_call | solution.py:329
  (59 shorter events, 6.6 us)
Async XLA Ops:
  0.6 43.4 %copy-start.2 = (f32[16,128,128]{2,1,0:T(8,128)S(1)}, f32[16,128,128]{2,1,0:T(8,128)}, u32[]{:S(2)}) copy-start(f32[16,128,128]{2,1,0:T(8,128)} %refs_0_.1) | copy-start | bytes 3145732
  0.6 10.5 %collective-permute-start.2 = (f32[1,4,128,128]{3,2,1,0:T(8,128)}, f32[1,4,128,128]{3,2,1,0:T(8,128)}, u32[]{:S(2)}, u32[]{:S(2)}) collective-permute-start(f32[1,4,128,128]{3,2,1,0:T(8,128)} %bitcast.37), channel_id=1, source_target_pairs={{0,2},{1,3},{2,0},{3,1},{4,6},{5,7},{6,4},{7,5},{8,10},{9,11},{10,... | collective-permute-start | bytes 786440 | tf_op jit(solution)/shard_map/ppermute | solution.py:25
  0.7 13.1 %collective-permute-start.1 = (f32[1,4,128,128]{3,2,1,0:T(8,128)}, f32[1,4,128,128]{3,2,1,0:T(8,128)}, u32[]{:S(2)}, u32[]{:S(2)}) collective-permute-start(f32[1,4,128,128]{3,2,1,0:T(8,128)} %bitcast.38), channel_id=1, source_target_pairs={{0,4},{1,5},{2,6},{3,7},{4,0},{5,1},{6,2},{7,3},{8,12},{9,13},{10,... | collective-permute-start | bytes 786440 | tf_op jit(solution)/shard_map/ppermute | solution.py:25
  2.2 11.5 %collective-permute-start = (f32[1,4,128,128]{3,2,1,0:T(8,128)}, f32[1,4,128,128]{3,2,1,0:T(8,128)}, u32[]{:S(2)}, u32[]{:S(2)}) collective-permute-start(f32[1,4,128,128]{3,2,1,0:T(8,128)} %bitcast.39), channel_id=1, source_target_pairs={{0,8},{1,9},{2,10},{3,11},{4,12},{5,13},{6,14},{7,15},{8,0},{9,1},... | collective-permute-start | bytes 786440 | tf_op jit(solution)/shard_map/ppermute | solution.py:25
  4.5 41.1 %copy-start = (f32[2,256,1024]{2,1,0:T(8,128)S(1)}, f32[2,256,1024]{2,1,0:T(8,128)}, u32[]{:S(2)}) copy-start(f32[2,256,1024]{2,1,0:T(8,128)} %obj.3) | copy-start | bytes 6291460
  7.7 35.9 %collective-permute-start.7 = (f32[2,128,1024]{2,1,0:T(8,128)}, f32[2,128,1024]{2,1,0:T(8,128)}, u32[]{:S(2)}, u32[]{:S(2)}) collective-permute-start(f32[2,128,1024]{2,1,0:T(8,128)} %slice.137), channel_id=1, source_target_pairs={{1,0},{2,1},{3,2},{4,3},{5,4},{6,5},{7,6},{8,7},{9,8},{10,9},{11,1... | collective-permute-start | bytes 3145736 | tf_op jit(solution)/shard_map/ppermute | solution.py:21
  13.8 6.4 %collective-permute-start.3 = (f32[1,4,128,128]{3,2,1,0:T(8,128)}, f32[1,4,128,128]{3,2,1,0:T(8,128)}, u32[]{:S(2)}, u32[]{:S(2)}) collective-permute-start(f32[1,4,128,128]{3,2,1,0:T(8,128)} %collective-permute-done.2.rest_5_), channel_id=1, source_target_pairs={{0,4},{1,5},{2,6},{3,7},{4,0},{5,1},{6,2},{7,3},{8,12},{9,13},{10,... | collective-permute-start | bytes 786440 | tf_op jit(solution)/shard_map/ppermute | solution.py:25
  16.1 15.7 %collective-permute-start.8 = (f32[1,4,128,128]{3,2,1,0:T(8,128)}, f32[1,4,128,128]{3,2,1,0:T(8,128)}, u32[]{:S(2)}, u32[]{:S(2)}) collective-permute-start(f32[1,4,128,128]{3,2,1,0:T(8,128)} %collective-permute-done.rest_0_), channel_id=1, source_target_pairs={{0,2},{1,3},{2,0},{3,1},{4,6},{5,7},{6,4},{7,5},{8,10},{9,11},{10,... | collective-permute-start | bytes 786440 | tf_op jit(solution)/shard_map/ppermute | solution.py:25
  20.2 13.5 %collective-permute-start.4 = (f32[1,4,128,128]{3,2,1,0:T(8,128)}, f32[1,4,128,128]{3,2,1,0:T(8,128)}, u32[]{:S(2)}, u32[]{:S(2)}) collective-permute-start(f32[1,4,128,128]{3,2,1,0:T(8,128)} %collective-permute-done.3.rest_6_), channel_id=1, source_target_pairs={{0,1},{1,0},{2,3},{3,2},{4,5},{5,4},{6,7},{7,6},{8,9},{9,8},{10,11... | collective-permute-start | bytes 786440 | tf_op jit(solution)/shard_map/ppermute | solution.py:25
  24.5 13.7 %collective-permute-start.14 = (f32[1,4,128,128]{3,2,1,0:T(8,128)S(1)}, f32[1,4,128,128]{3,2,1,0:T(8,128)}, u32[]{:S(2)}, u32[]{:S(2)}) collective-permute-start(f32[1,4,128,128]{3,2,1,0:T(8,128)S(1)} %bitcast.40), channel_id=1, source_target_pairs={{0,1},{1,0},{2,3},{3,2},{4,5},{5,4},{6,7},{7,6},{8,9},{9,8},{10,11... | collective-permute-start | bytes 786440 | tf_op jit(solution)/shard_map/ppermute | solution.py:25
  24.5 17.0 %collective-permute-start.6 = (f32[1,4,128,128]{3,2,1,0:T(8,128)}, f32[1,4,128,128]{3,2,1,0:T(8,128)}, u32[]{:S(2)}, u32[]{:S(2)}) collective-permute-start(f32[1,4,128,128]{3,2,1,0:T(8,128)} %collective-permute-done.rest_0_), channel_id=1, source_target_pairs={{0,4},{1,5},{2,6},{3,7},{4,0},{5,1},{6,2},{7,3},{8,12},{9,13},{10,... | collective-permute-start | bytes 786440 | tf_op jit(solution)/shard_map/ppermute | solution.py:25
  31.8 9.6 %collective-permute-start.16 = (f32[1,4,128,128]{3,2,1,0:T(8,128)}, f32[1,4,128,128]{3,2,1,0:T(8,128)}, u32[]{:S(2)}, u32[]{:S(2)}) collective-permute-start(f32[1,4,128,128]{3,2,1,0:T(8,128)} %collective-permute-done.1.rest_7_), channel_id=1, source_target_pairs={{0,1},{1,0},{2,3},{3,2},{4,5},{5,4},{6,7},{7,6},{8,9},{9,8},{10,11... | collective-permute-start | bytes 786440 | tf_op jit(solution)/shard_map/ppermute | solution.py:25
  33.6 9.3 %collective-permute-start.9 = (f32[1,4,128,128]{3,2,1,0:T(8,128)}, f32[1,4,128,128]{3,2,1,0:T(8,128)}, u32[]{:S(2)}, u32[]{:S(2)}) collective-permute-start(f32[1,4,128,128]{3,2,1,0:T(8,128)} %collective-permute-done.8.rest_1_), channel_id=1, source_target_pairs={{0,4},{1,5},{2,6},{3,7},{4,0},{5,1},{6,2},{7,3},{8,12},{9,13},{10,... | collective-permute-start | bytes 786440 | tf_op jit(solution)/shard_map/ppermute | solution.py:25
  38.2 5.3 %collective-permute-start.5 = (s32[64]{0:T(128)S(1)}, s32[64]{0:T(128)S(1)}, u32[]{:S(2)}, u32[]{:S(2)}) collective-permute-start(s32[64]{0:T(128)S(1)} %reshape.39.meta), channel_id=1, source_target_pairs={{0,1},{1,2},{2,3},{3,4},{4,5},{5,6},{6,7},{7,8},{8,9},{9,10},{10,1... | collective-permute-start | bytes 776 | tf_op jit(solution)/shard_map/ppermute | solution.py:21
  41.5 3.8 %collective-permute-start.15 = (f32[1,4,128,128]{3,2,1,0:T(8,128)}, f32[1,4,128,128]{3,2,1,0:T(8,128)S(1)}, u32[]{:S(2)}, u32[]{:S(2)}) collective-permute-start(f32[1,4,128,128]{3,2,1,0:T(8,128)} %collective-permute-done.2.rest_5_), channel_id=1, source_target_pairs={{0,1},{1,0},{2,3},{3,2},{4,5},{5,4},{6,7},{7,6},{8,9},{9,8},{10,11... | collective-permute-start | bytes 786440 | tf_op jit(solution)/shard_map/ppermute | solution.py:25
  41.6 3.7 %collective-permute-start.10 = (f32[1,4,128,128]{3,2,1,0:T(8,128)}, f32[1,4,128,128]{3,2,1,0:T(8,128)S(1)}, u32[]{:S(2)}, u32[]{:S(2)}) collective-permute-start(f32[1,4,128,128]{3,2,1,0:T(8,128)} %collective-permute-done.rest_0_), channel_id=1, source_target_pairs={{0,1},{1,0},{2,3},{3,2},{4,5},{5,4},{6,7},{7,6},{8,9},{9,8},{10,11... | collective-permute-start | bytes 786440 | tf_op jit(solution)/shard_map/ppermute | solution.py:25
  42.9 2.3 %collective-permute-start.11 = (f32[1,4,128,128]{3,2,1,0:T(8,128)}, f32[1,4,128,128]{3,2,1,0:T(8,128)S(1)}, u32[]{:S(2)}, u32[]{:S(2)}) collective-permute-start(f32[1,4,128,128]{3,2,1,0:T(8,128)} %collective-permute-done.8.rest_1_), channel_id=1, source_target_pairs={{0,1},{1,0},{2,3},{3,2},{4,5},{5,4},{6,7},{7,6},{8,9},{9,8},{10,11... | collective-permute-start | bytes 786440 | tf_op jit(solution)/shard_map/ppermute | solution.py:25
  43.5 1.8 %collective-permute-start.13 = (f32[1,4,128,128]{3,2,1,0:T(8,128)}, f32[1,4,128,128]{3,2,1,0:T(8,128)S(1)}, u32[]{:S(2)}, u32[]{:S(2)}) collective-permute-start(f32[1,4,128,128]{3,2,1,0:T(8,128)} %collective-permute-done.6.rest_3_), channel_id=1, source_target_pairs={{0,1},{1,0},{2,3},{3,2},{4,5},{5,4},{6,7},{7,6},{8,9},{9,8},{10,11... | collective-permute-start | bytes 786440 | tf_op jit(solution)/shard_map/ppermute | solution.py:25
  43.5 2.1 %collective-permute-start.12 = (f32[1,4,128,128]{3,2,1,0:T(8,128)}, f32[1,4,128,128]{3,2,1,0:T(8,128)S(1)}, u32[]{:S(2)}, u32[]{:S(2)}) collective-permute-start(f32[1,4,128,128]{3,2,1,0:T(8,128)} %collective-permute-done.9.rest_2_), channel_id=1, source_target_pairs={{0,1},{1,0},{2,3},{3,2},{4,5},{5,4},{6,7},{7,6},{8,9},{9,8},{10,11... | collective-permute-start | bytes 786440 | tf_op jit(solution)/shard_map/ppermute | solution.py:25
  54.7 8.4 %collective-permute-start.17 = (f32[4,5,128,128]{3,2,1,0:T(8,128)S(1)}, f32[4,5,128,128]{3,2,1,0:T(8,128)S(1)}, u32[]{:S(2)}, u32[]{:S(2)}) collective-permute-start(f32[4,5,128,128]{3,2,1,0:T(8,128)S(1)} %get-tuple-element.39), channel_id=1, source_target_pairs={{0,1},{1,0},{2,3},{3,2},{4,5},{5,4},{6,7},{7,6},{8,9},{9,8},{10,11... | collective-permute-start | bytes 3932168 | tf_op jit(solution)/shard_map/ppermute | solution.py:25
  60.4 7.9 %collective-permute-start.21 = (f32[4,5,128,128]{3,2,1,0:T(8,128)S(1)}, f32[4,5,128,128]{3,2,1,0:T(8,128)S(1)}, u32[]{:S(2)}, u32[]{:S(2)}) collective-permute-start(f32[4,5,128,128]{3,2,1,0:T(8,128)S(1)} %get-tuple-element.44), channel_id=1, source_target_pairs={{0,1},{1,0},{2,3},{3,2},{4,5},{5,4},{6,7},{7,6},{8,9},{9,8},{10,11... | collective-permute-start | bytes 3932168 | tf_op jit(solution)/shard_map/ppermute | solution.py:25
  63.2 12.7 %collective-permute-start.18 = (f32[2,5,64,128]{3,2,1,0:T(8,128)S(1)}, f32[2,5,64,128]{3,2,1,0:T(8,128)S(1)}, u32[]{:S(2)}, u32[]{:S(2)}) collective-permute-start(f32[2,5,64,128]{3,2,1,0:T(8,128)S(1)} %pad_maximum_fusion), channel_id=1, source_target_pairs={{0,2},{1,3},{2,0},{3,1},{4,6},{5,7},{6,4},{7,5},{8,10},{9,11},{10,... | collective-permute-start | bytes 983048 | tf_op jit(solution)/shard_map/ppermute | solution.py:25
  68.2 8.7 %collective-permute-start.19 = (f32[2,5,64,128]{3,2,1,0:T(8,128)S(1)}, f32[2,5,64,128]{3,2,1,0:T(8,128)S(1)}, u32[]{:S(2)}, u32[]{:S(2)}) collective-permute-start(f32[2,5,64,128]{3,2,1,0:T(8,128)S(1)} %pad_maximum_fusion.1), channel_id=1, source_target_pairs={{0,4},{1,5},{2,6},{3,7},{4,0},{5,1},{6,2},{7,3},{8,12},{9,13},{10,... | collective-permute-start | bytes 983048 | tf_op jit(solution)/shard_map/ppermute | solution.py:25
  68.4 17.2 %collective-permute-start.22 = (f32[2,5,64,128]{3,2,1,0:T(8,128)S(1)}, f32[2,5,64,128]{3,2,1,0:T(8,128)S(1)}, u32[]{:S(2)}, u32[]{:S(2)}) collective-permute-start(f32[2,5,64,128]{3,2,1,0:T(8,128)S(1)} %pad_maximum_fusion.2), channel_id=1, source_target_pairs={{0,2},{1,3},{2,0},{3,1},{4,6},{5,7},{6,4},{7,5},{8,10},{9,11},{10,... | collective-permute-start | bytes 983048 | tf_op jit(solution)/shard_map/ppermute | solution.py:25
  70.0 15.6 %collective-permute-start.26 = (f32[2,5,64,128]{3,2,1,0:T(8,128)S(1)}, f32[2,5,64,128]{3,2,1,0:T(8,128)S(1)}, u32[]{:S(2)}, u32[]{:S(2)}) collective-permute-start(f32[2,5,64,128]{3,2,1,0:T(8,128)S(1)} %pad_maximum_fusion.3), channel_id=1, source_target_pairs={{0,4},{1,5},{2,6},{3,7},{4,0},{5,1},{6,2},{7,3},{8,12},{9,13},{10,... | collective-permute-start | bytes 983048 | tf_op jit(solution)/shard_map/ppermute | solution.py:25
  76.9 9.5 %collective-permute-start.28 = (f32[5,64,128]{2,1,0:T(8,128)S(1)}, f32[5,64,128]{2,1,0:T(8,128)S(1)}, u32[]{:S(2)}, u32[]{:S(2)}) collective-permute-start(f32[5,64,128]{2,1,0:T(8,128)S(1)} %get-tuple-element.56), channel_id=1, source_target_pairs={{0,2},{1,3},{2,0},{3,1},{4,6},{5,7},{6,4},{7,5},{8,10},{9,11},{10,... | collective-permute-start | bytes 491528 | tf_op jit(solution)/shard_map/ppermute | solution.py:25
  77.3 36.9 %collective-permute-start.20 = (f32[2,8,128,128]{3,2,1,0:T(8,128)S(1)}, f32[2,8,128,128]{3,2,1,0:T(8,128)S(1)}, u32[]{:S(2)}, u32[]{:S(2)}) collective-permute-start(f32[2,8,128,128]{3,2,1,0:T(8,128)S(1)} %get-tuple-element.40), channel_id=1, source_target_pairs={{0,1},{1,2},{2,3},{3,4},{4,5},{5,6},{6,7},{7,8},{8,9},{9,10},{10,1... | collective-permute-start | bytes 3145736 | tf_op jit(solution)/shard_map/ppermute | solution.py:21
  82.7 17.1 %collective-permute-start.24 = (f32[5,64,128]{2,1,0:T(8,128)S(1)}, f32[5,64,128]{2,1,0:T(8,128)S(1)}, u32[]{:S(2)}, u32[]{:S(2)}) collective-permute-start(f32[5,64,128]{2,1,0:T(8,128)S(1)} %get-tuple-element.45), channel_id=1, source_target_pairs={{0,4},{1,5},{2,6},{3,7},{4,0},{5,1},{6,2},{7,3},{8,12},{9,13},{10,... | collective-permute-start | bytes 491528 | tf_op jit(solution)/shard_map/ppermute | solution.py:25
  85.7 19.8 %collective-permute-start.27 = (f32[5,64,128]{2,1,0:T(8,128)S(1)}, f32[5,64,128]{2,1,0:T(8,128)S(1)}, u32[]{:S(2)}, u32[]{:S(2)}) collective-permute-start(f32[5,64,128]{2,1,0:T(8,128)S(1)} %get-tuple-element.48), channel_id=1, source_target_pairs={{0,2},{1,3},{2,0},{3,1},{4,6},{5,7},{6,4},{7,5},{8,10},{9,11},{10,... | collective-permute-start | bytes 491528 | tf_op jit(solution)/shard_map/ppermute | solution.py:25
  85.8 19.7 %collective-permute-start.23 = (f32[5,64,128]{2,1,0:T(8,128)S(1)}, f32[5,64,128]{2,1,0:T(8,128)S(1)}, u32[]{:S(2)}, u32[]{:S(2)}) collective-permute-start(f32[5,64,128]{2,1,0:T(8,128)S(1)} %get-tuple-element.49), channel_id=1, source_target_pairs={{0,4},{1,5},{2,6},{3,7},{4,0},{5,1},{6,2},{7,3},{8,12},{9,13},{10,... | collective-permute-start | bytes 491528 | tf_op jit(solution)/shard_map/ppermute | solution.py:25
  99.9 10.0 %collective-permute-start.29 = (f32[5,64,128]{2,1,0:T(8,128)S(1)}, f32[5,64,128]{2,1,0:T(8,128)S(1)}, u32[]{:S(2)}, u32[]{:S(2)}) collective-permute-start(f32[5,64,128]{2,1,0:T(8,128)S(1)} %get-tuple-element.54), channel_id=1, source_target_pairs={{0,8},{1,9},{2,10},{3,11},{4,12},{5,13},{6,14},{7,15},{8,0},{9,1},... | collective-permute-start | bytes 491528 | tf_op jit(solution)/shard_map/ppermute | solution.py:25
  105.4 8.0 %collective-permute-start.25 = (f32[5,64,128]{2,1,0:T(8,128)S(1)}, f32[5,64,128]{2,1,0:T(8,128)S(1)}, u32[]{:S(2)}, u32[]{:S(2)}) collective-permute-start(f32[5,64,128]{2,1,0:T(8,128)S(1)} %get-tuple-element.55), channel_id=1, source_target_pairs={{0,8},{1,9},{2,10},{3,11},{4,12},{5,13},{6,14},{7,15},{8,0},{9,1},... | collective-permute-start | bytes 491528 | tf_op jit(solution)/shard_map/ppermute | solution.py:25
  (2 other events, 25.0 us)
